TPU v7x, 256 devices: a whole 4x4x8 slice. The times are simulated.
256 devices in a mesh: dp: 32 (over z, x), gen: 8 (over y, core).
Axes of the slice: x: 4, y: 4, z: 8, core: 2. Of those that a mesh axis runs over, the one named last changes fastest.
Arguments:
- private: bfloat16 [32768, 1024], P('dp', 'gen'), may hold values from -12 to 12, as said below
- generated: bfloat16 [16384, 1024], P(('gen', 'dp')), may hold values from -12 to 12, as said below
- noise: float32 [16384, 1024], P(('gen', 'dp')), may hold values from -3 to 3
Outputs:
- update: float32 [16384, 1024], P(('gen', 'dp'))
Inputs may be any that keep to these rules, and one draw needn't show every extreme that they name: `private`: private embeddings, drawn from a seed. `generated`: generated embeddings, drawn from a seed.
All inputs are finite; a program needn't handle non-finite values.
Results may differ from a plain program's by a relative error of at most 0.0024.
Values may be sent and summed in bfloat16 or wider, within the bound.
No kernel may reach another device: no remote copies, remote signals or barrier semaphores. Data moves between devices by JAX's collectives and lax.ppermute only.
A program may use at most 64 MiB of HBM per device.

v0:
```python
import math

import jax
import jax.numpy as jnp
from jax import lax
from jax.sharding import PartitionSpec as P

ITERS = 3


smoothing_epsilon = 0.02


def source_softmax_normalizer(kernel_grid):
    maximal_element = jnp.max(kernel_grid, axis=1)
    accumulated_exponential = jnp.sum(jnp.exp(kernel_grid - maximal_element[:, None]), axis=1)
    highest = lax.pmax(maximal_element, "gen")
    accumulated_exponential = lax.psum(
        accumulated_exponential * jnp.exp(maximal_element - highest), "gen"
    )
    maximal_element = highest
    return maximal_element + jnp.log(accumulated_exponential)


def target_softmax_normalizer(kernel_grid):
    maximal_element = jnp.max(kernel_grid, axis=0)
    accumulated_exponential = jnp.sum(jnp.exp(kernel_grid - maximal_element[None, :]), axis=0)
    highest = lax.pmax(maximal_element, "dp")
    accumulated_exponential = lax.psum(
        accumulated_exponential * jnp.exp(maximal_element - highest), "dp"
    )
    maximal_element = highest
    return maximal_element + jnp.log(accumulated_exponential)


def shards(private, generated, noise):
    private_rows = lax.all_gather(private, "gen", axis=1, tiled=True)
    features = private_rows.shape[1]
    private_sq = jnp.sum(private_rows.astype(jnp.float32) ** 2, axis=1)
    block_rows = lax.all_gather(generated, "dp", axis=0, tiled=True)
    block_sq = jnp.sum(block_rows.astype(jnp.float32) ** 2, axis=1)
    cross = jnp.einsum("id,jd->ij", private_rows, block_rows, preferred_element_type=jnp.float32)
    distance_grid = (private_sq[:, None] + block_sq[None, :] - 2.0 * cross) / features
    source_mass_logarithm = math.log(private_rows.shape[0] * lax.axis_size("dp"))
    target_mass_logarithm = math.log(distance_grid.shape[1] * lax.axis_size("gen"))
    target_lagrange_vector = jnp.zeros((distance_grid.shape[1],), jnp.float32)
    for step_index in range(ITERS):
        source_lagrange_vector = -smoothing_epsilon * (
            source_softmax_normalizer(
                (target_lagrange_vector[None, :] - distance_grid) / smoothing_epsilon
            )
            - target_mass_logarithm
        )
        target_lagrange_vector = -smoothing_epsilon * (
            target_softmax_normalizer(
                (source_lagrange_vector[:, None] - distance_grid) / smoothing_epsilon
            )
            - source_mass_logarithm
        )
    coupling_plan = jnp.exp(
        (source_lagrange_vector[:, None] + target_lagrange_vector[None, :] - distance_grid)
        / smoothing_epsilon
        - source_mass_logarithm
    )
    coupling_plan = coupling_plan.astype(jnp.bfloat16)
    partial_sums = jnp.einsum(
        "ij,id->jd", coupling_plan, private_rows, preferred_element_type=jnp.float32
    )
    barycenter = lax.psum_scatter(partial_sums, "dp", scatter_dimension=0, tiled=True)
    return generated.astype(jnp.float32) - barycenter + noise


def solution(mesh):
    in_specs = (P("dp", "gen"), P(("gen", "dp"), None), P(("gen", "dp"), None))
    out_specs = P(("gen", "dp"), None)
    return jax.shard_map(shards, mesh=mesh, in_specs=in_specs, out_specs=out_specs, check_vma=False)
```

profile of v0, /device:TPU:1, one launch (start us, length us, event | category | flops | bytes accessed | tf_op | source)
XLA Modules:
  0.0 937.3 jit_solution(494788625342452514)
XLA Ops:
  6.5 0.0 all-gather.3.cloned.1.call-start
  6.5 0.7 all-gather.3.cloned.1.call-update
  7.3 0.0 all-gather.5.cloned.1.call-start
  7.3 0.7 all-gather.5.cloned.1.call-update
  8.0 0.0 reduce-scatter.2.cloned.1.call-start
  8.1 35.2 %all-gather.3.cloned.1.call-done = bf16[1024,1024]{1,0:T(8,128)(2,1)} async-done(((bf16[1024,128]{1,0:T(8,128)(2,1)}), bf16[1024,1024]{1,0:T(8,128)(2,1)}) %all-gather.3.cloned.1.call-update) | async-done | bytes 2097168 | tf_op jit(solution)/shard_map/all_gather | solution.py:37
  43.3 2.1 multiply_reduce_fusion.1
  45.3 80.3 %all-gather.5.cloned.1.call-done = bf16[2048,1024]{1,0:T(8,128)(2,1)} async-done(((bf16[64,1024]{1,0:T(8,128)(2,1)}), bf16[2048,1024]{1,0:T(8,128)(2,1)}) %all-gather.5.cloned.1.call-update) | async-done | bytes 4194320 | tf_op jit(solution)/shard_map/all_gather | solution.py:40
  125.6 3.1 multiply_reduce_fusion
  128.7 11.0 %fusion = (f32[1024]{0:T(1024)S(1)}, f32[1024,2048]{1,0:T(8,128)}) fusion(bf16[1024,1024]{1,0:T(8,128)(2,1)} %all-gather.3.cloned.1.call-done, bf16[2048,1024]{1,0:T(8,128)(2,1)} %all-gather.5.cloned.1.call-done, f32[2048]{0:T(1024)S(1)} %multiply_reduce_fusion, f32[1024]{0:T(1024)S(1)} %multiply_reduce_fusion.1), kind=kOutput, calls=%fused_computation.15 | convolution fusion | flops 4309646336 | bytes 14696448 | tf_op jit(solution)/shard_map/id,jd->ij/dot_general | solution.py:42
  139.7 15.1 %pmax.42 = f32[1024]{0:T(1024)S(1)} all-reduce(f32[1024]{0:T(1024)S(1)} %get-tuple-element.5), channel_id=1, replica_groups=mesh['dp'=32,'gen'=8] {'gen'}, use_global_device_ids=true, to_apply=%region_3.0 | all-reduce | flops 1024 | bytes 8192 | tf_op jit(solution)/shard_map/pmax | solution.py:17
  154.8 4.5 exponential_reduce_fusion.5
  159.3 12.4 %psum.42 = f32[1024]{0:T(1024)S(1)} all-reduce(f32[1024]{0:T(1024)S(1)} %exponential_multiply_fusion.5), channel_id=1, replica_groups=mesh['dp'=32,'gen'=8] {'gen'}, use_global_device_ids=true, to_apply=%region_5.0 | all-reduce | flops 1024 | bytes 8192 | tf_op jit(solution)/shard_map/psum | solution.py:18
  171.7 4.3 fusion.1
  176.0 4.5 exponential_reduce_fusion.4
  180.5 60.0 %pmax.43 = f32[2048]{0:T(1024)S(1)} all-reduce(f32[2048]{0:T(1024)S(1)} %fusion.1), channel_id=1, replica_groups=mesh['dp'=32,'gen'=8] {'dp'}, use_global_device_ids=true, to_apply=%region_7.0 | all-reduce | flops 2048 | bytes 16384 | tf_op jit(solution)/shard_map/pmax | solution.py:28
  240.5 57.1 %psum.43 = f32[2048]{0:T(1024)S(1)} all-reduce(f32[2048]{0:T(1024)S(1)} %exponential_multiply_fusion.2), channel_id=1, replica_groups=mesh['dp'=32,'gen'=8] {'dp'}, use_global_device_ids=true, to_apply=%region_9.0 | all-reduce | flops 2048 | bytes 16384 | tf_op jit(solution)/shard_map/psum | solution.py:29
  297.6 4.3 fusion.2
  301.9 4.5 exponential_reduce_fusion.3
  306.4 39.6 %pmax.44 = f32[1024]{0:T(1024)S(1)} all-reduce(f32[1024]{0:T(1024)S(1)} %fusion.2), channel_id=1, replica_groups=mesh['dp'=32,'gen'=8] {'gen'}, use_global_device_ids=true, to_apply=%region_11.0 | all-reduce | flops 1024 | bytes 8192 | tf_op jit(solution)/shard_map/pmax | solution.py:17
  346.0 12.6 %psum.44 = f32[1024]{0:T(1024)S(1)} all-reduce(f32[1024]{0:T(1024)S(1)} %exponential_multiply_fusion.4), channel_id=1, replica_groups=mesh['dp'=32,'gen'=8] {'gen'}, use_global_device_ids=true, to_apply=%region_13.0 | all-reduce | flops 1024 | bytes 8192 | tf_op jit(solution)/shard_map/psum | solution.py:18
  358.6 4.3 fusion.3
  362.9 4.5 exponential_reduce_fusion.2
  367.4 59.2 %pmax.45 = f32[2048]{0:T(1024)S(1)} all-reduce(f32[2048]{0:T(1024)S(1)} %fusion.3), channel_id=1, replica_groups=mesh['dp'=32,'gen'=8] {'dp'}, use_global_device_ids=true, to_apply=%region_15.0 | all-reduce | flops 2048 | bytes 16384 | tf_op jit(solution)/shard_map/pmax | solution.py:28
  426.6 57.0 %psum.45 = f32[2048]{0:T(1024)S(1)} all-reduce(f32[2048]{0:T(1024)S(1)} %exponential_multiply_fusion.1), channel_id=1, replica_groups=mesh['dp'=32,'gen'=8] {'dp'}, use_global_device_ids=true, to_apply=%region_17.0 | all-reduce | flops 2048 | bytes 16384 | tf_op jit(solution)/shard_map/psum | solution.py:29
  483.7 4.3 fusion.4
  488.0 4.5 exponential_reduce_fusion.1
  492.5 39.6 %pmax.46 = f32[1024]{0:T(1024)S(1)} all-reduce(f32[1024]{0:T(1024)S(1)} %fusion.4), channel_id=1, replica_groups=mesh['dp'=32,'gen'=8] {'gen'}, use_global_device_ids=true, to_apply=%region_19.0 | all-reduce | flops 1024 | bytes 8192 | tf_op jit(solution)/shard_map/pmax | solution.py:17
  532.1 12.4 %psum.46 = f32[1024]{0:T(1024)S(1)} all-reduce(f32[1024]{0:T(1024)S(1)} %exponential_multiply_fusion.3), channel_id=1, replica_groups=mesh['dp'=32,'gen'=8] {'gen'}, use_global_device_ids=true, to_apply=%region_21.0 | all-reduce | flops 1024 | bytes 8192 | tf_op jit(solution)/shard_map/psum | solution.py:18
  544.5 0.0 copy-start
  544.5 4.4 fusion.5
  549.0 59.1 %pmax.47 = f32[2048]{0:T(1024)S(1)} all-reduce(f32[2048]{0:T(1024)S(1)} %fusion.5), channel_id=1, replica_groups=mesh['dp'=32,'gen'=8] {'dp'}, use_global_device_ids=true, to_apply=%region_23.0 | all-reduce | flops 2048 | bytes 16384 | tf_op jit(solution)/shard_map/pmax | solution.py:28
  608.1 4.5 exponential_reduce_fusion
  612.6 57.1 %psum.47 = f32[2048]{0:T(1024)S(1)} all-reduce(f32[2048]{0:T(1024)S(1)} %exponential_multiply_fusion), channel_id=1, replica_groups=mesh['dp'=32,'gen'=8] {'dp'}, use_global_device_ids=true, to_apply=%region_25.0 | all-reduce | flops 2048 | bytes 16384 | tf_op jit(solution)/shard_map/psum | solution.py:29
  669.7 0.0 copy-done
  669.7 11.7 %fusion.6 = f32[2048,1024]{1,0:T(8,128)} fusion(bf16[1024,1024]{1,0:T(8,128)(2,1)S(1)} %copy-done, f32[1024,2048]{1,0:T(8,128)} %get-tuple-element.6, f32[2048]{0:T(1024)S(1)} %add_multiply_fusion, f32[1024]{0:T(1024)S(1)} %add_multiply_fusion.3), kind=kOutput, calls=%fused_computation.21 | convolution fusion | flops 4305453056 | bytes 18886656 | tf_op jit(solution)/shard_map/ij,id->jd/dot_general | solution.py:66
  681.4 0.0 copy-start.1
  681.4 0.0 copy-start.2
  681.4 0.0 reduce-scatter.2.cloned.1.call-update
  681.4 247.6 %reduce-scatter.2.cloned.1.call-done = f32[64,1024]{1,0:T(8,128)} async-done(((f32[2048,1024]{1,0:T(8,128)}), f32[64,1024]{1,0:T(8,128)}) %reduce-scatter.2.cloned.1.call-update) | async-done | bytes 262160 | tf_op jit(solution)/shard_map/reduce_scatter | solution.py:69
  929.1 0.0 copy-done.1
  929.1 0.0 copy-done.2
  929.1 1.7 subtract_add_fusion
  (12 shorter events, 0.1 us)
Async XLA Ops:
  6.5 36.7 %all-gather.3.cloned.1.call-start = ((), (), s32[]{:S(2)}) async-start(), calls=%async_computation.1 | async-start | bytes 2359296 | tf_op jit(solution)/shard_map/all_gather | solution.py:37
  7.3 118.3 %all-gather.5.cloned.1.call-start = ((), (), s32[]{:S(2)}) async-start(), calls=%async_computation.2 | async-start | bytes 4325376 | tf_op jit(solution)/shard_map/all_gather | solution.py:40
  8.0 921.1 %reduce-scatter.2.cloned.1.call-start = ((), (), s32[]{:S(2)}) async-start(), calls=%async_computation.3 | async-start | bytes 8650752 | tf_op jit(solution)/shard_map/reduce_scatter | solution.py:69
  544.5 125.2 %copy-start = (bf16[1024,1024]{1,0:T(8,128)(2,1)S(1)}, bf16[1024,1024]{1,0:T(8,128)(2,1)}, u32[]{:S(2)}) copy-start(bf16[1024,1024]{1,0:T(8,128)(2,1)} %all-gather.3.cloned.1.call-done) | copy-start | bytes 6291460
  681.4 247.7 %copy-start.1 = (bf16[64,1024]{1,0:T(8,128)(2,1)S(1)}, bf16[64,1024]{1,0:T(8,128)(2,1)}, u32[]{:S(2)}) copy-start(bf16[64,1024]{1,0:T(8,128)(2,1)} %param.4) | copy-start | bytes 393220
  681.4 247.7 %copy-start.2 = (f32[64,1024]{1,0:T(8,128)S(1)}, f32[64,1024]{1,0:T(8,128)}, u32[]{:S(2)}) copy-start(f32[64,1024]{1,0:T(8,128)} %param.5) | copy-start | bytes 786436
Sparse Core Ops, SparseCore 0:
  9.2 34.0 all-gather.2
  45.8 79.7 all-gather.4
  681.6 247.4 reduce-scatter.1
where the time goes:
time: 941 us; the launch traced here: 937 us
  blocking collectives  481 us (51%)
  waiting for transfers between devices  365 us (39%)
  other arithmetic  55.5 us (6%)
  matrix products  22.7 us (2%)
  between operations  13.3 us (1%)
    reduce_scatter x1, waiting for transfers between devices, shards(): lax.psum_scatter(partial_sums, 'dp', scatter_dimension=0, tiled=True)  248 us
    pmax x3, blocking collectives, target_softmax_normalizer(): highest = lax.pmax(maximal_element, 'dp')  178 us
    psum x3, blocking collectives, target_softmax_normalizer(): lax.psum(accumulated_exponential * jnp.exp(maximal_element - highest), 'dp')  171 us
    pmax x3, blocking collectives, source_softmax_normalizer(): highest = lax.pmax(maximal_element, 'gen')  94.3 us
    all_gather x1, waiting for transfers between devices, shards(): block_rows = lax.all_gather(generated, 'dp', axis=0, tiled=True)  80.3 us
    psum x3, blocking collectives, source_softmax_normalizer(): lax.psum(accumulated_exponential * jnp.exp(maximal_element - highest), 'g...  37.4 us
    all_gather x1, waiting for transfers between devices, shards(): private_rows = lax.all_gather(private, 'gen', axis=1, tiled=True)  35.2 us
  transfers between devices with their start and end apart: 3, of which 3 were waited for; matrix products, arithmetic and copies ran while one was open for 0% of the time, Pallas kernels for 0%

commit v1 on v0

v1 whole, which is shorter than its diff:
```python
import functools
import math

import jax
import jax.numpy as jnp
from jax import lax
from jax.experimental import pallas as pl
from jax.experimental.pallas import tpu as pltpu
from jax.sharding import Mesh
from jax.sharding import PartitionSpec as P


EPS = 0.02
F32 = jnp.float32
BF16 = jnp.bfloat16
F16 = jnp.float16
LANES = 128
SUB = 64


def to_rows(column):
    flat = jnp.transpose(column)[0:1, :]
    return jnp.concatenate(
        [flat[:, q * LANES:(q + 1) * LANES] for q in range(column.shape[0] // LANES)], axis=0
    )


def sum_to_rows(lanes):
    flat = jnp.sum(jnp.transpose(lanes), axis=0, keepdims=True)
    return jnp.concatenate(
        [flat[:, q * LANES:(q + 1) * LANES] for q in range(lanes.shape[0] // LANES)], axis=0
    )


def to_columns(rows, out_ref):
    for q in range(rows.shape[0]):
        out_ref[q * LANES:(q + 1) * LANES, :] = jnp.transpose(
            jnp.broadcast_to(rows[q:q + 1, :], (LANES, LANES))
        )


def logsumexp0(x):
    top = jnp.max(x, axis=0)
    return top + jnp.log(jnp.sum(jnp.exp(x - top[None]), axis=0))


def score_kernel(scale, p_ref, g_ref, t_ref, l_ref, c0_ref, rows_ref):
    step = pl.program_id(0)
    tiles = t_ref.shape[0]

    @pl.when(step == 0)
    def _():
        g = g_ref[...].astype(F32)
        sq = jnp.sum(g * g, axis=1, keepdims=True)
        c0_ref[...] = jnp.broadcast_to(sq * (-0.5 * scale), c0_ref.shape)

    p = jnp.concatenate([p_ref[0, f] for f in range(p_ref.shape[1])], axis=1)
    cross = lax.dot_general(g_ref[...], p, (((1,), (1,)), ((), ())), preferred_element_type=F32)
    for k in range(tiles):
        t = cross[:, k * LANES:(k + 1) * LANES] * scale + c0_ref[...]
        t_ref[k] = t
        top = jnp.max(t, axis=0, keepdims=True)
        rows_ref[pl.ds(step * tiles + k, 1), :] = top + jnp.log(
            jnp.sum(jnp.exp(t - top), axis=0, keepdims=True)
        )

    @pl.when(step == pl.num_programs(0) - 1)
    def _():
        l_ref[...] = jnp.broadcast_to(rows_ref[...][None], l_ref.shape)


def first_column_kernel(log_ng, l_ref, t_ref, r_ref, lc_ref, m_ref, s_ref):
    step = pl.program_id(0)
    tiles = t_ref.shape[0]

    @pl.when(step == 0)
    def _():
        r_ref[...] = log_ng - logsumexp0(l_ref[...])
        m_ref[...] = jnp.full(m_ref.shape, -1e38, F32)
        s_ref[...] = jnp.zeros(s_ref.shape, F32)

    r = [r_ref[pl.ds(step * tiles + k, 1), :] for k in range(tiles)]

    @pl.loop(0, m_ref.shape[0], step=SUB)
    def _(c):
        at = pl.ds(pl.multiple_of(c, SUB), SUB)
        u = [t_ref[k, at, :] + r[k] for k in range(tiles)]
        old = m_ref[at, :]
        top = old
        for k in range(tiles):
            top = jnp.maximum(top, u[k])
        s = s_ref[at, :] * jnp.exp(old - top)
        for k in range(tiles):
            s = s + jnp.exp(u[k] - top)
        m_ref[at, :] = top
        s_ref[at, :] = s

    @pl.when(step == pl.num_programs(0) - 1)
    def _():
        m = m_ref[...]
        top = jnp.max(m, axis=1, keepdims=True)
        total = jnp.sum(s_ref[...] * jnp.exp(m - top), axis=1, keepdims=True)
        lc = to_rows(jnp.broadcast_to(top + jnp.log(total), m.shape))
        lc_ref[...] = jnp.broadcast_to(lc[None], lc_ref.shape)


def plan_kernel(log_np, lc_ref, r_ref, t_ref, k_ref, rho_ref, c_ref, rows_ref):
    step = pl.program_id(0)
    tiles = t_ref.shape[0]

    @pl.when(step == 0)
    def _():
        to_columns(log_np - logsumexp0(lc_ref[...]), c_ref)

    for k in range(tiles):
        r = r_ref[pl.ds(step * tiles + k, 1), :]

        def body(i, total, k=k, r=r):
            at = pl.ds(pl.multiple_of(i * SUB, SUB), SUB)
            value = jnp.exp(t_ref[k, at, :] + (r + c_ref[at, :]))
            k_ref[k, at, :] = value
            return total + jnp.sum(value.reshape(SUB // 8, 8, LANES), axis=0)

        total = lax.fori_loop(0, c_ref.shape[0] // SUB, body, jnp.zeros((8, LANES), F32), unroll=2)
        rows_ref[pl.ds(step * tiles + k, 1), :] = jnp.sum(total, axis=0, keepdims=True)

    @pl.when(step == pl.num_programs(0) - 1)
    def _():
        rho_ref[...] = jnp.broadcast_to(rows_ref[...][None], rho_ref.shape)


def column_sum_kernel(ng, rho_ref, k_ref, sums_ref, u_ref, acc_ref):
    step = pl.program_id(0)
    tiles = k_ref.shape[0]

    @pl.when(step == 0)
    def _():
        u_ref[...] = ng / jnp.sum(rho_ref[...], axis=0)
        acc_ref[...] = jnp.zeros(acc_ref.shape, F32)

    u = [u_ref[pl.ds(step * tiles + k, 1), :] for k in range(tiles)]

    @pl.loop(0, acc_ref.shape[0], step=SUB)
    def _(c):
        at = pl.ds(pl.multiple_of(c, SUB), SUB)
        total = acc_ref[at, :]
        for k in range(tiles):
            total = total + k_ref[k, at, :] * u[k]
        acc_ref[at, :] = total

    @pl.when(step == pl.num_programs(0) - 1)
    def _():
        sums_ref[...] = jnp.broadcast_to(sum_to_rows(acc_ref[...])[None], sums_ref.shape)


def row_sum_kernel(np_, sums_ref, k_ref, v_ref, rho_ref, rows_ref):
    step = pl.program_id(0)
    tiles = k_ref.shape[0]

    @pl.when(step == 0)
    def _():
        to_columns(np_ / jnp.sum(sums_ref[...], axis=0), v_ref)

    def body(i, totals):
        at = pl.ds(pl.multiple_of(i * SUB, SUB), SUB)
        v = v_ref[at, :]
        return tuple(
            totals[k] + jnp.sum((k_ref[k, at, :] * v).reshape(SUB // 8, 8, LANES), axis=0)
            for k in range(tiles)
        )

    totals = lax.fori_loop(
        0, v_ref.shape[0] // SUB, body, tuple(jnp.zeros((8, LANES), F32) for _ in range(tiles))
    )
    for k in range(tiles):
        rows_ref[pl.ds(step * tiles + k, 1), :] = jnp.sum(totals[k], axis=0, keepdims=True)

    @pl.when(step == pl.num_programs(0) - 1)
    def _():
        rho_ref[...] = jnp.broadcast_to(rows_ref[...][None], rho_ref.shape)


def barycenter_kernel(ng, rho_ref, v_ref, k_ref, p_ref, out_ref, u_ref, mass_ref, acc_ref, w_ref):
    step = pl.program_id(0)
    tiles = k_ref.shape[0]

    @pl.when(step == 0)
    def _():
        u_ref[...] = ng / jnp.sum(rho_ref[...], axis=0)
        mass_ref[...] = jnp.zeros(mass_ref.shape, F32)
        acc_ref[...] = jnp.zeros(acc_ref.shape, F32)

    u = [u_ref[pl.ds(step * tiles + k, 1), :] for k in range(tiles)]

    @pl.loop(0, mass_ref.shape[0], step=SUB)
    def _(c):
        at = pl.ds(pl.multiple_of(c, SUB), SUB)
        v = v_ref[at, :]
        total = mass_ref[at, :]
        for k in range(tiles):
            w = k_ref[k, at, :] * u[k] * v
            total = total + w
            w_ref[at, k * LANES:(k + 1) * LANES] = w.astype(BF16)
        mass_ref[at, :] = total

    p = jnp.concatenate([p_ref[0, f] for f in range(p_ref.shape[1])], axis=1)
    acc_ref[...] += jnp.dot(w_ref[...], p, preferred_element_type=F32)

    @pl.when(step == pl.num_programs(0) - 1)
    def _():
        owners = out_ref.shape[0]
        rows = acc_ref.shape[0] // owners
        blocks = acc_ref.shape[1] // LANES
        mass = jnp.maximum(jnp.sum(mass_ref[...], axis=1, keepdims=True), 1e-30)
        inverse = jnp.broadcast_to(1.0 / mass, mass_ref.shape)
        log_mass = jnp.transpose(jnp.broadcast_to(jnp.log(mass), mass_ref.shape))[0:1, :]
        for z in range(owners):
            at = slice(z * rows, (z + 1) * rows)
            for q in range(blocks):
                out_ref[z, q * rows:(q + 1) * rows, :] = (
                    acc_ref[at, q * LANES:(q + 1) * LANES] * inverse[at, :]
                )
            part = jnp.concatenate([log_mass[:, at]] * (LANES // rows), axis=1)
            high = jnp.round(part * 16.0) * 0.0625
            low = part - high
            tail = jnp.concatenate([high] * 8 + [low] * 8, axis=0)
            out_ref[z, blocks * rows:, :] = tail


def update_kernel(parts_ref, g_ref, n_ref, out_ref):
    sources = parts_ref.shape[0]
    rows = g_ref.shape[0]
    blocks = g_ref.shape[1] // LANES
    at = blocks * rows
    logs = jnp.concatenate(
        [parts_ref[d, at:at + 1, :] + parts_ref[d, at + 8:at + 9, :] for d in range(sources)], axis=0
    )
    weights = jnp.exp(logs - jnp.max(logs, axis=0, keepdims=True))
    weights = weights / jnp.sum(weights, axis=0, keepdims=True)
    columns = [
        jnp.transpose(jnp.broadcast_to(weights[d:d + 1, :], (LANES, LANES)))[0:rows, :]
        for d in range(sources)
    ]
    for q in range(blocks):
        lanes = slice(q * LANES, (q + 1) * LANES)
        total = parts_ref[0, q * rows:(q + 1) * rows, :] * columns[0]
        for d in range(1, sources):
            total = total + parts_ref[d, q * rows:(q + 1) * rows, :] * columns[d]
        out_ref[:, lanes] = g_ref[:, lanes].astype(F32) - total + n_ref[:, lanes]


def whole(shape):
    return pl.BlockSpec(shape, lambda b: (0,) * len(shape))


def shards(private, generated, noise):
    rows_per, width = private.shape
    own, features = generated.shape
    nz, nx = lax.axis_size("z"), lax.axis_size("x")
    peers = ("x", "y", "core")
    n_peers = lax.axis_size(peers)
    cols = own * nz
    rows = rows_per * nx
    np_ = rows * nz
    ng = cols * n_peers
    scale = 2.0 / (features * EPS)
    row_tiles = rows // LANES
    col_tiles = cols // LANES
    tiles = 4
    steps = row_tiles // tiles
    block = tiles * LANES
    per = rows_per // block

    p = lax.all_gather(private, peers, axis=0, tiled=False)
    p = p.reshape(nx, n_peers // nx, rows_per, width)
    g = jnp.broadcast_to(generated[None], (nz, own, features))
    g = lax.all_to_all(g, "z", 0, 0, tiled=True).reshape(cols, features)

    params = pltpu.CompilerParams(
        dimension_semantics=("arbitrary",), vmem_limit_bytes=32 * 1024 * 1024
    )
    p_spec = pl.BlockSpec(
        (1, n_peers // nx, block, width), lambda b: (b // per, 0, b % per, 0)
    )
    t_spec = pl.BlockSpec((tiles, cols, LANES), lambda b: (b, 0, 0))
    t_shape = jax.ShapeDtypeStruct((row_tiles, cols, LANES), F32)
    row_shape = (n_peers, row_tiles, LANES)
    col_shape = (nz, col_tiles, LANES)
    row_out = jax.ShapeDtypeStruct(row_shape, F32)
    col_out = jax.ShapeDtypeStruct(col_shape, F32)
    rows_scratch = pltpu.VMEM((row_tiles, LANES), F32)
    cols_scratch = pltpu.VMEM((cols, LANES), F32)

    def over_peers(a):
        return lax.all_to_all(a, peers, 0, 0, tiled=True)

    def over_z(a):
        return lax.all_to_all(a, "z", 0, 0, tiled=True)

    t, lr = pl.pallas_call(
        functools.partial(score_kernel, scale),
        grid=(steps,),
        in_specs=[p_spec, whole((cols, features))],
        out_specs=[t_spec, whole(row_shape)],
        out_shape=[t_shape, row_out],
        scratch_shapes=[cols_scratch, rows_scratch],
        compiler_params=params,
        name="scores",
    )(p, g)
    lr = over_peers(lr)

    r, lc = pl.pallas_call(
        functools.partial(first_column_kernel, math.log(ng)),
        grid=(steps,),
        in_specs=[whole(row_shape), t_spec],
        out_specs=[whole((row_tiles, LANES)), whole(col_shape)],
        out_shape=[jax.ShapeDtypeStruct((row_tiles, LANES), F32), col_out],
        scratch_shapes=[cols_scratch, cols_scratch],
        compiler_params=params,
        name="first_columns",
    )(lr, t)
    lc = over_z(lc)

    k, rho = pl.pallas_call(
        functools.partial(plan_kernel, math.log(np_)),
        grid=(steps,),
        in_specs=[whole(col_shape), whole((row_tiles, LANES)), t_spec],
        out_specs=[t_spec, whole(row_shape)],
        out_shape=[t_shape, row_out],
        scratch_shapes=[cols_scratch, rows_scratch],
        compiler_params=params,
        name="plan",
    )(lc, r, t)
    rho = over_peers(rho)

    sums = pl.pallas_call(
        functools.partial(column_sum_kernel, float(ng)),
        grid=(steps,),
        in_specs=[whole(row_shape), t_spec],
        out_specs=whole(col_shape),
        out_shape=col_out,
        scratch_shapes=[rows_scratch, cols_scratch],
        compiler_params=params,
        name="column_sums",
    )(rho, k)
    sums = over_z(sums)

    v, rho = pl.pallas_call(
        functools.partial(row_sum_kernel, float(np_)),
        grid=(steps,),
        in_specs=[whole(col_shape), t_spec],
        out_specs=[whole((cols, LANES)), whole(row_shape)],
        out_shape=[jax.ShapeDtypeStruct((cols, LANES), F32), row_out],
        scratch_shapes=[rows_scratch],
        compiler_params=params,
        name="row_sums",
    )(sums, k)
    rho = over_peers(rho)

    part_shape = (nz, own * (features // LANES) + 16, LANES)
    parts = pl.pallas_call(
        functools.partial(barycenter_kernel, float(ng)),
        grid=(steps,),
        in_specs=[whole(row_shape), whole((cols, LANES)), t_spec, p_spec],
        out_specs=whole(part_shape),
        out_shape=jax.ShapeDtypeStruct(part_shape, F32),
        scratch_shapes=[
            rows_scratch,
            cols_scratch,
            pltpu.VMEM((cols, features), F32),
            pltpu.VMEM((cols, block), BF16),
        ],
        compiler_params=params,
        name="barycenter",
    )(rho, v, k, p)
    parts = over_z(parts.astype(F16)).astype(F32)

    return pl.pallas_call(
        update_kernel,
        out_shape=jax.ShapeDtypeStruct((own, features), F32),
        compiler_params=pltpu.CompilerParams(vmem_limit_bytes=32 * 1024 * 1024),
        name="update",
    )(parts, generated, noise)


def solution(mesh):
    fine = Mesh(mesh.devices.reshape(8, 4, 4, 2), ("z", "x", "y", "core"))
    in_specs = (
        P(("z", "x"), ("y", "core")),
        P(("y", "core", "z", "x"), None),
        P(("y", "core", "z", "x"), None),
    )
    out_specs = P(("y", "core", "z", "x"), None)
    return jax.shard_map(shards, mesh=fine, in_specs=in_specs, out_specs=out_specs, check_vma=False)
```

time: 941 us -> 219 us (0.23)
  blocking collectives: 481 us -> 140 us
  waiting for transfers between devices: 365 us -> 28.5 us
  other arithmetic: 55.5 us -> 0.28 us
  Pallas kernels: 0 us -> 27.5 us
  matrix products: 22.7 us -> 0 us
    pmax x6 -> x0, blocking collectives: 273 us -> none  [the longest x3 178 us: target_softmax_normalizer(): highest = lax.pmax(maximal_element, 'dp')]
    reduce_scatter x1 -> x0, waiting for transfers between devices: 248 us -> none  [shards(): lax.psum_scatter(partial_sums, 'dp', scatter_dimension=0, tiled=True)]
    psum x6 -> x0, blocking collectives: 209 us -> none  [the longest x3 171 us: target_softmax_normalizer(): lax.psum(accumulated_exponential * jnp.exp(maximal_element - highest), 'dp')]
    all_to_all x0 -> x7, blocking collectives: none -> 140 us  [the longest x3 54.5 us: over_z(): return lax.all_to_all(a, 'z', 0, 0, tiled=True)]
    all_gather x2 -> x1, waiting for transfers between devices: 115 us -> 27.8 us  [shards(): p = lax.all_gather(private, peers, axis=0, tiled=False)]
    reduce_sum x8 -> x0, other arithmetic: 32.2 us -> none  [the longest x3 13.5 us: target_softmax_normalizer(): jnp.sum(jnp.exp(kernel_grid - maximal_element[None, :]), axis=0)]
    pallas_call x0 -> x7, Pallas kernels: none -> 27.5 us  [the longest x1 8.59 us: shards(): pl.pallas_call(functools.partial(score_kernel, scale), grid=(steps,), in_...]
    dot_general x2 -> x0, matrix products: 22.7 us -> none  [the longest x1 11.7 us: shards(): jnp.einsum('ij,id->jd', coupling_plan, private_rows, preferred_element_ty...]
  transfers between devices with their start and end apart: 3 -> 1, of which waited for: 3 -> 1; matrix products, arithmetic and copies ran while one was open for 0% -> 0% of each run, Pallas kernels for 0% -> 0%
where the time goes in v1:
time: 219 us; the launch traced here: 218 us
  blocking collectives  140 us (64%)
  waiting for transfers between devices  28.5 us (13%)
  Pallas kernels  27.5 us (13%)
  between operations  13.5 us (6%)
  local copies, waits for them, and re-layouts  8.67 us (4%)
    all_to_all x3, blocking collectives, over_z(): return lax.all_to_all(a, 'z', 0, 0, tiled=True)  54.5 us
    all_to_all x3, blocking collectives, over_peers(): return lax.all_to_all(a, peers, 0, 0, tiled=True)  49.5 us
    all_to_all x1, blocking collectives, shards(): g = lax.all_to_all(g, 'z', 0, 0, tiled=True).reshape(cols, features)  36 us
    all_gather x1, waiting for transfers between devices, shards(): p = lax.all_gather(private, peers, axis=0, tiled=False)  27.8 us
    pallas_call x1, Pallas kernels, shards(): pl.pallas_call(functools.partial(score_kernel, scale), grid=(steps,), in_...  8.59 us
    pallas_call x1, Pallas kernels, shards(): pl.pallas_call(functools.partial(barycenter_kernel, float(ng)), grid=(ste...  8.54 us
    unnamed x14, local copies, waits for them, and re-layouts  7.65 us
  transfers between devices with their start and end apart: 1, of which 1 were waited for; matrix products, arithmetic and copies ran while one was open for 0% of the time, Pallas kernels for 0%

profile of v1, /device:TPU:1, one launch (start us, length us, event | category | flops | bytes accessed | tf_op | source)
XLA Modules:
  0.0 218.5 jit_solution(13948320822557684990)
XLA Ops:
  6.5 0.0 all-gather.3.cloned.1.call-start
  6.5 0.7 all-gather.3.cloned.1.call-update
  7.3 1.0 broadcast_in_dim.2
  8.3 36.0 %all_to_all.35 = bf16[8,64,1024]{2,1,0:T(8,128)(2,1)S(1)} all-to-all(bf16[8,64,1024]{2,1,0:T(8,128)(2,1)S(1)} %broadcast_in_dim.2), channel_id=1, replica_groups=mesh['z'=8,'x'=4,'y'=4,'core'=2] {'z'}, dimensions={0} | all-to-all | bytes 2097152 | tf_op jit(solution)/shard_map/all_to_all | solution.py:277
  44.3 27.8 %all-gather.3.cloned.1.call-done = bf16[32768,128]{1,0:T(8,128)(2,1)} async-done(((bf16[1024,128]{1,0:T(8,128)(2,1)}), bf16[32768,128]{1,0:T(8,128)(2,1)}) %all-gather.3.cloned.1.call-update) | async-done | bytes 8388624 | tf_op jit(solution)/shard_map/all_gather | solution.py:274
  72.1 0.0 copy-start
  72.1 3.4 %copy-done = bf16[32768,128]{1,0:T(8,128)(2,1)S(1)} copy-done((bf16[32768,128]{1,0:T(8,128)(2,1)S(1)}, bf16[32768,128]{1,0:T(8,128)(2,1)}, u32[]{:S(2)}) %copy-start) | copy-done | bytes 8388632
  75.5 8.6 %scores.1 = (f32[32,512,128]{2,1,0:T(8,128)S(1)}, f32[32,32,128]{2,1,0:T(8,128)S(1)}) custom-call(bf16[4,8,1024,128]{3,2,1,0:T(8,128)(2,1)S(1)} %bitcast.2, bf16[512,1024]{1,0:T(8,128)(2,1)S(1)} %bitcast.6), custom_call_target="tpu_custom_call" | custom-call | tf_op jit(solution)/shard_map/scores/pallas_call | solution.py:300
  84.1 0.0 copy-start.1
  84.1 16.9 %all_to_all.36.l_ref = f32[32,32,128]{2,1,0:T(8,128)S(1)} all-to-all(f32[32,32,128]{2,1,0:T(8,128)S(1)} %get-tuple-element.13), channel_id=1, replica_groups=mesh['z'=8,'x'=4,'y'=4,'core'=2] {'x','y','core'}, dimensions={0} | all-to-all | bytes 1048576 | tf_op jit(solution)/shard_map/all_to_all | solution.py:295
  101.0 3.0 %first_columns.1 = (f32[32,128]{1,0:T(8,128)S(1)}, f32[8,4,128]{2,1,0:T(4,128)S(1)}) custom-call(f32[32,32,128]{2,1,0:T(8,128)S(1)} %all_to_all.36.l_ref, f32[32,512,128]{2,1,0:T(8,128)S(1)} %get-tuple-element.14.t_ref), custom_call_target="tpu_custom_call" | custom-call | tf_op jit(solution)/shard_map/first_columns/pallas_call | solution.py:312
  103.9 0.0 copy-done.1
  104.0 13.2 %all_to_all.37.lc_ref = f32[8,4,128]{2,1,0:T(4,128)S(1)} all-to-all(f32[8,4,128]{2,1,0:T(4,128)S(1)} %get-tuple-element.15), channel_id=1, replica_groups=mesh['z'=8,'x'=4,'y'=4,'core'=2] {'z'}, dimensions={0} | all-to-all | bytes 32768 | tf_op jit(solution)/shard_map/all_to_all | solution.py:298
  117.1 0.0 copy-start.2
  117.1 3.4 %copy-done.2 = f32[32,512,128]{2,1,0:T(8,128)S(1)} copy-done((f32[32,512,128]{2,1,0:T(8,128)S(1)}, f32[32,512,128]{2,1,0:T(8,128)}, u32[]{:S(2)}) %copy-start.2) | copy-done | bytes 8388632
  120.5 3.6 %plan.1 = (f32[32,512,128]{2,1,0:T(8,128)S(1)}, f32[32,32,128]{2,1,0:T(8,128)S(1)}) custom-call(f32[8,4,128]{2,1,0:T(4,128)S(1)} %all_to_all.37.lc_ref, f32[32,128]{1,0:T(8,128)S(1)} %get-tuple-element.16.r_ref, f32[32,512,128]{2,1,0:T(8,128)S(1)} %copy-done.2), custom_call_target="tpu_custom_call" | custom-call | tf_op jit(solution)/shard_map/plan/pallas_call | solution.py:324
  124.1 16.5 %all_to_all.38.rho_ref = f32[32,32,128]{2,1,0:T(8,128)S(1)} all-to-all(f32[32,32,128]{2,1,0:T(8,128)S(1)} %get-tuple-element.17), channel_id=1, replica_groups=mesh['z'=8,'x'=4,'y'=4,'core'=2] {'x','y','core'}, dimensions={0} | all-to-all | bytes 1048576 | tf_op jit(solution)/shard_map/all_to_all | solution.py:295
  140.6 0.0 slice-start
  140.6 1.3 column_sums.1
  141.9 9.0 %all_to_all.39.sums_ref = f32[8,4,128]{2,1,0:T(4,128)S(1)} all-to-all(f32[8,4,128]{2,1,0:T(4,128)S(1)} %column_sums.1), channel_id=1, replica_groups=mesh['z'=8,'x'=4,'y'=4,'core'=2] {'z'}, dimensions={0} | all-to-all | bytes 32768 | tf_op jit(solution)/shard_map/all_to_all | solution.py:298
  150.9 0.0 slice-start.1
  150.9 1.5 row_sums.1
  152.3 16.2 %all_to_all.40.rho_ref = f32[32,32,128]{2,1,0:T(8,128)S(1)} all-to-all(f32[32,32,128]{2,1,0:T(8,128)S(1)} %get-tuple-element.19), channel_id=1, replica_groups=mesh['z'=8,'x'=4,'y'=4,'core'=2] {'x','y','core'}, dimensions={0} | all-to-all | bytes 1048576 | tf_op jit(solution)/shard_map/all_to_all | solution.py:295
  168.5 0.0 slice-done
  168.6 0.0 slice-done.1
  168.6 8.5 %barycenter.1 = f32[8,528,128]{2,1,0:T(8,128)S(1)} custom-call(f32[32,32,128]{2,1,0:T(8,128)S(1)} %all_to_all.40.rho_ref, f32[512,128]{1,0:T(8,128)S(1)} %get-tuple-element.20.v_ref, f32[32,512,128]{2,1,0:T(8,128)S(1)} %get-tuple-element.18.k_ref, bf16[4,8,1024,128]{3,2,1,0:T(8,128)(2,1)S(1)} %bitcast.5), custom_call_target="tpu_custom_call" | custom-call | tf_op jit(solution)/shard_map/barycenter/pallas_call | solution.py:361
  177.1 0.1 convert_element_type.6
  177.3 32.4 %all_to_all.41 = f16[8,528,128]{2,1,0:T(8,128)(2,1)S(1)} all-to-all(f16[8,528,128]{2,1,0:T(8,128)(2,1)S(1)} %convert_element_type.6), channel_id=1, replica_groups=mesh['z'=8,'x'=4,'y'=4,'core'=2] {'z'}, dimensions={0} | all-to-all | bytes 2162688 | tf_op jit(solution)/shard_map/all_to_all | solution.py:298
  209.6 0.0 copy-start.3
  209.6 0.0 copy-start.4
  209.6 0.1 convert_element_type.7.parts_ref
  209.8 0.8 copy-done.3
  210.5 0.1 copy-done.4
  210.6 1.0 update.1
  (1 shorter events, 0.0 us)
Async XLA Ops:
  6.5 65.5 %all-gather.3.cloned.1.call-start = ((), (), s32[]{:S(2)}) async-start(), calls=%async_computation.7 | async-start | bytes 8650752 | tf_op jit(solution)/shard_map/all_gather | solution.py:274
  72.1 3.4 %copy-start = (bf16[32768,128]{1,0:T(8,128)(2,1)S(1)}, bf16[32768,128]{1,0:T(8,128)(2,1)}, u32[]{:S(2)}) copy-start(bf16[32768,128]{1,0:T(8,128)(2,1)} %all-gather.3.cloned.1.call-done) | copy-start | bytes 25165828
  84.1 19.9 %copy-start.1 = (f32[32,512,128]{2,1,0:T(8,128)}, f32[32,512,128]{2,1,0:T(8,128)S(1)}, u32[]{:S(2)}) copy-start(f32[32,512,128]{2,1,0:T(8,128)S(1)} %get-tuple-element.14.t_ref) | copy-start | bytes 25165828
  117.1 3.4 %copy-start.2 = (f32[32,512,128]{2,1,0:T(8,128)S(1)}, f32[32,512,128]{2,1,0:T(8,128)}, u32[]{:S(2)}) copy-start(f32[32,512,128]{2,1,0:T(8,128)} %copy-done.1) | copy-start | bytes 25165828
  140.6 28.0 %slice-start = ((s8[8388608]{0:T(1024)(128)(4,1)}), s8[4194304]{0:T(1024)(128)(4,1)S(1)}, s32[]{:S(2)}) async-start(s8[8388608]{0:T(1024)(128)(4,1)} %bitcast.3), calls=%async_computation.8 | async-start | bytes 8388608
  150.9 17.7 %slice-start.1 = ((s8[8388608]{0:T(1024)(128)(4,1)}), s8[4194304]{0:T(1024)(128)(4,1)S(1)}, s32[]{:S(2)}) async-start(s8[8388608]{0:T(1024)(128)(4,1)} %bitcast.3), calls=%async_computation.9 | async-start | bytes 8388608
  209.6 0.9 copy-start.3
  209.6 1.0 copy-start.4
Sparse Core Ops, SparseCore 0:
  9.9 62.1 all-gather.2

commit v2 on v1

--- a/solution.py
+++ b/solution.py
@@ -1,4 +1,5 @@
 import functools
+import itertools
 import math
 
 import jax
@@ -44,25 +45,62 @@
     return top + jnp.log(jnp.sum(jnp.exp(x - top[None]), axis=0))
 
 
-def score_kernel(scale, p_ref, g_ref, t_ref, l_ref, c0_ref, rows_ref):
-    step = pl.program_id(0)
+def score_kernel(scale, *refs):
+    blocks, (own_ref, far_ref, near_ref, swapped_ref) = refs[:8], refs[8:12]
+    p_ref, t_ref, l_ref, g_ref, c0_ref, rows_ref = refs[12:]
+    step = pl.program_id(0)
+    nx, slices, rows, width = p_ref.shape
+    ny = slices // 2
+    nz = 8
+    x, y, z, core = (lax.axis_index(a) for a in ("x", "y", "z", "core"))
     tiles = t_ref.shape[0]
 
     @pl.when(step == 0)
     def _():
-        g = g_ref[...].astype(F32)
-        sq = jnp.sum(g * g, axis=1, keepdims=True)
-        c0_ref[...] = jnp.broadcast_to(sq * (-0.5 * scale), c0_ref.shape)
-
-    p = jnp.concatenate([p_ref[0, f] for f in range(p_ref.shape[1])], axis=1)
-    cross = lax.dot_general(g_ref[...], p, (((1,), (1,)), ((), ())), preferred_element_type=F32)
-    for k in range(tiles):
-        t = cross[:, k * LANES:(k + 1) * LANES] * scale + c0_ref[...]
-        t_ref[k] = t
-        top = jnp.max(t, axis=0, keepdims=True)
-        rows_ref[pl.ds(step * tiles + k, 1), :] = top + jnp.log(
-            jnp.sum(jnp.exp(t - top), axis=0, keepdims=True)
-        )
+        first = ((0, -1), (1, -2))
+        for ref, pair, second in zip(blocks, (0, 1, 0, 0, 1, 1, 0, 1), (0, 0, -1, 1, -1, 1, -2, 2)):
+            for n in range(2):
+                a, b = first[pair][n], second
+                px = lax.rem(x + jnp.where(core == 0, a, b) + nx, nx)
+                py = lax.rem(y + jnp.where(core == 0, b, a) + ny, ny)
+                for f in range(2):
+                    p_ref[px, 2 * py + f] = ref[n, f]
+
+        own = g_ref.shape[0] // (2 * nz)
+
+        def put(ref, at, k):
+            pz = lax.rem(z + k + nz, nz)
+            for c in range(2):
+                g_ref[pl.ds(pl.multiple_of((c * nz + pz) * own, own), own), :] = ref[at + (c,)]
+
+        sign = jnp.where(core == 0, -1, 1)
+        put(own_ref, (), 0)
+        put(far_ref, (), 4)
+        for k in range(1, 4):
+            put(near_ref, (k - 1,), sign * k)
+            put(swapped_ref, (k - 1,), -sign * k)
+
+        def squares(i, carry):
+            at = pl.ds(pl.multiple_of(i * LANES, LANES), LANES)
+            g = g_ref[at, :].astype(F32)
+            sq = jnp.sum(g * g, axis=1, keepdims=True)
+            c0_ref[at, :] = jnp.broadcast_to(sq * (-0.5 * scale), (LANES, LANES))
+            return carry
+
+        lax.fori_loop(0, g_ref.shape[0] // LANES, squares, 0)
+
+    for half in range(2):
+        at = slice(half * rows // 2, (half + 1) * rows // 2)
+        p = jnp.concatenate([p_ref[step, f, at, :] for f in range(slices)], axis=1)
+        cross = lax.dot_general(g_ref[...], p, (((1,), (1,)), ((), ())), preferred_element_type=F32)
+        for n in range(tiles // 2):
+            k = half * (tiles // 2) + n
+            t = cross[:, n * LANES:(n + 1) * LANES] * scale + c0_ref[...]
+            t_ref[k] = t
+            top = jnp.max(t, axis=0, keepdims=True)
+            rows_ref[pl.ds(step * tiles + k, 1), :] = top + jnp.log(
+                jnp.sum(jnp.exp(t - top), axis=0, keepdims=True)
+            )
 
     @pl.when(step == pl.num_programs(0) - 1)
     def _():
@@ -180,51 +218,60 @@
         rho_ref[...] = jnp.broadcast_to(rows_ref[...][None], rho_ref.shape)
 
 
-def barycenter_kernel(ng, rho_ref, v_ref, k_ref, p_ref, out_ref, u_ref, mass_ref, acc_ref, w_ref):
+def barycenter_kernel(ng, other, rho_ref, v_ref, k_ref, p_ref, out_ref, u_ref, mass_ref, w_ref):
     step = pl.program_id(0)
     tiles = k_ref.shape[0]
+    cols, features = mass_ref.shape[0], out_ref.shape[1]
+    core = lax.axis_index("core")
+    begin = pl.multiple_of((1 - core if other else core) * cols, cols)
 
     @pl.when(step == 0)
     def _():
         u_ref[...] = ng / jnp.sum(rho_ref[...], axis=0)
         mass_ref[...] = jnp.zeros(mass_ref.shape, F32)
-        acc_ref[...] = jnp.zeros(acc_ref.shape, F32)
+        out_ref[...] = jnp.zeros(out_ref.shape, F32)
 
     u = [u_ref[pl.ds(step * tiles + k, 1), :] for k in range(tiles)]
 
-    @pl.loop(0, mass_ref.shape[0], step=SUB)
+    @pl.loop(0, cols, step=SUB)
     def _(c):
         at = pl.ds(pl.multiple_of(c, SUB), SUB)
-        v = v_ref[at, :]
+        source = pl.ds(pl.multiple_of(begin + c, SUB), SUB)
+        v = v_ref[source, :]
         total = mass_ref[at, :]
         for k in range(tiles):
-            w = k_ref[k, at, :] * u[k] * v
+            w = k_ref[k, source, :] * u[k] * v
             total = total + w
             w_ref[at, k * LANES:(k + 1) * LANES] = w.astype(BF16)
         mass_ref[at, :] = total
 
     p = jnp.concatenate([p_ref[0, f] for f in range(p_ref.shape[1])], axis=1)
-    acc_ref[...] += jnp.dot(w_ref[...], p, preferred_element_type=F32)
-
-    @pl.when(step == pl.num_programs(0) - 1)
-    def _():
-        owners = out_ref.shape[0]
-        rows = acc_ref.shape[0] // owners
-        blocks = acc_ref.shape[1] // LANES
-        mass = jnp.maximum(jnp.sum(mass_ref[...], axis=1, keepdims=True), 1e-30)
-        inverse = jnp.broadcast_to(1.0 / mass, mass_ref.shape)
-        log_mass = jnp.transpose(jnp.broadcast_to(jnp.log(mass), mass_ref.shape))[0:1, :]
-        for z in range(owners):
-            at = slice(z * rows, (z + 1) * rows)
-            for q in range(blocks):
-                out_ref[z, q * rows:(q + 1) * rows, :] = (
-                    acc_ref[at, q * LANES:(q + 1) * LANES] * inverse[at, :]
-                )
-            part = jnp.concatenate([log_mass[:, at]] * (LANES // rows), axis=1)
-            high = jnp.round(part * 16.0) * 0.0625
-            low = part - high
-            tail = jnp.concatenate([high] * 8 + [low] * 8, axis=0)
-            out_ref[z, blocks * rows:, :] = tail
+    out_ref[0:cols, :] += jnp.dot(w_ref[...], p, preferred_element_type=F32)
+
+    @pl.when(step == pl.num_programs(0) - 1)
+    def _():
+        mass = jnp.sum(jnp.transpose(mass_ref[...]), axis=0, keepdims=True)
+        out_ref[cols:, 0:cols] = jnp.broadcast_to(mass, (out_ref.shape[0] - cols, cols))
+
+
+def mean_kernel(a_ref, b_ref, out_ref):
+    owners = out_ref.shape[0]
+    features = a_ref.shape[1]
+    blocks = features // LANES
+    rows = (out_ref.shape[1] - 16) // blocks
+    cols = owners * rows
+    mass = jnp.maximum(a_ref[cols:cols + 1, 0:cols] + b_ref[cols:cols + 1, 0:cols], 1e-30)
+    log_mass = jnp.log(mass)
+    inverse = jnp.transpose(jnp.broadcast_to(1.0 / mass, (LANES, cols)))
+    for z in range(owners):
+        at = slice(z * rows, (z + 1) * rows)
+        for q in range(blocks):
+            lanes = slice(q * LANES, (q + 1) * LANES)
+            out_ref[z, q * rows:(q + 1) * rows, :] = (a_ref[at, lanes] + b_ref[at, lanes]) * inverse[at, :]
+        part = jnp.concatenate([log_mass[:, at]] * (LANES // rows), axis=1)
+        high = jnp.round(part * 16.0) * 0.0625
+        low = part - high
+        out_ref[z, blocks * rows:, :] = jnp.concatenate([high] * 8 + [low] * 8, axis=0)
 
 
 def update_kernel(parts_ref, g_ref, n_ref, out_ref):
@@ -253,61 +300,101 @@
     return pl.BlockSpec(shape, lambda b: (0,) * len(shape))
 
 
+def permuted(a, axes, moved):
+    sizes = [lax.axis_size(n) for n in axes]
+    flat = lambda at: functools.reduce(lambda f, cn: f * cn[1] + cn[0] % cn[1], zip(at, sizes), 0)
+    pairs = [(flat(at), flat(moved(*at))) for at in itertools.product(*map(range, sizes))]
+    return lax.ppermute(a, axes, pairs)
+
+
+def along(first, d, a):
+    return permuted(
+        a,
+        ("x", "y", "core"),
+        lambda x, y, c: (x + d, y, c) if (c == 0) == first else (x, y + d, c),
+    )
+
+
+def swap(a):
+    return permuted(a, ("core",), lambda c: (1 - c,))
+
+
+def gather_private(private):
+    core = lax.axis_index("core")
+    rows, width = private.shape
+    halves = private.reshape(2, rows // 2, width)
+    mine = lax.dynamic_index_in_dim(halves, core, 0, False)
+    got = swap(lax.dynamic_index_in_dim(halves, 1 - core, 0, False))
+    a0 = jnp.where(core == 0, jnp.stack([mine, got]), jnp.stack([got, mine]))
+    a1 = along(True, 1, a0)
+    a2 = along(True, -1, a0)
+    a3 = along(True, 1, a1)
+    s, t = jnp.stack([a0, a1]), jnp.stack([a2, a3])
+    s1, s2 = along(False, 1, s), along(False, -1, s)
+    t1, t2 = along(False, 1, t), along(False, -1, t)
+    return s, t, s1, s2, t1, t2, along(False, 1, s1), along(False, -1, t2)
+
+
+def gather_generated(generated):
+    core = lax.axis_index("core")
+    got = swap(generated)
+    pair = jnp.where(core == 0, jnp.stack([generated, got]), jnp.stack([got, generated]))
+    chain = [pair]
+    for _ in range(4):
+        chain.append(
+            permuted(chain[-1], ("z", "core"), lambda z, c: (z + (1 if c == 0 else -1), c))
+        )
+    near = jnp.stack(chain[1:4])
+    return pair, chain[4], near, swap(near)
+
+
 def shards(private, generated, noise):
     rows_per, width = private.shape
     own, features = generated.shape
-    nz, nx = lax.axis_size("z"), lax.axis_size("x")
-    peers = ("x", "y", "core")
-    n_peers = lax.axis_size(peers)
-    cols = own * nz
-    rows = rows_per * nx
-    np_ = rows * nz
-    ng = cols * n_peers
+    nz, nx, ny = lax.axis_size("z"), lax.axis_size("x"), lax.axis_size("y")
+    cols = own * nz * 2
+    rows = rows_per // 2 * nx
+    np_ = rows * nz * 2
+    ng = cols * nx * ny
     scale = 2.0 / (features * EPS)
     row_tiles = rows // LANES
     col_tiles = cols // LANES
     tiles = 4
     steps = row_tiles // tiles
     block = tiles * LANES
-    per = rows_per // block
-
-    p = lax.all_gather(private, peers, axis=0, tiled=False)
-    p = p.reshape(nx, n_peers // nx, rows_per, width)
-    g = jnp.broadcast_to(generated[None], (nz, own, features))
-    g = lax.all_to_all(g, "z", 0, 0, tiled=True).reshape(cols, features)
 
     params = pltpu.CompilerParams(
-        dimension_semantics=("arbitrary",), vmem_limit_bytes=32 * 1024 * 1024
-    )
-    p_spec = pl.BlockSpec(
-        (1, n_peers // nx, block, width), lambda b: (b // per, 0, b % per, 0)
-    )
+        dimension_semantics=("arbitrary",), vmem_limit_bytes=40 * 1024 * 1024
+    )
+    p_shape = (nx, 2 * ny, rows_per // 2, width)
+    p_spec = pl.BlockSpec((1,) + p_shape[1:], lambda b: (b, 0, 0, 0))
     t_spec = pl.BlockSpec((tiles, cols, LANES), lambda b: (b, 0, 0))
     t_shape = jax.ShapeDtypeStruct((row_tiles, cols, LANES), F32)
-    row_shape = (n_peers, row_tiles, LANES)
-    col_shape = (nz, col_tiles, LANES)
+    row_shape = (nx * ny, row_tiles, LANES)
+    col_shape = (nz * 2, col_tiles, LANES)
     row_out = jax.ShapeDtypeStruct(row_shape, F32)
     col_out = jax.ShapeDtypeStruct(col_shape, F32)
     rows_scratch = pltpu.VMEM((row_tiles, LANES), F32)
     cols_scratch = pltpu.VMEM((cols, LANES), F32)
 
-    def over_peers(a):
-        return lax.all_to_all(a, peers, 0, 0, tiled=True)
-
-    def over_z(a):
-        return lax.all_to_all(a, "z", 0, 0, tiled=True)
-
-    t, lr = pl.pallas_call(
+    def over_rows(a):
+        return lax.all_to_all(a, ("x", "y"), 0, 0, tiled=True)
+
+    def over_columns(a):
+        return lax.all_to_all(a, ("z", "core"), 0, 0, tiled=True)
+
+    gathered = gather_private(private) + gather_generated(generated)
+    p, t, lr = pl.pallas_call(
         functools.partial(score_kernel, scale),
         grid=(steps,),
-        in_specs=[p_spec, whole((cols, features))],
-        out_specs=[t_spec, whole(row_shape)],
-        out_shape=[t_shape, row_out],
-        scratch_shapes=[cols_scratch, rows_scratch],
+        in_specs=[whole(a.shape) for a in gathered],
+        out_specs=[whole(p_shape), t_spec, whole(row_shape)],
+        out_shape=[jax.ShapeDtypeStruct(p_shape, BF16), t_shape, row_out],
+        scratch_shapes=[pltpu.VMEM((cols, features), BF16), cols_scratch, rows_scratch],
         compiler_params=params,
         name="scores",
-    )(p, g)
-    lr = over_peers(lr)
+    )(*gathered)
+    lr = over_rows(lr)
 
     r, lc = pl.pallas_call(
         functools.partial(first_column_kernel, math.log(ng)),
@@ -319,7 +406,7 @@
         compiler_params=params,
         name="first_columns",
     )(lr, t)
-    lc = over_z(lc)
+    lc = over_columns(lc)
 
     k, rho = pl.pallas_call(
         functools.partial(plan_kernel, math.log(np_)),
@@ -331,7 +418,7 @@
         compiler_params=params,
         name="plan",
     )(lc, r, t)
-    rho = over_peers(rho)
+    rho = over_rows(rho)
 
     sums = pl.pallas_call(
         functools.partial(column_sum_kernel, float(ng)),
@@ -343,7 +430,7 @@
         compiler_params=params,
         name="column_sums",
     )(rho, k)
-    sums = over_z(sums)
+    sums = over_columns(sums)
 
     v, rho = pl.pallas_call(
         functools.partial(row_sum_kernel, float(np_)),
@@ -355,30 +442,43 @@
         compiler_params=params,
         name="row_sums",
     )(sums, k)
-    rho = over_peers(rho)
-
-    part_shape = (nz, own * (features // LANES) + 16, LANES)
+    rho = over_rows(rho)
+
+    def barycenter(other):
+        half = cols // 2
+        return pl.pallas_call(
+            functools.partial(barycenter_kernel, float(ng), other),
+            grid=(steps,),
+            in_specs=[whole(row_shape), whole((cols, LANES)), t_spec, p_spec],
+            out_specs=whole((half + 8, features)),
+            out_shape=jax.ShapeDtypeStruct((half + 8, features), F32),
+            scratch_shapes=[
+                rows_scratch,
+                pltpu.VMEM((half, LANES), F32),
+                pltpu.VMEM((half, block), BF16),
+            ],
+            compiler_params=params,
+            cost_estimate=pl.CostEstimate(
+                flops=2 * half * rows * features, bytes_accessed=16 << 20, transcendentals=0
+            ),
+            name="barycenter_other" if other else "barycenter_own",
+        )(rho, v, k, p)
+
+    theirs = swap(barycenter(True))
+    mine = barycenter(False)
+    small = pltpu.CompilerParams(vmem_limit_bytes=32 * 1024 * 1024)
     parts = pl.pallas_call(
-        functools.partial(barycenter_kernel, float(ng)),
-        grid=(steps,),
-        in_specs=[whole(row_shape), whole((cols, LANES)), t_spec, p_spec],
-        out_specs=whole(part_shape),
-        out_shape=jax.ShapeDtypeStruct(part_shape, F32),
-        scratch_shapes=[
-            rows_scratch,
-            cols_scratch,
-            pltpu.VMEM((cols, features), F32),
-            pltpu.VMEM((cols, block), BF16),
-        ],
-        compiler_params=params,
-        name="barycenter",
-    )(rho, v, k, p)
-    parts = over_z(parts.astype(F16)).astype(F32)
+        mean_kernel,
+        out_shape=jax.ShapeDtypeStruct((nz, own * (features // LANES) + 16, LANES), F32),
+        compiler_params=small,
+        name="means",
+    )(mine, theirs)
+    parts = lax.all_to_all(parts.astype(F16), "z", 0, 0, tiled=True).astype(F32)
 
     return pl.pallas_call(
         update_kernel,
         out_shape=jax.ShapeDtypeStruct((own, features), F32),
-        compiler_params=pltpu.CompilerParams(vmem_limit_bytes=32 * 1024 * 1024),
+        compiler_params=small,
         name="update",
     )(parts, generated, noise)
 

time: 219 us -> 183 us (0.84)
  blocking collectives: 140 us -> 95.3 us
  starting transfers between devices: 0.01 us -> 29.8 us
  waiting for transfers between devices: 28.5 us -> 14.5 us
  between operations: 13.5 us -> 0.14 us
  Pallas kernels: 27.5 us -> 35.9 us
  local copies, waits for them, and re-layouts: 8.67 us -> 5.25 us
    all_to_all x7 -> x6, blocking collectives: 140 us -> 95.3 us  [the longest x1 31.9 us: shards(): parts = lax.all_to_all(parts.astype(F16), 'z', 0, 0, tiled=True).astype(F32)]
    ppermute x0 -> x17, starting transfers between devices: none -> 29.8 us  [permuted(): return lax.ppermute(a, axes, pairs)]
    all_gather x1 -> x0, waiting for transfers between devices: 27.8 us -> none  [shards(): p = lax.all_gather(private, peers, axis=0, tiled=False)]
    ppermute x0 -> x17, waiting for transfers between devices: none -> 14.5 us  [permuted(): return lax.ppermute(a, axes, pairs)]
    pallas_call x1 -> x3, Pallas kernels: 8.54 us -> 13.1 us  [the longest x2 12.8 us: barycenter(): pl.pallas_call(functools.partial(barycenter_kernel, float(ng), other), gr...]
    unnamed x14 -> x8, local copies, waits for them, and re-layouts: 7.65 us -> 4.26 us
    pallas_call x1, Pallas kernels: 3.62 us -> 6.39 us  [shards(): pl.pallas_call(functools.partial(plan_kernel, math.log(np_)), grid=(steps...]
  transfers between devices with their start and end apart: 1 -> 17, of which waited for: 1 -> 9; matrix products, arithmetic and copies ran while one was open for 0% -> 1% of each run, Pallas kernels for 0% -> 3%
where the time goes in v2:
time: 183 us; the launch traced here: 182 us
  blocking collectives  95.3 us (52%)
  Pallas kernels  35.9 us (20%)
  starting transfers between devices  29.8 us (16%)
  waiting for transfers between devices  14.5 us (8%)
  local copies, waits for them, and re-layouts  5.25 us (3%)
    all_to_all x1, blocking collectives, shards(): parts = lax.all_to_all(parts.astype(F16), 'z', 0, 0, tiled=True).astype(F32)  31.9 us
    all_to_all x3, blocking collectives, over_rows(): return lax.all_to_all(a, ('x', 'y'), 0, 0, tiled=True)  31.7 us
    all_to_all x2, blocking collectives, over_columns(): return lax.all_to_all(a, ('z', 'core'), 0, 0, tiled=True)  31.7 us
    ppermute x17, starting transfers between devices, permuted(): return lax.ppermute(a, axes, pairs)  29.8 us
    ppermute x17, waiting for transfers between devices, permuted(): return lax.ppermute(a, axes, pairs)  14.5 us
    pallas_call x2, Pallas kernels, barycenter(): pl.pallas_call(functools.partial(barycenter_kernel, float(ng), other), gr...  12.8 us
    pallas_call x1, Pallas kernels, shards(): pl.pallas_call(functools.partial(score_kernel, scale), grid=(steps,), in_...  9.7 us
    pallas_call x1, Pallas kernels, shards(): pl.pallas_call(functools.partial(plan_kernel, math.log(np_)), grid=(steps...  6.39 us
  transfers between devices with their start and end apart: 17, of which 9 were waited for; matrix products, arithmetic and copies ran while one was open for 1% of the time, Pallas kernels for 3%

profile of v2, /device:TPU:1, one launch (start us, length us, event | category | flops | bytes accessed | tf_op | source)
XLA Modules:
  0.0 182.5 jit_solution(18375744058785754842)
XLA Ops:
  0.0 3.2 %collective-permute-start.10 = (bf16[64,1024]{1,0:T(8,128)(2,1)}, bf16[64,1024]{1,0:T(8,128)(2,1)S(1)}, u32[]{:S(2)}, u32[]{:S(2)}) collective-permute-start(bf16[64,1024]{1,0:T(8,128)(2,1)} %g_ref.1), channel_id=1, source_target_pairs={{0,1},{1,0},{2,3},{3,2},{4,5},{5,4},{6,7},{7,6},{8,9},{9,8},{10,11... | collective-permute-start | bytes 393224 | tf_op jit(solution)/shard_map/ppermute | solution.py:307
  3.2 1.0 constant_dynamic-slice_fusion
  4.2 0.1 collective-permute-start
  4.3 0.1 collective-permute-done.10
  4.4 1.0 maximum_select_fusion.2.refs_8_
  5.5 3.9 %collective-permute-start.11 = (bf16[2,64,1024]{2,1,0:T(8,128)(2,1)S(1)}, bf16[2,64,1024]{2,1,0:T(8,128)(2,1)S(1)}, u32[]{:S(2)}, u32[]{:S(2)}) collective-permute-start(bf16[2,64,1024]{2,1,0:T(8,128)(2,1)S(1)} %maximum_select_fusion.2.refs_8_), channel_id=1, source_target_pairs={{0,32},{1,225},{32,64},{33,1},{64,96},{65,33},{96,128},{97,65},{12... | collective-permute-start | bytes 786440 | tf_op jit(solution)/shard_map/ppermute | solution.py:307
  9.4 1.4 collective-permute-start.1
  10.8 1.9 %collective-permute-done.11 = bf16[2,64,1024]{2,1,0:T(8,128)(2,1)S(1)} collective-permute-done((bf16[2,64,1024]{2,1,0:T(8,128)(2,1)S(1)}, bf16[2,64,1024]{2,1,0:T(8,128)(2,1)S(1)}, u32[]{:S(2)}, u32[]{:S(2)}) %collective-permute-start.11) | collective-permute-done | bytes 262176 | tf_op jit(solution)/shard_map/ppermute | solution.py:307
  12.7 3.4 %collective-permute-start.12 = (bf16[2,64,1024]{2,1,0:T(8,128)(2,1)S(1)}, bf16[2,64,1024]{2,1,0:T(8,128)(2,1)S(1)}, u32[]{:S(2)}, u32[]{:S(2)}) collective-permute-start(bf16[2,64,1024]{2,1,0:T(8,128)(2,1)S(1)} %collective-permute-done.11), channel_id=1, source_target_pairs={{0,32},{1,225},{32,64},{33,1},{64,96},{65,33},{96,128},{97,65},{12... | collective-permute-start | bytes 786440 | tf_op jit(solution)/shard_map/ppermute | solution.py:307
  16.1 2.7 %collective-permute-start.2 = (bf16[2,512,128]{2,1,0:T(8,128)(2,1)S(1)}, bf16[2,512,128]{2,1,0:T(8,128)(2,1)S(1)}, u32[]{:S(2)}, u32[]{:S(2)}) collective-permute-start(bf16[2,512,128]{2,1,0:T(8,128)(2,1)S(1)} %maximum_select_fusion.1), channel_id=1, source_target_pairs={{0,24},{1,7},{2,26},{3,1},{4,28},{5,3},{6,30},{7,5},{8,0},{9,15},{... | collective-permute-start | bytes 786440 | tf_op jit(solution)/shard_map/ppermute | solution.py:307
  18.9 0.5 collective-permute-done.12
  19.4 3.1 %collective-permute-start.13 = (bf16[2,64,1024]{2,1,0:T(8,128)(2,1)S(1)}, bf16[2,64,1024]{2,1,0:T(8,128)(2,1)S(1)}, u32[]{:S(2)}, u32[]{:S(2)}) collective-permute-start(bf16[2,64,1024]{2,1,0:T(8,128)(2,1)S(1)} %collective-permute-done.12), channel_id=1, source_target_pairs={{0,32},{1,225},{32,64},{33,1},{64,96},{65,33},{96,128},{97,65},{12... | collective-permute-start | bytes 786440 | tf_op jit(solution)/shard_map/ppermute | solution.py:307
  22.6 1.0 collective-permute-start.4
  23.6 1.7 collective-permute-done.3
  25.3 2.3 %collective-permute-start.7 = (bf16[2,2,512,128]{3,2,1,0:T(8,128)(2,1)S(1)}, bf16[2,2,512,128]{3,2,1,0:T(8,128)(2,1)S(1)}, u32[]{:S(2)}, u32[]{:S(2)}) collective-permute-start(bf16[2,2,512,128]{3,2,1,0:T(8,128)(2,1)S(1)} %pad_maximum_fusion.2.refs_1_), channel_id=1, source_target_pairs={{0,6},{1,25},{2,0},{3,27},{4,2},{5,29},{6,4},{7,31},{8,14},{9,1},{... | collective-permute-start | bytes 1572872 | tf_op jit(solution)/shard_map/ppermute | solution.py:307
  27.6 0.5 collective-permute-start.5
  28.1 0.1 pad_maximum_fusion.refs_10_
  28.2 1.5 collective-permute-start.15
  29.7 1.2 collective-permute-start.6
  31.0 1.2 collective-permute-done.4.refs_2_
  32.1 0.1 collective-permute-start.8
  32.2 1.6 collective-permute-done.7.refs_5_
  33.7 3.4 %collective-permute-start.9 = (bf16[2,2,512,128]{3,2,1,0:T(8,128)(2,1)S(1)}, bf16[2,2,512,128]{3,2,1,0:T(8,128)(2,1)S(1)}, u32[]{:S(2)}, u32[]{:S(2)}) collective-permute-start(bf16[2,2,512,128]{3,2,1,0:T(8,128)(2,1)S(1)} %collective-permute-done.7.refs_5_), channel_id=1, source_target_pairs={{0,6},{1,25},{2,0},{3,27},{4,2},{5,29},{6,4},{7,31},{8,14},{9,1},{... | collective-permute-start | bytes 1572872 | tf_op jit(solution)/shard_map/ppermute | solution.py:307
  37.1 2.2 %collective-permute-done.5.refs_3_ = bf16[2,2,512,128]{3,2,1,0:T(8,128)(2,1)S(1)} collective-permute-done((bf16[2,2,512,128]{3,2,1,0:T(8,128)(2,1)S(1)}, bf16[2,2,512,128]{3,2,1,0:T(8,128)(2,1)S(1)}, u32[]{:S(2)}, u32[]{:S(2)}) %collective-permute-start.5) | collective-permute-done | bytes 524320 | tf_op jit(solution)/shard_map/ppermute | solution.py:307
  39.3 0.3 collective-permute-start.14
  39.7 5.2 %collective-permute-done.14.refs_9_ = bf16[2,64,1024]{2,1,0:T(8,128)(2,1)S(1)} collective-permute-done((bf16[2,64,1024]{2,1,0:T(8,128)(2,1)S(1)}, bf16[2,64,1024]{2,1,0:T(8,128)(2,1)S(1)}, u32[]{:S(2)}, u32[]{:S(2)}) %collective-permute-start.14) | collective-permute-done | bytes 262176 | tf_op jit(solution)/shard_map/ppermute | solution.py:307
  44.9 0.1 collective-permute-done.9.refs_7_
  45.0 9.7 %scores.1 = (bf16[4,8,512,128]{3,2,1,0:T(8,128)(2,1)S(1)}, f32[16,1024,128]{2,1,0:T(8,128)}, f32[16,16,128]{2,1,0:T(8,128)S(1)}) custom-call(bf16[2,2,512,128]{3,2,1,0:T(8,128)(2,1)S(1)} %pad_maximum_fusion.1.refs_0_, bf16[2,2,512,128]{3,2,1,0:T(8,128)(2,1)S(1)} %pad_maximum_fusion.2.refs_1_, bf16[2,2,512,128]{3,2,1,0:T(8,128)(2,1)S(1)} %collective-permute-done.4.refs_2_, ...), custom_call_target="tpu_custom_call" | custom-call | tf_op jit(solution)/shard_map/scores/pallas_call | solution.py:387
  54.7 12.0 %all_to_all.30.l_ref = f32[16,16,128]{2,1,0:T(8,128)S(1)} all-to-all(f32[16,16,128]{2,1,0:T(8,128)S(1)} %get-tuple-element.14), channel_id=1, replica_groups=mesh['z'=8,'x'=4,'y'=4,'core'=2] {'x','y'}, dimensions={0} | all-to-all | bytes 262144 | tf_op jit(solution)/shard_map/all_to_all | solution.py:381
  66.7 3.4 %copy-done.1 = f32[16,1024,128]{2,1,0:T(8,128)S(1)} copy-done((f32[16,1024,128]{2,1,0:T(8,128)S(1)}, f32[16,1024,128]{2,1,0:T(8,128)}, u32[]{:S(2)}) %copy-start.1) | copy-done | bytes 8388632
  70.1 3.0 %first_columns.1 = (f32[16,128]{1,0:T(8,128)S(1)}, f32[16,8,128]{2,1,0:T(8,128)S(1)}) custom-call(f32[16,16,128]{2,1,0:T(8,128)S(1)} %all_to_all.30.l_ref, f32[16,1024,128]{2,1,0:T(8,128)S(1)} %copy-done.1), custom_call_target="tpu_custom_call" | custom-call | tf_op jit(solution)/shard_map/first_columns/pallas_call | solution.py:399
  73.1 19.9 %all_to_all.31.lc_ref = f32[16,8,128]{2,1,0:T(8,128)S(1)} all-to-all(f32[16,8,128]{2,1,0:T(8,128)S(1)} %get-tuple-element.16), channel_id=1, replica_groups=mesh['z'=8,'x'=4,'y'=4,'core'=2] {'z','core'}, dimensions={0} | all-to-all | bytes 131072 | tf_op jit(solution)/shard_map/all_to_all | solution.py:384
  93.0 6.4 %plan.1 = (f32[16,1024,128]{2,1,0:T(8,128)S(1)}, f32[16,16,128]{2,1,0:T(8,128)S(1)}) custom-call(f32[16,8,128]{2,1,0:T(8,128)S(1)} %all_to_all.31.lc_ref, f32[16,128]{1,0:T(8,128)S(1)} %get-tuple-element.17.r_ref, f32[16,1024,128]{2,1,0:T(8,128)} %get-tuple-element.15.t_ref), custom_call_target="tpu_custom_call" | custom-call | tf_op jit(solution)/shard_map/plan/pallas_call | solution.py:411
  99.4 9.9 %all_to_all.32.rho_ref = f32[16,16,128]{2,1,0:T(8,128)S(1)} all-to-all(f32[16,16,128]{2,1,0:T(8,128)S(1)} %get-tuple-element.18), channel_id=1, replica_groups=mesh['z'=8,'x'=4,'y'=4,'core'=2] {'x','y'}, dimensions={0} | all-to-all | bytes 262144 | tf_op jit(solution)/shard_map/all_to_all | solution.py:381
  109.2 1.3 column_sums.1
  110.5 11.8 %all_to_all.33.sums_ref = f32[16,8,128]{2,1,0:T(8,128)S(1)} all-to-all(f32[16,8,128]{2,1,0:T(8,128)S(1)} %column_sums.1), channel_id=1, replica_groups=mesh['z'=8,'x'=4,'y'=4,'core'=2] {'z','core'}, dimensions={0} | all-to-all | bytes 131072 | tf_op jit(solution)/shard_map/all_to_all | solution.py:384
  122.3 1.4 row_sums.1
  123.8 9.9 %all_to_all.34.rho_ref = f32[16,16,128]{2,1,0:T(8,128)S(1)} all-to-all(f32[16,16,128]{2,1,0:T(8,128)S(1)} %get-tuple-element.20), channel_id=1, replica_groups=mesh['z'=8,'x'=4,'y'=4,'core'=2] {'x','y'}, dimensions={0} | all-to-all | bytes 262144 | tf_op jit(solution)/shard_map/all_to_all | solution.py:381
  133.6 6.4 %barycenter_other.1 = f32[520,1024]{1,0:T(8,128)S(1)} custom-call(f32[16,16,128]{2,1,0:T(8,128)S(1)} %all_to_all.34.rho_ref, f32[1024,128]{1,0:T(8,128)S(1)} %get-tuple-element.21.v_ref, f32[16,1024,128]{2,1,0:T(8,128)} %copy-done, bf16[4,8,512,128]{3,2,1,0:T(8,128)(2,1)S(1)} %get-tuple-element.22.p_ref), custom_call_target="tpu_custom_call" | custom-call | flops 2147483648 | bytes 16777216 | tf_op jit(solution)/shard_map/barycenter_other/pallas_call | solution.py:449
  140.0 1.6 collective-permute-start.16
  141.6 6.4 %barycenter_own.1.a_ref = f32[520,1024]{1,0:T(8,128)S(1)} custom-call(f32[16,16,128]{2,1,0:T(8,128)S(1)} %all_to_all.34.rho_ref, f32[1024,128]{1,0:T(8,128)S(1)} %get-tuple-element.21.v_ref, f32[16,1024,128]{2,1,0:T(8,128)} %copy-done, bf16[4,8,512,128]{3,2,1,0:T(8,128)(2,1)S(1)} %get-tuple-element.22.p_ref), custom_call_target="tpu_custom_call" | custom-call | flops 2147483648 | bytes 16777216 | tf_op jit(solution)/shard_map/barycenter_own/pallas_call | solution.py:449
  148.0 0.3 means.1
  148.4 0.1 convert_element_type.6
  148.5 31.9 %all_to_all.35 = f16[8,528,128]{2,1,0:T(8,128)(2,1)S(1)} all-to-all(f16[8,528,128]{2,1,0:T(8,128)(2,1)S(1)} %convert_element_type.6), channel_id=1, replica_groups=mesh['z'=8,'x'=4,'y'=4,'core'=2] {'z'}, dimensions={0} | all-to-all | bytes 2162688 | tf_op jit(solution)/shard_map/all_to_all | solution.py:476
  180.5 0.1 convert_element_type.7.parts_ref
  180.6 0.8 copy-done.2
  181.4 0.1 copy-done.3
  181.5 1.0 update.1
  (18 shorter events, 0.2 us)
Async XLA Ops:
  0.0 4.4 %collective-permute-start.10 = (bf16[64,1024]{1,0:T(8,128)(2,1)}, bf16[64,1024]{1,0:T(8,128)(2,1)S(1)}, u32[]{:S(2)}, u32[]{:S(2)}) collective-permute-start(bf16[64,1024]{1,0:T(8,128)(2,1)} %g_ref.1), channel_id=1, source_target_pairs={{0,1},{1,0},{2,3},{3,2},{4,5},{5,4},{6,7},{7,6},{8,9},{9,8},{10,11... | collective-permute-start | bytes 393224 | tf_op jit(solution)/shard_map/ppermute | solution.py:307
  4.2 5.1 %collective-permute-start = (bf16[512,128]{1,0:T(8,128)(2,1)S(1)}, bf16[512,128]{1,0:T(8,128)(2,1)S(1)}, u32[]{:S(2)}, u32[]{:S(2)}) collective-permute-start(bf16[512,128]{1,0:T(8,128)(2,1)S(1)} %get-tuple-element.24), channel_id=1, source_target_pairs={{0,1},{1,0},{2,3},{3,2},{4,5},{5,4},{6,7},{7,6},{8,9},{9,8},{10,11... | collective-permute-start | bytes 393224 | tf_op jit(solution)/shard_map/ppermute | solution.py:307
  5.5 7.2 %collective-permute-start.11 = (bf16[2,64,1024]{2,1,0:T(8,128)(2,1)S(1)}, bf16[2,64,1024]{2,1,0:T(8,128)(2,1)S(1)}, u32[]{:S(2)}, u32[]{:S(2)}) collective-permute-start(bf16[2,64,1024]{2,1,0:T(8,128)(2,1)S(1)} %maximum_select_fusion.2.refs_8_), channel_id=1, source_target_pairs={{0,32},{1,225},{32,64},{33,1},{64,96},{65,33},{96,128},{97,65},{12... | collective-permute-start | bytes 786440 | tf_op jit(solution)/shard_map/ppermute | solution.py:307
  9.4 9.4 %collective-permute-start.1 = (bf16[2,512,128]{2,1,0:T(8,128)(2,1)S(1)}, bf16[2,512,128]{2,1,0:T(8,128)(2,1)S(1)}, u32[]{:S(2)}, u32[]{:S(2)}) collective-permute-start(bf16[2,512,128]{2,1,0:T(8,128)(2,1)S(1)} %maximum_select_fusion.1), channel_id=1, source_target_pairs={{0,8},{1,3},{2,10},{3,5},{4,12},{5,7},{6,14},{7,1},{8,16},{9,11},{... | collective-permute-start | bytes 786440 | tf_op jit(solution)/shard_map/ppermute | solution.py:307
  12.7 6.7 %collective-permute-start.12 = (bf16[2,64,1024]{2,1,0:T(8,128)(2,1)S(1)}, bf16[2,64,1024]{2,1,0:T(8,128)(2,1)S(1)}, u32[]{:S(2)}, u32[]{:S(2)}) collective-permute-start(bf16[2,64,1024]{2,1,0:T(8,128)(2,1)S(1)} %collective-permute-done.11), channel_id=1, source_target_pairs={{0,32},{1,225},{32,64},{33,1},{64,96},{65,33},{96,128},{97,65},{12... | collective-permute-start | bytes 786440 | tf_op jit(solution)/shard_map/ppermute | solution.py:307
  16.1 7.5 %collective-permute-start.2 = (bf16[2,512,128]{2,1,0:T(8,128)(2,1)S(1)}, bf16[2,512,128]{2,1,0:T(8,128)(2,1)S(1)}, u32[]{:S(2)}, u32[]{:S(2)}) collective-permute-start(bf16[2,512,128]{2,1,0:T(8,128)(2,1)S(1)} %maximum_select_fusion.1), channel_id=1, source_target_pairs={{0,24},{1,7},{2,26},{3,1},{4,28},{5,3},{6,30},{7,5},{8,0},{9,15},{... | collective-permute-start | bytes 786440 | tf_op jit(solution)/shard_map/ppermute | solution.py:307
  18.8 6.4 %collective-permute-start.3 = (bf16[2,512,128]{2,1,0:T(8,128)(2,1)S(1)}, bf16[2,512,128]{2,1,0:T(8,128)(2,1)S(1)}, u32[]{:S(2)}, u32[]{:S(2)}) collective-permute-start(bf16[2,512,128]{2,1,0:T(8,128)(2,1)S(1)} %collective-permute-done.1), channel_id=1, source_target_pairs={{0,8},{1,3},{2,10},{3,5},{4,12},{5,7},{6,14},{7,1},{8,16},{9,11},{... | collective-permute-start | bytes 786440 | tf_op jit(solution)/shard_map/ppermute | solution.py:307
  19.4 8.7 %collective-permute-start.13 = (bf16[2,64,1024]{2,1,0:T(8,128)(2,1)S(1)}, bf16[2,64,1024]{2,1,0:T(8,128)(2,1)S(1)}, u32[]{:S(2)}, u32[]{:S(2)}) collective-permute-start(bf16[2,64,1024]{2,1,0:T(8,128)(2,1)S(1)} %collective-permute-done.12), channel_id=1, source_target_pairs={{0,32},{1,225},{32,64},{33,1},{64,96},{65,33},{96,128},{97,65},{12... | collective-permute-start | bytes 786440 | tf_op jit(solution)/shard_map/ppermute | solution.py:307
  22.6 9.5 %collective-permute-start.4 = (bf16[2,2,512,128]{3,2,1,0:T(8,128)(2,1)S(1)}, bf16[2,2,512,128]{3,2,1,0:T(8,128)(2,1)S(1)}, u32[]{:S(2)}, u32[]{:S(2)}) collective-permute-start(bf16[2,2,512,128]{3,2,1,0:T(8,128)(2,1)S(1)} %pad_maximum_fusion.1.refs_0_), channel_id=1, source_target_pairs={{0,2},{1,9},{2,4},{3,11},{4,6},{5,13},{6,0},{7,15},{8,10},{9,17},{... | collective-permute-start | bytes 1572872 | tf_op jit(solution)/shard_map/ppermute | solution.py:307
  25.3 8.4 %collective-permute-start.7 = (bf16[2,2,512,128]{3,2,1,0:T(8,128)(2,1)S(1)}, bf16[2,2,512,128]{3,2,1,0:T(8,128)(2,1)S(1)}, u32[]{:S(2)}, u32[]{:S(2)}) collective-permute-start(bf16[2,2,512,128]{3,2,1,0:T(8,128)(2,1)S(1)} %pad_maximum_fusion.2.refs_1_), channel_id=1, source_target_pairs={{0,6},{1,25},{2,0},{3,27},{4,2},{5,29},{6,4},{7,31},{8,14},{9,1},{... | collective-permute-start | bytes 1572872 | tf_op jit(solution)/shard_map/ppermute | solution.py:307
  27.6 11.8 %collective-permute-start.5 = (bf16[2,2,512,128]{3,2,1,0:T(8,128)(2,1)S(1)}, bf16[2,2,512,128]{3,2,1,0:T(8,128)(2,1)S(1)}, u32[]{:S(2)}, u32[]{:S(2)}) collective-permute-start(bf16[2,2,512,128]{3,2,1,0:T(8,128)(2,1)S(1)} %pad_maximum_fusion.1.refs_0_), channel_id=1, source_target_pairs={{0,6},{1,25},{2,0},{3,27},{4,2},{5,29},{6,4},{7,31},{8,14},{9,1},{... | collective-permute-start | bytes 1572872 | tf_op jit(solution)/shard_map/ppermute | solution.py:307
  28.2 16.7 %collective-permute-start.15 = (bf16[3,2,64,1024]{3,2,1,0:T(8,128)(2,1)S(1)}, bf16[3,2,64,1024]{3,2,1,0:T(8,128)(2,1)S(1)}, u32[]{:S(2)}, u32[]{:S(2)}) collective-permute-start(bf16[3,2,64,1024]{3,2,1,0:T(8,128)(2,1)S(1)} %pad_maximum_fusion.refs_10_), channel_id=1, source_target_pairs={{0,1},{1,0},{2,3},{3,2},{4,5},{5,4},{6,7},{7,6},{8,9},{9,8},{10,11... | collective-permute-start | bytes 2359304 | tf_op jit(solution)/shard_map/ppermute | solution.py:307
  29.7 9.9 %collective-permute-start.6 = (bf16[2,2,512,128]{3,2,1,0:T(8,128)(2,1)S(1)}, bf16[2,2,512,128]{3,2,1,0:T(8,128)(2,1)S(1)}, u32[]{:S(2)}, u32[]{:S(2)}) collective-permute-start(bf16[2,2,512,128]{3,2,1,0:T(8,128)(2,1)S(1)} %pad_maximum_fusion.2.refs_1_), channel_id=1, source_target_pairs={{0,2},{1,9},{2,4},{3,11},{4,6},{5,13},{6,0},{7,15},{8,10},{9,17},{... | collective-permute-start | bytes 1572872 | tf_op jit(solution)/shard_map/ppermute | solution.py:307
  32.1 12.8 %collective-permute-start.8 = (bf16[2,2,512,128]{3,2,1,0:T(8,128)(2,1)S(1)}, bf16[2,2,512,128]{3,2,1,0:T(8,128)(2,1)S(1)}, u32[]{:S(2)}, u32[]{:S(2)}) collective-permute-start(bf16[2,2,512,128]{3,2,1,0:T(8,128)(2,1)S(1)} %collective-permute-done.4.refs_2_), channel_id=1, source_target_pairs={{0,2},{1,9},{2,4},{3,11},{4,6},{5,13},{6,0},{7,15},{8,10},{9,17},{... | collective-permute-start | bytes 1572872 | tf_op jit(solution)/shard_map/ppermute | solution.py:307
  33.7 11.2 %collective-permute-start.9 = (bf16[2,2,512,128]{3,2,1,0:T(8,128)(2,1)S(1)}, bf16[2,2,512,128]{3,2,1,0:T(8,128)(2,1)S(1)}, u32[]{:S(2)}, u32[]{:S(2)}) collective-permute-start(bf16[2,2,512,128]{3,2,1,0:T(8,128)(2,1)S(1)} %collective-permute-done.7.refs_5_), channel_id=1, source_target_pairs={{0,6},{1,25},{2,0},{3,27},{4,2},{5,29},{6,4},{7,31},{8,14},{9,1},{... | collective-permute-start | bytes 1572872 | tf_op jit(solution)/shard_map/ppermute | solution.py:307
  39.3 5.5 %collective-permute-start.14 = (bf16[2,64,1024]{2,1,0:T(8,128)(2,1)S(1)}, bf16[2,64,1024]{2,1,0:T(8,128)(2,1)S(1)}, u32[]{:S(2)}, u32[]{:S(2)}) collective-permute-start(bf16[2,64,1024]{2,1,0:T(8,128)(2,1)S(1)} %collective-permute-done.13), channel_id=1, source_target_pairs={{0,32},{1,225},{32,64},{33,1},{64,96},{65,33},{96,128},{97,65},{12... | collective-permute-start | bytes 786440 | tf_op jit(solution)/shard_map/ppermute | solution.py:307
  66.7 3.4 %copy-start.1 = (f32[16,1024,128]{2,1,0:T(8,128)S(1)}, f32[16,1024,128]{2,1,0:T(8,128)}, u32[]{:S(2)}) copy-start(f32[16,1024,128]{2,1,0:T(8,128)} %get-tuple-element.15.t_ref) | copy-start | bytes 25165828
  99.4 23.0 %copy-start = (f32[16,1024,128]{2,1,0:T(8,128)}, f32[16,1024,128]{2,1,0:T(8,128)S(1)}, u32[]{:S(2)}) copy-start(f32[16,1024,128]{2,1,0:T(8,128)S(1)} %get-tuple-element.19.k_ref) | copy-start | bytes 25165828
  140.0 8.0 %collective-permute-start.16 = (f32[520,1024]{1,0:T(8,128)S(1)}, f32[520,1024]{1,0:T(8,128)S(1)}, u32[]{:S(2)}, u32[]{:S(2)}) collective-permute-start(f32[520,1024]{1,0:T(8,128)S(1)} %barycenter_other.1), channel_id=1, source_target_pairs={{0,1},{1,0},{2,3},{3,2},{4,5},{5,4},{6,7},{7,6},{8,9},{9,8},{10,11... | collective-permute-start | bytes 6389768 | tf_op jit(solution)/shard_map/ppermute | solution.py:307
  180.5 0.9 copy-start.2
  180.5 1.0 copy-start.3

commit v3 on v0

v3 whole, which is shorter than its diff:
```python
import functools
import itertools
import math

import jax
import jax.numpy as jnp
from jax import lax
from jax.experimental import pallas as pl
from jax.experimental.pallas import tpu as pltpu
from jax.sharding import Mesh
from jax.sharding import PartitionSpec as P


EPS = 0.02
F32 = jnp.float32
BF16 = jnp.bfloat16
F16 = jnp.float16
LANES = 128
SUB = 64


def to_rows(column):
    flat = jnp.transpose(column)[0:1, :]
    return jnp.concatenate(
        [flat[:, q * LANES:(q + 1) * LANES] for q in range(column.shape[0] // LANES)], axis=0
    )


def sum_to_rows(lanes):
    flat = jnp.sum(jnp.transpose(lanes), axis=0, keepdims=True)
    return jnp.concatenate(
        [flat[:, q * LANES:(q + 1) * LANES] for q in range(lanes.shape[0] // LANES)], axis=0
    )


def to_columns(rows, out_ref):
    for q in range(rows.shape[0]):
        out_ref[q * LANES:(q + 1) * LANES, :] = jnp.transpose(
            jnp.broadcast_to(rows[q:q + 1, :], (LANES, LANES))
        )


def logsumexp0(x):
    top = jnp.max(x, axis=0)
    return top + jnp.log2(jnp.sum(jnp.exp2(x - top[None]), axis=0))


def chunks(n):
    return [pl.ds(c, SUB) for c in range(0, n, SUB)]


def score_kernel(scale, *refs):
    blocks, (own_ref, far_ref, near_ref, swapped_ref) = refs[:8], refs[8:12]
    p_ref, t_ref, l_ref, g_ref, c0_ref, rows_ref = refs[12:]
    nx, slices, rows, width = p_ref.shape
    ny = slices // 2
    nz = 8
    x, y, z, core = (lax.axis_index(a) for a in ("x", "y", "z", "core"))

    first = ((0, -1), (1, -2))
    for ref, pair, second in zip(blocks, (0, 1, 0, 0, 1, 1, 0, 1), (0, 0, -1, 1, -1, 1, -2, 2)):
        for n in range(2):
            a, b = first[pair][n], second
            px = lax.rem(x + jnp.where(core == 0, a, b) + nx, nx)
            py = lax.rem(y + jnp.where(core == 0, b, a) + ny, ny)
            for f in range(2):
                p_ref[px, 2 * py + f] = ref[n, f]

    own = g_ref.shape[0] // (2 * nz)

    def put(ref, at, k):
        pz = lax.rem(z + k + nz, nz)
        for c in range(2):
            g = ref[at + (c,)]
            to = pl.ds(pl.multiple_of((c * nz + pz) * own, own), own)
            g_ref[to, :] = g
            g = g.astype(F32)
            sq = jnp.sum(g * g, axis=1, keepdims=True)
            c0_ref[to, :] = jnp.broadcast_to(sq * (-0.5 * scale), (own, LANES))

    sign = jnp.where(core == 0, -1, 1)
    put(own_ref, (), 0)
    put(far_ref, (), 4)
    for k in range(1, 4):
        put(near_ref, (k - 1,), sign * k)
        put(swapped_ref, (k - 1,), -sign * k)

    cols = g_ref.shape[0]
    wide = 2 * LANES

    def scores(n):
        at = pl.ds(n % (rows // wide) * wide, wide)
        p = jnp.concatenate([p_ref[n // (rows // wide), f, at, :] for f in range(slices)], axis=1)
        return lax.dot_general(g_ref[...], p, (((1,), (1,)), ((), ())), preferred_element_type=F32)

    def reduce(n):
        for k in (2 * n, 2 * n + 1):
            top = jnp.full((8, LANES), -jnp.inf, F32)
            for at in chunks(cols):
                top = jnp.maximum(top, jnp.max(t_ref[k, at, :].reshape(SUB // 8, 8, LANES), axis=0))
            top = jnp.max(top, axis=0, keepdims=True)
            total = jnp.zeros((8, LANES), F32)
            for at in chunks(cols):
                e = jnp.exp2(t_ref[k, at, :] - top)
                total = total + jnp.sum(e.reshape(SUB // 8, 8, LANES), axis=0)
            rows_ref[k:k + 1, :] = top + jnp.log2(jnp.sum(total, axis=0, keepdims=True))

    steps = nx * rows // wide
    for n in range(steps):
        cross = scores(n)
        if n:
            reduce(n - 1)
        for k in range(2):
            t_ref[2 * n + k] = cross[:, k * LANES:(k + 1) * LANES] * scale + c0_ref[...]
    reduce(steps - 1)
    l_ref[...] = jnp.broadcast_to(rows_ref[...][None], l_ref.shape)


def first_column_kernel(log_ng, l_ref, t_ref, g_ref, n_ref, r_ref, k_ref, lc_ref, base_ref, m_ref, s_ref):
    tiles, cols, _ = t_ref.shape
    base_ref[...] = g_ref[...].astype(F32) + n_ref[...]
    r_ref[...] = log_ng - logsumexp0(l_ref[...])
    r = [r_ref[n:n + 1, :] for n in range(tiles)]

    @pl.loop(0, cols, step=SUB)
    def _(c):
        at = pl.ds(pl.multiple_of(c, SUB), SUB)
        total = jnp.zeros((SUB, LANES), F32)
        for n in range(tiles):
            e = jnp.exp2(t_ref[n, at, :] + r[n])
            k_ref[n, at, :] = e
            total = total + e
        s_ref[at, :] = total

    sums = sum_to_rows(s_ref[...])
    lc_ref[...] = jnp.broadcast_to(jnp.log2(sums)[None], lc_ref.shape)

    @pl.when(jnp.min(sums) < 1e-30)
    def _():
        @pl.loop(0, cols, step=SUB)
        def _(c):
            at = pl.ds(pl.multiple_of(c, SUB), SUB)
            top = t_ref[0, at, :] + r[0]
            for n in range(1, tiles):
                top = jnp.maximum(top, t_ref[n, at, :] + r[n])
            total = jnp.zeros((SUB, LANES), F32)
            for n in range(tiles):
                total = total + jnp.exp2(t_ref[n, at, :] + r[n] - top)
            m_ref[at, :] = top
            s_ref[at, :] = total

        m = m_ref[...]
        top = jnp.max(m, axis=1, keepdims=True)
        total = jnp.sum(s_ref[...] * jnp.exp2(m - top), axis=1, keepdims=True)
        lc = to_rows(jnp.broadcast_to(top + jnp.log2(total), m.shape))
        lc_ref[...] = jnp.broadcast_to(lc[None], lc_ref.shape)


def scaled_row_sums(k_ref, v_ref, rho_ref):
    tiles, cols, _ = k_ref.shape

    def body(i, totals):
        at = pl.ds(pl.multiple_of(i * SUB, SUB), SUB)
        v = v_ref[at, :]
        return tuple(
            totals[n] + jnp.sum((k_ref[n, at, :] * v).reshape(SUB // 8, 8, LANES), axis=0)
            for n in range(tiles)
        )

    totals = lax.fori_loop(
        0, cols // SUB, body, tuple(jnp.zeros((8, LANES), F32) for _ in range(tiles))
    )
    rho = jnp.concatenate([jnp.sum(total, axis=0, keepdims=True) for total in totals], axis=0)
    rho_ref[...] = jnp.broadcast_to(rho[None], rho_ref.shape)


def second_row_kernel(log_np, lc_ref, r_ref, t_ref, old_ref, k_ref, rho_ref, v_ref):
    del old_ref
    tiles, cols, _ = t_ref.shape
    c1 = log_np - logsumexp0(lc_ref[...])
    fits = jnp.max(c1) <= 66.0
    to_columns(jnp.where(fits, jnp.exp2(c1), c1), v_ref)

    @pl.when(jnp.logical_not(fits))
    def _():
        @pl.loop(0, cols, step=SUB)
        def _(c):
            at = pl.ds(pl.multiple_of(c, SUB), SUB)
            for n in range(tiles):
                k_ref[n, at, :] = jnp.exp2(t_ref[n, at, :] + r_ref[n:n + 1, :] + v_ref[at, :])
            v_ref[at, :] = jnp.ones((SUB, LANES), F32)

    scaled_row_sums(k_ref, v_ref, rho_ref)


def column_sum_kernel(ng, rho_ref, k_ref, sums_ref, acc_ref):
    tiles, cols, _ = k_ref.shape
    scaled = ng / jnp.sum(rho_ref[...], axis=0)
    u = [scaled[n:n + 1, :] for n in range(tiles)]

    @pl.loop(0, cols, step=SUB)
    def _(c):
        at = pl.ds(pl.multiple_of(c, SUB), SUB)
        total = k_ref[0, at, :] * u[0]
        for n in range(1, tiles):
            total = total + k_ref[n, at, :] * u[n]
        acc_ref[at, :] = total

    sums_ref[...] = jnp.broadcast_to(sum_to_rows(acc_ref[...])[None], sums_ref.shape)


def row_sum_kernel(np_, sums_ref, k_ref, v_ref, rho_ref):
    to_columns(np_ / jnp.sum(sums_ref[...], axis=0), v_ref)
    scaled_row_sums(k_ref, v_ref, rho_ref)


def barycenter_kernel(ng, other, rho_ref, v_ref, k_ref, p_ref, out_ref, mass_ref, w_ref):
    tiles = k_ref.shape[0]
    cols = mass_ref.shape[0]
    core = lax.axis_index("core")
    begin = (1 - core if other else core) * cols
    scaled = ng / jnp.sum(rho_ref[...], axis=0)
    u = [scaled[n:n + 1, :] for n in range(tiles)]

    @pl.loop(0, cols, step=SUB)
    def _(c):
        at = pl.ds(pl.multiple_of(c, SUB), SUB)
        source = pl.ds(pl.multiple_of(begin + c, SUB), SUB)
        v = v_ref[source, :]
        total = jnp.zeros((SUB, LANES), F32)
        for n in range(tiles):
            w = k_ref[n, source, :] * u[n] * v
            total = total + w
            w_ref[at, n * LANES:(n + 1) * LANES] = w.astype(BF16)
        mass_ref[at, :] = total

    p = jnp.concatenate(
        [
            jnp.concatenate([p_ref[x, f] for f in range(p_ref.shape[1])], axis=1)
            for x in range(p_ref.shape[0])
        ],
        axis=0,
    )
    out_ref[0:cols, :] = jnp.dot(w_ref[...], p, preferred_element_type=F32)
    mass = jnp.sum(jnp.transpose(mass_ref[...]), axis=0, keepdims=True)
    out_ref[cols:, 0:cols] = jnp.broadcast_to(mass, (out_ref.shape[0] - cols, cols))


def mean_kernel(a_ref, b_ref, out_ref):
    owners = out_ref.shape[0]
    features = a_ref.shape[1]
    blocks = features // LANES
    rows = (out_ref.shape[1] - 16) // blocks
    cols = owners * rows
    mass = jnp.maximum(a_ref[cols:cols + 1, 0:cols] + b_ref[cols:cols + 1, 0:cols], 1e-30)
    log_mass = jnp.log2(mass)
    inverse = jnp.transpose(jnp.broadcast_to(1.0 / mass, (LANES, cols)))
    for z in range(owners):
        at = slice(z * rows, (z + 1) * rows)
        for q in range(blocks):
            lanes = slice(q * LANES, (q + 1) * LANES)
            out_ref[z, q * rows:(q + 1) * rows, :] = (a_ref[at, lanes] + b_ref[at, lanes]) * inverse[at, :]
        part = jnp.concatenate([log_mass[:, at]] * (LANES // rows), axis=1)
        high = jnp.round(part * 16.0) * 0.0625
        low = part - high
        out_ref[z, blocks * rows:, :] = jnp.concatenate([high] * 8 + [low] * 8, axis=0)


def update_kernel(parts_ref, base_ref, out_ref):
    sources = parts_ref.shape[0]
    rows = base_ref.shape[0]
    blocks = base_ref.shape[1] // LANES
    at = blocks * rows
    logs = jnp.concatenate(
        [parts_ref[d, at:at + 1, :] + parts_ref[d, at + 8:at + 9, :] for d in range(sources)], axis=0
    )
    weights = jnp.exp2(logs - jnp.max(logs, axis=0, keepdims=True))
    weights = weights / jnp.sum(weights, axis=0, keepdims=True)
    columns = [
        jnp.transpose(jnp.broadcast_to(weights[d:d + 1, :], (LANES, LANES)))[0:rows, :]
        for d in range(sources)
    ]
    for q in range(blocks):
        lanes = slice(q * LANES, (q + 1) * LANES)
        total = parts_ref[0, q * rows:(q + 1) * rows, :] * columns[0]
        for d in range(1, sources):
            total = total + parts_ref[d, q * rows:(q + 1) * rows, :] * columns[d]
        out_ref[:, lanes] = base_ref[:, lanes] - total


def permuted(a, axes, moved):
    sizes = [lax.axis_size(n) for n in axes]
    flat = lambda at: functools.reduce(lambda f, cn: f * cn[1] + cn[0] % cn[1], zip(at, sizes), 0)
    pairs = [(flat(at), flat(moved(*at))) for at in itertools.product(*map(range, sizes))]
    return lax.ppermute(a, axes, pairs)


def along(first, d, a):
    return permuted(
        a,
        ("x", "y", "core"),
        lambda x, y, c: (x + d, y, c) if (c == 0) == first else (x, y + d, c),
    )


def swap(a):
    return permuted(a, ("core",), lambda c: (1 - c,))


def gather_private(private):
    core = lax.axis_index("core")
    rows, width = private.shape
    halves = private.reshape(2, rows // 2, width)
    mine = lax.dynamic_index_in_dim(halves, core, 0, False)
    got = swap(lax.dynamic_index_in_dim(halves, 1 - core, 0, False))
    a0 = jnp.where(core == 0, jnp.stack([mine, got]), jnp.stack([got, mine]))
    a1 = along(True, 1, a0)
    a2 = along(True, -1, a0)
    a3 = along(True, 1, a1)
    s, t = jnp.stack([a0, a1]), jnp.stack([a2, a3])
    s1, s2 = along(False, 1, s), along(False, -1, s)
    t1, t2 = along(False, 1, t), along(False, -1, t)
    return s, t, s1, s2, t1, t2, along(False, 1, s1), along(False, -1, t2)


def gather_generated(generated):
    core = lax.axis_index("core")
    got = swap(generated)
    pair = jnp.where(core == 0, jnp.stack([generated, got]), jnp.stack([got, generated]))
    chain = [pair]
    for _ in range(4):
        chain.append(
            permuted(chain[-1], ("z", "core"), lambda z, c: (z + (1 if c == 0 else -1), c))
        )
    near = jnp.stack(chain[1:4])
    return pair, chain[4], near, swap(near)


def shards(private, generated, noise):
    rows_per, width = private.shape
    own, features = generated.shape
    nz, nx, ny = lax.axis_size("z"), lax.axis_size("x"), lax.axis_size("y")
    cols = own * nz * 2
    rows = rows_per // 2 * nx
    np_ = rows * nz * 2
    ng = cols * nx * ny
    scale = 2.0 / (features * EPS) * math.log2(math.e)
    row_tiles = rows // LANES
    col_tiles = cols // LANES
    half = cols // 2

    def call(body, name, out_shape, scratch, *args, limit=24, cost=None, aliases=None):
        return pl.pallas_call(
            body,
            out_shape=out_shape,
            scratch_shapes=scratch,
            compiler_params=pltpu.CompilerParams(vmem_limit_bytes=limit << 20),
            cost_estimate=cost,
            input_output_aliases=aliases or {},
            name=name,
        )(*args)

    def f32(*shape):
        return jax.ShapeDtypeStruct(shape, F32)

    row_out = f32(nx * ny, row_tiles, LANES)
    col_out = f32(nz * 2, col_tiles, LANES)
    k_shape = f32(row_tiles, cols, LANES)
    v_shape = f32(cols, LANES)
    lanes = pltpu.VMEM((cols, LANES), F32)

    def over_rows(a):
        return lax.all_to_all(a, ("x", "y"), 0, 0, tiled=True)

    def over_columns(a):
        return lax.all_to_all(a, ("z", "core"), 0, 0, tiled=True)

    gathered = gather_private(private) + gather_generated(generated)
    p, t, lr = call(
        functools.partial(score_kernel, scale),
        "scores",
        [jax.ShapeDtypeStruct((nx, 2 * ny, rows_per // 2, width), BF16), k_shape, row_out],
        [pltpu.VMEM((cols, features), BF16), lanes, pltpu.VMEM((row_tiles, LANES), F32)],
        *gathered,
    )
    r, k, lc, base = call(
        functools.partial(first_column_kernel, math.log2(ng)),
        "first_columns",
        [f32(row_tiles, LANES), k_shape, col_out, f32(own, features)],
        [lanes, lanes],
        over_rows(lr), t, generated, noise,
    )
    k, rho, v = call(
        functools.partial(second_row_kernel, math.log2(np_)),
        "second_rows",
        [k_shape, row_out, v_shape],
        [],
        over_columns(lc), r, t, k,
        aliases={3: 0},
    )
    sums = call(
        functools.partial(column_sum_kernel, float(ng)),
        "column_sums",
        col_out,
        [lanes],
        over_rows(rho), k,
    )
    v, rho = call(
        functools.partial(row_sum_kernel, float(np_)),
        "row_sums",
        [v_shape, row_out],
        [],
        over_columns(sums), k,
    )
    rho = over_rows(rho)

    def barycenter(other):
        return call(
            functools.partial(barycenter_kernel, float(ng), other),
            "barycenter_other" if other else "barycenter_own",
            f32(half + 8, features),
            [pltpu.VMEM((half, LANES), F32), pltpu.VMEM((half, rows), BF16)],
            rho, v, k, p,
            cost=pl.CostEstimate(
                flops=2 * half * rows * features, bytes_accessed=16 << 20, transcendentals=0
            ),
        )

    theirs = swap(barycenter(True))
    mine = barycenter(False)
    parts = call(
        mean_kernel, "means", f32(nz, own * (features // LANES) + 16, LANES), [], mine, theirs
    )
    parts = lax.all_to_all(parts.astype(F16), "z", 0, 0, tiled=True).astype(F32)
    return call(update_kernel, "update", f32(own, features), [], parts, base)


def solution(mesh):
    fine = Mesh(mesh.devices.reshape(8, 4, 4, 2), ("z", "x", "y", "core"))
    in_specs = (
        P(("z", "x"), ("y", "core")),
        P(("y", "core", "z", "x"), None),
        P(("y", "core", "z", "x"), None),
    )
    out_specs = P(("y", "core", "z", "x"), None)
    return jax.shard_map(shards, mesh=fine, in_specs=in_specs, out_specs=out_specs, check_vma=False)
```

time: 941 us -> 166 us (0.18)
  blocking collectives: 481 us -> 95.2 us
  waiting for transfers between devices: 365 us -> 15.3 us
  other arithmetic: 55.5 us -> 1.54 us
  starting transfers between devices: 0.08 us -> 29.8 us
  matrix products: 22.7 us -> 0 us
  Pallas kernels: 0 us -> 22.7 us
  between operations: 13.3 us -> 0.12 us
    pmax x6 -> x0, blocking collectives: 273 us -> none  [the longest x3 178 us: target_softmax_normalizer(): highest = lax.pmax(maximal_element, 'dp')]
    reduce_scatter x1 -> x0, waiting for transfers between devices: 248 us -> none  [shards(): lax.psum_scatter(partial_sums, 'dp', scatter_dimension=0, tiled=True)]
    psum x6 -> x0, blocking collectives: 209 us -> none  [the longest x3 171 us: target_softmax_normalizer(): lax.psum(accumulated_exponential * jnp.exp(maximal_element - highest), 'dp')]
    all_gather x2 -> x0, waiting for transfers between devices: 115 us -> none  [the longest x1 80.3 us: shards(): block_rows = lax.all_gather(generated, 'dp', axis=0, tiled=True)]
    all_to_all x0 -> x6, blocking collectives: none -> 95.2 us  [the longest x1 31.9 us: shards(): parts = lax.all_to_all(parts.astype(F16), 'z', 0, 0, tiled=True).astype(F32)]
    reduce_sum x8 -> x0, other arithmetic: 32.2 us -> none  [the longest x3 13.5 us: target_softmax_normalizer(): jnp.sum(jnp.exp(kernel_grid - maximal_element[None, :]), axis=0)]
    ppermute x0 -> x17, starting transfers between devices: none -> 29.8 us  [permuted(): return lax.ppermute(a, axes, pairs)]
    dot_general x2 -> x0, matrix products: 22.7 us -> none  [the longest x1 11.7 us: shards(): jnp.einsum('ij,id->jd', coupling_plan, private_rows, preferred_element_ty...]
  transfers between devices with their start and end apart: 3 -> 17, of which waited for: 3 -> 10; matrix products, arithmetic and copies ran while one was open for 0% -> 1% of each run, Pallas kernels for 0% -> 2%
where the time goes in v3:
time: 166 us
  blocking collectives  95.2 us (57%)
  starting transfers between devices  29.8 us (18%)
  Pallas kernels  22.7 us (14%)
  waiting for transfers between devices  15.3 us (9%)
    all_to_all x1, blocking collectives, shards(): parts = lax.all_to_all(parts.astype(F16), 'z', 0, 0, tiled=True).astype(F32)  31.9 us
    all_to_all x3, blocking collectives, over_rows(): return lax.all_to_all(a, ('x', 'y'), 0, 0, tiled=True)  31.7 us
    all_to_all x2, blocking collectives, over_columns(): return lax.all_to_all(a, ('z', 'core'), 0, 0, tiled=True)  31.6 us
    ppermute x17, starting transfers between devices, permuted(): return lax.ppermute(a, axes, pairs)  29.8 us
    pallas_call x9, Pallas kernels, call(): pl.pallas_call(body, out_shape=out_shape, scratch_shapes=scratch, compile...  22.7 us
    ppermute x17, waiting for transfers between devices, permuted(): return lax.ppermute(a, axes, pairs)  15.3 us
  transfers between devices with their start and end apart: 17, of which 10 were waited for; matrix products, arithmetic and copies ran while one was open for 1% of the time, Pallas kernels for 2%

profile of v3, /device:TPU:1, one launch (start us, length us, event | category | flops | bytes accessed | tf_op | source)
XLA Modules:
  0.0 165.7 jit_solution(2665159993531147295)
XLA Ops:
  0.0 3.2 %collective-permute-start.10 = (bf16[64,1024]{1,0:T(8,128)(2,1)}, bf16[64,1024]{1,0:T(8,128)(2,1)S(1)}, u32[]{:S(2)}, u32[]{:S(2)}) collective-permute-start(bf16[64,1024]{1,0:T(8,128)(2,1)} %g_ref.1), channel_id=1, source_target_pairs={{0,1},{1,0},{2,3},{3,2},{4,5},{5,4},{6,7},{7,6},{8,9},{9,8},{10,11... | collective-permute-start | bytes 393224 | tf_op jit(solution)/shard_map/ppermute | solution.py:295
  3.2 1.0 constant_dynamic-slice_fusion
  4.2 0.1 collective-permute-start
  4.3 0.1 collective-permute-done.10
  4.4 1.0 maximum_select_fusion.2.refs_8_
  5.5 3.9 %collective-permute-start.11 = (bf16[2,64,1024]{2,1,0:T(8,128)(2,1)S(1)}, bf16[2,64,1024]{2,1,0:T(8,128)(2,1)S(1)}, u32[]{:S(2)}, u32[]{:S(2)}) collective-permute-start(bf16[2,64,1024]{2,1,0:T(8,128)(2,1)S(1)} %maximum_select_fusion.2.refs_8_), channel_id=1, source_target_pairs={{0,32},{1,225},{32,64},{33,1},{64,96},{65,33},{96,128},{97,65},{12... | collective-permute-start | bytes 786440 | tf_op jit(solution)/shard_map/ppermute | solution.py:295
  9.4 1.4 collective-permute-start.1
  10.8 1.9 %collective-permute-done.11 = bf16[2,64,1024]{2,1,0:T(8,128)(2,1)S(1)} collective-permute-done((bf16[2,64,1024]{2,1,0:T(8,128)(2,1)S(1)}, bf16[2,64,1024]{2,1,0:T(8,128)(2,1)S(1)}, u32[]{:S(2)}, u32[]{:S(2)}) %collective-permute-start.11) | collective-permute-done | bytes 262176 | tf_op jit(solution)/shard_map/ppermute | solution.py:295
  12.7 3.4 %collective-permute-start.12 = (bf16[2,64,1024]{2,1,0:T(8,128)(2,1)S(1)}, bf16[2,64,1024]{2,1,0:T(8,128)(2,1)S(1)}, u32[]{:S(2)}, u32[]{:S(2)}) collective-permute-start(bf16[2,64,1024]{2,1,0:T(8,128)(2,1)S(1)} %collective-permute-done.11), channel_id=1, source_target_pairs={{0,32},{1,225},{32,64},{33,1},{64,96},{65,33},{96,128},{97,65},{12... | collective-permute-start | bytes 786440 | tf_op jit(solution)/shard_map/ppermute | solution.py:295
  16.1 2.7 %collective-permute-start.2 = (bf16[2,512,128]{2,1,0:T(8,128)(2,1)S(1)}, bf16[2,512,128]{2,1,0:T(8,128)(2,1)S(1)}, u32[]{:S(2)}, u32[]{:S(2)}) collective-permute-start(bf16[2,512,128]{2,1,0:T(8,128)(2,1)S(1)} %maximum_select_fusion.1), channel_id=1, source_target_pairs={{0,24},{1,7},{2,26},{3,1},{4,28},{5,3},{6,30},{7,5},{8,0},{9,15},{... | collective-permute-start | bytes 786440 | tf_op jit(solution)/shard_map/ppermute | solution.py:295
  18.9 0.5 collective-permute-done.12
  19.4 3.1 %collective-permute-start.13 = (bf16[2,64,1024]{2,1,0:T(8,128)(2,1)S(1)}, bf16[2,64,1024]{2,1,0:T(8,128)(2,1)S(1)}, u32[]{:S(2)}, u32[]{:S(2)}) collective-permute-start(bf16[2,64,1024]{2,1,0:T(8,128)(2,1)S(1)} %collective-permute-done.12), channel_id=1, source_target_pairs={{0,32},{1,225},{32,64},{33,1},{64,96},{65,33},{96,128},{97,65},{12... | collective-permute-start | bytes 786440 | tf_op jit(solution)/shard_map/ppermute | solution.py:295
  22.5 0.1 pad_maximum_fusion.1.refs_0_
  22.6 1.0 collective-permute-start.4
  23.6 1.7 %collective-permute-done.3 = bf16[2,512,128]{2,1,0:T(8,128)(2,1)S(1)} collective-permute-done((bf16[2,512,128]{2,1,0:T(8,128)(2,1)S(1)}, bf16[2,512,128]{2,1,0:T(8,128)(2,1)S(1)}, u32[]{:S(2)}, u32[]{:S(2)}) %collective-permute-start.3) | collective-permute-done | bytes 262176 | tf_op jit(solution)/shard_map/ppermute | solution.py:295
  25.3 0.1 pad_maximum_fusion.2.refs_1_
  25.3 2.3 %collective-permute-start.7 = (bf16[2,2,512,128]{3,2,1,0:T(8,128)(2,1)S(1)}, bf16[2,2,512,128]{3,2,1,0:T(8,128)(2,1)S(1)}, u32[]{:S(2)}, u32[]{:S(2)}) collective-permute-start(bf16[2,2,512,128]{3,2,1,0:T(8,128)(2,1)S(1)} %pad_maximum_fusion.2.refs_1_), channel_id=1, source_target_pairs={{0,6},{1,25},{2,0},{3,27},{4,2},{5,29},{6,4},{7,31},{8,14},{9,1},{... | collective-permute-start | bytes 1572872 | tf_op jit(solution)/shard_map/ppermute | solution.py:295
  27.6 0.5 collective-permute-start.5
  28.1 0.1 pad_maximum_fusion.refs_10_
  28.3 1.5 collective-permute-start.15
  29.8 1.2 collective-permute-start.6
  31.0 1.1 collective-permute-done.4.refs_2_
  32.1 0.1 collective-permute-start.8
  32.2 1.5 collective-permute-done.7.refs_5_
  33.7 3.4 %collective-permute-start.9 = (bf16[2,2,512,128]{3,2,1,0:T(8,128)(2,1)S(1)}, bf16[2,2,512,128]{3,2,1,0:T(8,128)(2,1)S(1)}, u32[]{:S(2)}, u32[]{:S(2)}) collective-permute-start(bf16[2,2,512,128]{3,2,1,0:T(8,128)(2,1)S(1)} %collective-permute-done.7.refs_5_), channel_id=1, source_target_pairs={{0,6},{1,25},{2,0},{3,27},{4,2},{5,29},{6,4},{7,31},{8,14},{9,1},{... | collective-permute-start | bytes 1572872 | tf_op jit(solution)/shard_map/ppermute | solution.py:295
  37.1 2.2 %collective-permute-done.5.refs_3_ = bf16[2,2,512,128]{3,2,1,0:T(8,128)(2,1)S(1)} collective-permute-done((bf16[2,2,512,128]{3,2,1,0:T(8,128)(2,1)S(1)}, bf16[2,2,512,128]{3,2,1,0:T(8,128)(2,1)S(1)}, u32[]{:S(2)}, u32[]{:S(2)}) %collective-permute-start.5) | collective-permute-done | bytes 524320 | tf_op jit(solution)/shard_map/ppermute | solution.py:295
  39.3 0.3 collective-permute-start.14
  39.7 5.2 %collective-permute-done.14.refs_9_ = bf16[2,64,1024]{2,1,0:T(8,128)(2,1)S(1)} collective-permute-done((bf16[2,64,1024]{2,1,0:T(8,128)(2,1)S(1)}, bf16[2,64,1024]{2,1,0:T(8,128)(2,1)S(1)}, u32[]{:S(2)}, u32[]{:S(2)}) %collective-permute-start.14) | collective-permute-done | bytes 262176 | tf_op jit(solution)/shard_map/ppermute | solution.py:295
  44.9 0.1 collective-permute-done.8.refs_6_
  45.0 6.3 %scores.1 = (bf16[4,8,512,128]{3,2,1,0:T(8,128)(2,1)S(1)}, f32[16,1024,128]{2,1,0:T(8,128)S(1)}, f32[16,16,128]{2,1,0:T(8,128)S(1)}) custom-call(bf16[2,2,512,128]{3,2,1,0:T(8,128)(2,1)S(1)} %pad_maximum_fusion.1.refs_0_, bf16[2,2,512,128]{3,2,1,0:T(8,128)(2,1)S(1)} %pad_maximum_fusion.2.refs_1_, ...), custom_call_target="tpu_custom_call" | custom-call | tf_op jit(solution)/shard_map/scores/pallas_call | solution.py:353
  51.3 12.0 %all_to_all.30.l_ref = f32[16,16,128]{2,1,0:T(8,128)S(1)} all-to-all(f32[16,16,128]{2,1,0:T(8,128)S(1)} %get-tuple-element.16), channel_id=1, replica_groups=mesh['z'=8,'x'=4,'y'=4,'core'=2] {'x','y'}, dimensions={0} | all-to-all | bytes 262144 | tf_op jit(solution)/shard_map/all_to_all | solution.py:373
  63.3 4.1 %first_columns.1 = (f32[16,128]{1,0:T(8,128)S(1)}, f32[16,1024,128]{2,1,0:T(8,128)S(1)}, f32[16,8,128]{2,1,0:T(8,128)S(1)}, f32[64,1024]{1,0:T(8,128)S(1)}) custom-call(f32[16,16,128]{2,1,0:T(8,128)S(1)} %all_to_all.30.l_ref, f32[16,1024,128]{2,1,0:T(8,128)S(1)} %get-tuple-element.17.t_ref, bf16[64,1024]{1,0:T(8,128)(2,1)S(1)} %copy-done, ...), custom_call_target="tpu_custom_call" | custom-call | tf_op jit(solution)/shard_map/first_columns/pallas_call | solution.py:353
  67.3 19.8 %all_to_all.31.lc_ref = f32[16,8,128]{2,1,0:T(8,128)S(1)} all-to-all(f32[16,8,128]{2,1,0:T(8,128)S(1)} %get-tuple-element.18), channel_id=1, replica_groups=mesh['z'=8,'x'=4,'y'=4,'core'=2] {'z','core'}, dimensions={0} | all-to-all | bytes 131072 | tf_op jit(solution)/shard_map/all_to_all | solution.py:376
  87.2 3.1 %second_rows.1 = (f32[16,1024,128]{2,1,0:T(8,128)S(1)}, f32[16,16,128]{2,1,0:T(8,128)S(1)}, f32[1024,128]{1,0:T(8,128)}) custom-call(f32[16,8,128]{2,1,0:T(8,128)S(1)} %all_to_all.31.lc_ref, f32[16,128]{1,0:T(8,128)S(1)} %get-tuple-element.19.r_ref, f32[16,1024,128]{2,1,0:T(8,128)S(1)} %get-tuple-element.17.t_ref, ...), custom_call_target="tpu_custom_call", output_to_operand_aliasing={{0}: (3, {})} | custom-call | tf_op jit(solution)/shard_map/second_rows/pallas_call | solution.py:353
  90.3 9.8 %all_to_all.32.rho_ref = f32[16,16,128]{2,1,0:T(8,128)S(1)} all-to-all(f32[16,16,128]{2,1,0:T(8,128)S(1)} %get-tuple-element.21), channel_id=1, replica_groups=mesh['z'=8,'x'=4,'y'=4,'core'=2] {'x','y'}, dimensions={0} | all-to-all | bytes 262144 | tf_op jit(solution)/shard_map/all_to_all | solution.py:373
  100.2 0.9 column_sums.1
  101.1 11.8 %all_to_all.33.sums_ref = f32[16,8,128]{2,1,0:T(8,128)S(1)} all-to-all(f32[16,8,128]{2,1,0:T(8,128)S(1)} %column_sums.1), channel_id=1, replica_groups=mesh['z'=8,'x'=4,'y'=4,'core'=2] {'z','core'}, dimensions={0} | all-to-all | bytes 131072 | tf_op jit(solution)/shard_map/all_to_all | solution.py:376
  112.9 1.0 row_sums.1
  113.8 9.9 %all_to_all.34.rho_ref = f32[16,16,128]{2,1,0:T(8,128)S(1)} all-to-all(f32[16,16,128]{2,1,0:T(8,128)S(1)} %get-tuple-element.23), channel_id=1, replica_groups=mesh['z'=8,'x'=4,'y'=4,'core'=2] {'x','y'}, dimensions={0} | all-to-all | bytes 262144 | tf_op jit(solution)/shard_map/all_to_all | solution.py:373
  123.7 3.0 %barycenter_other.1 = f32[520,1024]{1,0:T(8,128)S(1)} custom-call(f32[16,16,128]{2,1,0:T(8,128)S(1)} %all_to_all.34.rho_ref, f32[1024,128]{1,0:T(8,128)S(1)} %get-tuple-element.24.v_ref, f32[16,1024,128]{2,1,0:T(8,128)S(1)} %get-tuple-element.22.k_ref, bf16[4,8,512,128]{3,2,1,0:T(8,128)(2,1)S(1)} %get-tuple-element.25.p_ref), custom_call_target="tpu_custom_call" | custom-call | flops 2147483648 | bytes 16777216 | tf_op jit(solution)/shard_map/barycenter_other/pallas_call | solution.py:353
  126.7 1.6 collective-permute-start.16
  128.3 3.0 %barycenter_own.1.a_ref = f32[520,1024]{1,0:T(8,128)S(1)} custom-call(f32[16,16,128]{2,1,0:T(8,128)S(1)} %all_to_all.34.rho_ref, f32[1024,128]{1,0:T(8,128)S(1)} %get-tuple-element.24.v_ref, f32[16,1024,128]{2,1,0:T(8,128)S(1)} %get-tuple-element.22.k_ref, bf16[4,8,512,128]{3,2,1,0:T(8,128)(2,1)S(1)} %get-tuple-element.25.p_ref), custom_call_target="tpu_custom_call" | custom-call | flops 2147483648 | bytes 16777216 | tf_op jit(solution)/shard_map/barycenter_own/pallas_call | solution.py:353
  131.3 0.8 collective-permute-done.16.b_ref
  132.2 0.3 means.1
  132.5 0.1 convert_element_type.6
  132.7 31.9 %all_to_all.35 = f16[8,528,128]{2,1,0:T(8,128)(2,1)S(1)} all-to-all(f16[8,528,128]{2,1,0:T(8,128)(2,1)S(1)} %convert_element_type.6), channel_id=1, replica_groups=mesh['z'=8,'x'=4,'y'=4,'core'=2] {'z'}, dimensions={0} | all-to-all | bytes 2162688 | tf_op jit(solution)/shard_map/all_to_all | solution.py:434
  164.6 0.1 convert_element_type.7.parts_ref
  164.7 1.0 update.1
  (14 shorter events, 0.1 us)
Async XLA Ops:
  0.0 4.4 %collective-permute-start.10 = (bf16[64,1024]{1,0:T(8,128)(2,1)}, bf16[64,1024]{1,0:T(8,128)(2,1)S(1)}, u32[]{:S(2)}, u32[]{:S(2)}) collective-permute-start(bf16[64,1024]{1,0:T(8,128)(2,1)} %g_ref.1), channel_id=1, source_target_pairs={{0,1},{1,0},{2,3},{3,2},{4,5},{5,4},{6,7},{7,6},{8,9},{9,8},{10,11... | collective-permute-start | bytes 393224 | tf_op jit(solution)/shard_map/ppermute | solution.py:295
  4.2 5.1 %collective-permute-start = (bf16[512,128]{1,0:T(8,128)(2,1)S(1)}, bf16[512,128]{1,0:T(8,128)(2,1)S(1)}, u32[]{:S(2)}, u32[]{:S(2)}) collective-permute-start(bf16[512,128]{1,0:T(8,128)(2,1)S(1)} %get-tuple-element.28), channel_id=1, source_target_pairs={{0,1},{1,0},{2,3},{3,2},{4,5},{5,4},{6,7},{7,6},{8,9},{9,8},{10,11... | collective-permute-start | bytes 393224 | tf_op jit(solution)/shard_map/ppermute | solution.py:295
  5.5 7.2 %collective-permute-start.11 = (bf16[2,64,1024]{2,1,0:T(8,128)(2,1)S(1)}, bf16[2,64,1024]{2,1,0:T(8,128)(2,1)S(1)}, u32[]{:S(2)}, u32[]{:S(2)}) collective-permute-start(bf16[2,64,1024]{2,1,0:T(8,128)(2,1)S(1)} %maximum_select_fusion.2.refs_8_), channel_id=1, source_target_pairs={{0,32},{1,225},{32,64},{33,1},{64,96},{65,33},{96,128},{97,65},{12... | collective-permute-start | bytes 786440 | tf_op jit(solution)/shard_map/ppermute | solution.py:295
  9.4 9.4 %collective-permute-start.1 = (bf16[2,512,128]{2,1,0:T(8,128)(2,1)S(1)}, bf16[2,512,128]{2,1,0:T(8,128)(2,1)S(1)}, u32[]{:S(2)}, u32[]{:S(2)}) collective-permute-start(bf16[2,512,128]{2,1,0:T(8,128)(2,1)S(1)} %maximum_select_fusion.1), channel_id=1, source_target_pairs={{0,8},{1,3},{2,10},{3,5},{4,12},{5,7},{6,14},{7,1},{8,16},{9,11},{... | collective-permute-start | bytes 786440 | tf_op jit(solution)/shard_map/ppermute | solution.py:295
  12.7 6.7 %collective-permute-start.12 = (bf16[2,64,1024]{2,1,0:T(8,128)(2,1)S(1)}, bf16[2,64,1024]{2,1,0:T(8,128)(2,1)S(1)}, u32[]{:S(2)}, u32[]{:S(2)}) collective-permute-start(bf16[2,64,1024]{2,1,0:T(8,128)(2,1)S(1)} %collective-permute-done.11), channel_id=1, source_target_pairs={{0,32},{1,225},{32,64},{33,1},{64,96},{65,33},{96,128},{97,65},{12... | collective-permute-start | bytes 786440 | tf_op jit(solution)/shard_map/ppermute | solution.py:295
  16.1 7.5 %collective-permute-start.2 = (bf16[2,512,128]{2,1,0:T(8,128)(2,1)S(1)}, bf16[2,512,128]{2,1,0:T(8,128)(2,1)S(1)}, u32[]{:S(2)}, u32[]{:S(2)}) collective-permute-start(bf16[2,512,128]{2,1,0:T(8,128)(2,1)S(1)} %maximum_select_fusion.1), channel_id=1, source_target_pairs={{0,24},{1,7},{2,26},{3,1},{4,28},{5,3},{6,30},{7,5},{8,0},{9,15},{... | collective-permute-start | bytes 786440 | tf_op jit(solution)/shard_map/ppermute | solution.py:295
  18.8 6.4 %collective-permute-start.3 = (bf16[2,512,128]{2,1,0:T(8,128)(2,1)S(1)}, bf16[2,512,128]{2,1,0:T(8,128)(2,1)S(1)}, u32[]{:S(2)}, u32[]{:S(2)}) collective-permute-start(bf16[2,512,128]{2,1,0:T(8,128)(2,1)S(1)} %collective-permute-done.1), channel_id=1, source_target_pairs={{0,8},{1,3},{2,10},{3,5},{4,12},{5,7},{6,14},{7,1},{8,16},{9,11},{... | collective-permute-start | bytes 786440 | tf_op jit(solution)/shard_map/ppermute | solution.py:295
  19.4 8.7 %collective-permute-start.13 = (bf16[2,64,1024]{2,1,0:T(8,128)(2,1)S(1)}, bf16[2,64,1024]{2,1,0:T(8,128)(2,1)S(1)}, u32[]{:S(2)}, u32[]{:S(2)}) collective-permute-start(bf16[2,64,1024]{2,1,0:T(8,128)(2,1)S(1)} %collective-permute-done.12), channel_id=1, source_target_pairs={{0,32},{1,225},{32,64},{33,1},{64,96},{65,33},{96,128},{97,65},{12... | collective-permute-start | bytes 786440 | tf_op jit(solution)/shard_map/ppermute | solution.py:295
  22.6 9.5 %collective-permute-start.4 = (bf16[2,2,512,128]{3,2,1,0:T(8,128)(2,1)S(1)}, bf16[2,2,512,128]{3,2,1,0:T(8,128)(2,1)S(1)}, u32[]{:S(2)}, u32[]{:S(2)}) collective-permute-start(bf16[2,2,512,128]{3,2,1,0:T(8,128)(2,1)S(1)} %pad_maximum_fusion.1.refs_0_), channel_id=1, source_target_pairs={{0,2},{1,9},{2,4},{3,11},{4,6},{5,13},{6,0},{7,15},{8,10},{9,17},{... | collective-permute-start | bytes 1572872 | tf_op jit(solution)/shard_map/ppermute | solution.py:295
  25.3 8.4 %collective-permute-start.7 = (bf16[2,2,512,128]{3,2,1,0:T(8,128)(2,1)S(1)}, bf16[2,2,512,128]{3,2,1,0:T(8,128)(2,1)S(1)}, u32[]{:S(2)}, u32[]{:S(2)}) collective-permute-start(bf16[2,2,512,128]{3,2,1,0:T(8,128)(2,1)S(1)} %pad_maximum_fusion.2.refs_1_), channel_id=1, source_target_pairs={{0,6},{1,25},{2,0},{3,27},{4,2},{5,29},{6,4},{7,31},{8,14},{9,1},{... | collective-permute-start | bytes 1572872 | tf_op jit(solution)/shard_map/ppermute | solution.py:295
  27.6 11.8 %collective-permute-start.5 = (bf16[2,2,512,128]{3,2,1,0:T(8,128)(2,1)S(1)}, bf16[2,2,512,128]{3,2,1,0:T(8,128)(2,1)S(1)}, u32[]{:S(2)}, u32[]{:S(2)}) collective-permute-start(bf16[2,2,512,128]{3,2,1,0:T(8,128)(2,1)S(1)} %pad_maximum_fusion.1.refs_0_), channel_id=1, source_target_pairs={{0,6},{1,25},{2,0},{3,27},{4,2},{5,29},{6,4},{7,31},{8,14},{9,1},{... | collective-permute-start | bytes 1572872 | tf_op jit(solution)/shard_map/ppermute | solution.py:295
  28.2 35.0 %copy-start = (bf16[64,1024]{1,0:T(8,128)(2,1)S(1)}, bf16[64,1024]{1,0:T(8,128)(2,1)}, u32[]{:S(2)}) copy-start(bf16[64,1024]{1,0:T(8,128)(2,1)} %g_ref.1) | copy-start | bytes 393220
  28.2 35.0 %copy-start.1 = (f32[64,1024]{1,0:T(8,128)S(1)}, f32[64,1024]{1,0:T(8,128)}, u32[]{:S(2)}) copy-start(f32[64,1024]{1,0:T(8,128)} %n_ref.1) | copy-start | bytes 786436
  28.3 16.7 %collective-permute-start.15 = (bf16[3,2,64,1024]{3,2,1,0:T(8,128)(2,1)S(1)}, bf16[3,2,64,1024]{3,2,1,0:T(8,128)(2,1)S(1)}, u32[]{:S(2)}, u32[]{:S(2)}) collective-permute-start(bf16[3,2,64,1024]{3,2,1,0:T(8,128)(2,1)S(1)} %pad_maximum_fusion.refs_10_), channel_id=1, source_target_pairs={{0,1},{1,0},{2,3},{3,2},{4,5},{5,4},{6,7},{7,6},{8,9},{9,8},{10,11... | collective-permute-start | bytes 2359304 | tf_op jit(solution)/shard_map/ppermute | solution.py:295
  29.8 9.9 %collective-permute-start.6 = (bf16[2,2,512,128]{3,2,1,0:T(8,128)(2,1)S(1)}, bf16[2,2,512,128]{3,2,1,0:T(8,128)(2,1)S(1)}, u32[]{:S(2)}, u32[]{:S(2)}) collective-permute-start(bf16[2,2,512,128]{3,2,1,0:T(8,128)(2,1)S(1)} %pad_maximum_fusion.2.refs_1_), channel_id=1, source_target_pairs={{0,2},{1,9},{2,4},{3,11},{4,6},{5,13},{6,0},{7,15},{8,10},{9,17},{... | collective-permute-start | bytes 1572872 | tf_op jit(solution)/shard_map/ppermute | solution.py:295
  32.1 12.8 %collective-permute-start.8 = (bf16[2,2,512,128]{3,2,1,0:T(8,128)(2,1)S(1)}, bf16[2,2,512,128]{3,2,1,0:T(8,128)(2,1)S(1)}, u32[]{:S(2)}, u32[]{:S(2)}) collective-permute-start(bf16[2,2,512,128]{3,2,1,0:T(8,128)(2,1)S(1)} %collective-permute-done.4.refs_2_), channel_id=1, source_target_pairs={{0,2},{1,9},{2,4},{3,11},{4,6},{5,13},{6,0},{7,15},{8,10},{9,17},{... | collective-permute-start | bytes 1572872 | tf_op jit(solution)/shard_map/ppermute | solution.py:295
  33.7 11.2 %collective-permute-start.9 = (bf16[2,2,512,128]{3,2,1,0:T(8,128)(2,1)S(1)}, bf16[2,2,512,128]{3,2,1,0:T(8,128)(2,1)S(1)}, u32[]{:S(2)}, u32[]{:S(2)}) collective-permute-start(bf16[2,2,512,128]{3,2,1,0:T(8,128)(2,1)S(1)} %collective-permute-done.7.refs_5_), channel_id=1, source_target_pairs={{0,6},{1,25},{2,0},{3,27},{4,2},{5,29},{6,4},{7,31},{8,14},{9,1},{... | collective-permute-start | bytes 1572872 | tf_op jit(solution)/shard_map/ppermute | solution.py:295
  39.3 5.5 %collective-permute-start.14 = (bf16[2,64,1024]{2,1,0:T(8,128)(2,1)S(1)}, bf16[2,64,1024]{2,1,0:T(8,128)(2,1)S(1)}, u32[]{:S(2)}, u32[]{:S(2)}) collective-permute-start(bf16[2,64,1024]{2,1,0:T(8,128)(2,1)S(1)} %collective-permute-done.13), channel_id=1, source_target_pairs={{0,32},{1,225},{32,64},{33,1},{64,96},{65,33},{96,128},{97,65},{12... | collective-permute-start | bytes 786440 | tf_op jit(solution)/shard_map/ppermute | solution.py:295
  126.7 5.5 %collective-permute-start.16 = (f32[520,1024]{1,0:T(8,128)S(1)}, f32[520,1024]{1,0:T(8,128)S(1)}, u32[]{:S(2)}, u32[]{:S(2)}) collective-permute-start(f32[520,1024]{1,0:T(8,128)S(1)} %barycenter_other.1), channel_id=1, source_target_pairs={{0,1},{1,0},{2,3},{3,2},{4,5},{5,4},{6,7},{7,6},{8,9},{9,8},{10,11... | collective-permute-start | bytes 6389768 | tf_op jit(solution)/shard_map/ppermute | solution.py:295

commit v4 on v3

--- a/solution.py
+++ b/solution.py
@@ -49,49 +49,65 @@
     return [pl.ds(c, SUB) for c in range(0, n, SUB)]
 
 
-def score_kernel(scale, *refs):
-    blocks, (own_ref, far_ref, near_ref, swapped_ref) = refs[:8], refs[8:12]
-    p_ref, t_ref, l_ref, g_ref, c0_ref, rows_ref = refs[12:]
-    nx, slices, rows, width = p_ref.shape
-    ny = slices // 2
+WIDE = 2 * LANES
+
+
+def place(ref, pair, second, p_ref):
+    nx, ny = p_ref.shape[0], p_ref.shape[1] // 2
+    x, y, core = (lax.axis_index(a) for a in ("x", "y", "core"))
+    for n, first in enumerate(((0, -1), (1, -2))[pair]):
+        px = lax.rem(x + jnp.where(core == 0, first, second) + nx, nx)
+        py = lax.rem(y + jnp.where(core == 0, second, first) + ny, ny)
+        for f in range(2):
+            p_ref[px, 2 * py + f] = ref[n, f]
+
+
+def score_columns(scale, blocks, p_ref, t_ref, g_ref, c0_ref, after):
+    nx, slices, rows, _ = p_ref.shape
     nz = 8
-    x, y, z, core = (lax.axis_index(a) for a in ("x", "y", "z", "core"))
-
-    first = ((0, -1), (1, -2))
-    for ref, pair, second in zip(blocks, (0, 1, 0, 0, 1, 1, 0, 1), (0, 0, -1, 1, -1, 1, -2, 2)):
-        for n in range(2):
-            a, b = first[pair][n], second
-            px = lax.rem(x + jnp.where(core == 0, a, b) + nx, nx)
-            py = lax.rem(y + jnp.where(core == 0, b, a) + ny, ny)
-            for f in range(2):
-                p_ref[px, 2 * py + f] = ref[n, f]
-
-    own = g_ref.shape[0] // (2 * nz)
-
-    def put(ref, at, k):
+    z = lax.axis_index("z")
+    own = blocks[0][0].shape[1]
+    starts = []
+    for block, k in blocks:
         pz = lax.rem(z + k + nz, nz)
         for c in range(2):
-            g = ref[at + (c,)]
-            to = pl.ds(pl.multiple_of((c * nz + pz) * own, own), own)
-            g_ref[to, :] = g
+            at = pl.ds(len(starts) * own, own)
+            g = block[c]
+            g_ref[at, :] = g
             g = g.astype(F32)
             sq = jnp.sum(g * g, axis=1, keepdims=True)
-            c0_ref[to, :] = jnp.broadcast_to(sq * (-0.5 * scale), (own, LANES))
-
-    sign = jnp.where(core == 0, -1, 1)
-    put(own_ref, (), 0)
-    put(far_ref, (), 4)
-    for k in range(1, 4):
-        put(near_ref, (k - 1,), sign * k)
-        put(swapped_ref, (k - 1,), -sign * k)
-
-    cols = g_ref.shape[0]
-    wide = 2 * LANES
-
-    def scores(n):
-        at = pl.ds(n % (rows // wide) * wide, wide)
-        p = jnp.concatenate([p_ref[n // (rows // wide), f, at, :] for f in range(slices)], axis=1)
-        return lax.dot_general(g_ref[...], p, (((1,), (1,)), ((), ())), preferred_element_type=F32)
+            c0_ref[at, :] = jnp.broadcast_to(sq * (-0.5 * scale), (own, LANES))
+            starts.append(pl.multiple_of((c * nz + pz) * own, own))
+
+    per = rows // WIDE
+    for n in range(nx * per):
+        at = pl.ds(n % per * WIDE, WIDE)
+        p = jnp.concatenate([p_ref[n // per, f, at, :] for f in range(slices)], axis=1)
+        cross = lax.dot_general(g_ref[...], p, (((1,), (1,)), ((), ())), preferred_element_type=F32)
+        if n:
+            after(n - 1)
+        for k in range(2):
+            for m, start in enumerate(starts):
+                part = slice(m * own, (m + 1) * own)
+                t_ref[2 * n + k, pl.ds(start, own), :] = (
+                    cross[part, k * LANES:(k + 1) * LANES] * scale + c0_ref[part, :]
+                )
+    after(nx * per - 1)
+
+
+def early_score_kernel(scale, *refs):
+    blocks, (own_ref, far_ref, near_ref) = refs[:8], refs[8:11]
+    p_ref, t_ref, g_ref, c0_ref = refs[11:]
+    for ref, pair, second in zip(blocks, (0, 1, 0, 0, 1, 1, 0, 1), (0, 0, -1, 1, -1, 1, -2, 2)):
+        place(ref, pair, second, p_ref)
+    sign = jnp.where(lax.axis_index("core") == 0, -1, 1)
+    columns = [(own_ref, 0), (far_ref, 4)] + [(near_ref.at[k - 1], sign * k) for k in (1, 2, 3)]
+    score_columns(scale, columns, p_ref, t_ref, g_ref, c0_ref, lambda n: None)
+
+
+def late_score_kernel(scale, swapped_ref, p_ref, old_ref, t_ref, l_ref, g_ref, c0_ref, rows_ref):
+    del old_ref
+    cols = t_ref.shape[1]
 
     def reduce(n):
         for k in (2 * n, 2 * n + 1):
@@ -105,14 +121,9 @@
                 total = total + jnp.sum(e.reshape(SUB // 8, 8, LANES), axis=0)
             rows_ref[k:k + 1, :] = top + jnp.log2(jnp.sum(total, axis=0, keepdims=True))
 
-    steps = nx * rows // wide
-    for n in range(steps):
-        cross = scores(n)
-        if n:
-            reduce(n - 1)
-        for k in range(2):
-            t_ref[2 * n + k] = cross[:, k * LANES:(k + 1) * LANES] * scale + c0_ref[...]
-    reduce(steps - 1)
+    sign = jnp.where(lax.axis_index("core") == 0, 1, -1)
+    columns = [(swapped_ref.at[k - 1], sign * k) for k in (1, 2, 3)]
+    score_columns(scale, columns, p_ref, t_ref, g_ref, c0_ref, reduce)
     l_ref[...] = jnp.broadcast_to(rows_ref[...][None], l_ref.shape)
 
 
@@ -307,33 +318,26 @@
     return permuted(a, ("core",), lambda c: (1 - c,))
 
 
-def gather_private(private):
+def gather(private, generated):
     core = lax.axis_index("core")
     rows, width = private.shape
-    halves = private.reshape(2, rows // 2, width)
-    mine = lax.dynamic_index_in_dim(halves, core, 0, False)
-    got = swap(lax.dynamic_index_in_dim(halves, 1 - core, 0, False))
-    a0 = jnp.where(core == 0, jnp.stack([mine, got]), jnp.stack([got, mine]))
-    a1 = along(True, 1, a0)
-    a2 = along(True, -1, a0)
-    a3 = along(True, 1, a1)
+    mine, got = private.reshape(2, rows // 2, width), swap(private).reshape(2, rows // 2, width)
+    a0 = jnp.where(core == 0, jnp.stack([mine[0], got[0]]), jnp.stack([got[1], mine[1]]))
+    a1, a2 = along(True, 1, a0), along(True, -1, a0)
+    a3 = along(True, 2, a0)
     s, t = jnp.stack([a0, a1]), jnp.stack([a2, a3])
-    s1, s2 = along(False, 1, s), along(False, -1, s)
-    t1, t2 = along(False, 1, t), along(False, -1, t)
-    return s, t, s1, s2, t1, t2, along(False, 1, s1), along(False, -1, t2)
-
-
-def gather_generated(generated):
-    core = lax.axis_index("core")
+    s1, t2, t1, s2 = along(False, 1, s), along(False, -1, t), along(False, 1, t), along(False, -1, s)
+    h1, h2 = along(False, 1, s1), along(False, -1, t2)
+
     got = swap(generated)
-    pair = jnp.where(core == 0, jnp.stack([generated, got]), jnp.stack([got, generated]))
-    chain = [pair]
+    chain = [jnp.where(core == 0, jnp.stack([generated, got]), jnp.stack([got, generated]))]
     for _ in range(4):
         chain.append(
             permuted(chain[-1], ("z", "core"), lambda z, c: (z + (1 if c == 0 else -1), c))
         )
     near = jnp.stack(chain[1:4])
-    return pair, chain[4], near, swap(near)
+    near, far, t1, s2, h1, h2 = lax.optimization_barrier((near, chain[4], t1, s2, h1, h2))
+    return (s, t, s1, s2, t1, t2, h1, h2), (chain[0], far, near), swap(near)
 
 
 def shards(private, generated, noise):
@@ -375,13 +379,29 @@
     def over_columns(a):
         return lax.all_to_all(a, ("z", "core"), 0, 0, tiled=True)
 
-    gathered = gather_private(private) + gather_generated(generated)
-    p, t, lr = call(
-        functools.partial(score_kernel, scale),
-        "scores",
-        [jax.ShapeDtypeStruct((nx, 2 * ny, rows_per // 2, width), BF16), k_shape, row_out],
-        [pltpu.VMEM((cols, features), BF16), lanes, pltpu.VMEM((row_tiles, LANES), F32)],
-        *gathered,
+    blocks, columns, swapped = gather(private, generated)
+    others = cols * 3 // 8
+    p, t = call(
+        functools.partial(early_score_kernel, scale),
+        "early_scores",
+        [jax.ShapeDtypeStruct((nx, 2 * ny, rows_per // 2, width), BF16), k_shape],
+        [pltpu.VMEM((cols - others, features), BF16), pltpu.VMEM((cols - others, LANES), F32)],
+        *blocks, *columns,
+        cost=pl.CostEstimate(
+            flops=2 * (cols - others) * rows * features, bytes_accessed=24 << 20, transcendentals=0
+        ),
+    )
+    t, lr = call(
+        functools.partial(late_score_kernel, scale),
+        "late_scores",
+        [k_shape, row_out],
+        [
+            pltpu.VMEM((others, features), BF16),
+            pltpu.VMEM((others, LANES), F32),
+            pltpu.VMEM((row_tiles, LANES), F32),
+        ],
+        swapped, p, t,
+        aliases={2: 0},
     )
     r, k, lc, base = call(
         functools.partial(first_column_kernel, math.log2(ng)),

time: 166 us -> 161 us (0.970)
  waiting for transfers between devices: 15.3 us -> 8.33 us
  starting transfers between devices: 29.8 us -> 35.9 us
  blocking collectives: 95.2 us -> 91.1 us
    ppermute x17, waiting for transfers between devices: 15.3 us -> 8.33 us  [permuted(): return lax.ppermute(a, axes, pairs)]
    ppermute x17, starting transfers between devices: 29.8 us -> 35.9 us  [permuted(): return lax.ppermute(a, axes, pairs)]
    all_to_all x2, blocking collectives: 31.6 us -> 26.8 us  [over_columns(): return lax.all_to_all(a, ('z', 'core'), 0, 0, tiled=True)]
    pallas_call x9 -> x10, Pallas kernels: 22.7 us -> 23.7 us  [call(): pl.pallas_call(body, out_shape=out_shape, scratch_shapes=scratch, compile...]
  transfers between devices with their start and end apart: 17 -> 17, of which waited for: 10 -> 8; matrix products, arithmetic and copies ran while one was open for 1% -> 1% of each run, Pallas kernels for 2% -> 4%
where the time goes in v4:
time: 161 us
  blocking collectives  91.1 us (57%)
  starting transfers between devices  35.9 us (22%)
  Pallas kernels  23.7 us (15%)
  waiting for transfers between devices  8.33 us (5%)
    ppermute x17, starting transfers between devices, permuted(): return lax.ppermute(a, axes, pairs)  35.9 us
    all_to_all x3, blocking collectives, over_rows(): return lax.all_to_all(a, ('x', 'y'), 0, 0, tiled=True)  32.4 us
    all_to_all x1, blocking collectives, shards(): parts = lax.all_to_all(parts.astype(F16), 'z', 0, 0, tiled=True).astype(F32)  31.9 us
    all_to_all x2, blocking collectives, over_columns(): return lax.all_to_all(a, ('z', 'core'), 0, 0, tiled=True)  26.8 us
    pallas_call x10, Pallas kernels, call(): pl.pallas_call(body, out_shape=out_shape, scratch_shapes=scratch, compile...  23.7 us
    ppermute x17, waiting for transfers between devices, permuted(): return lax.ppermute(a, axes, pairs)  8.33 us
  transfers between devices with their start and end apart: 17, of which 8 were waited for; matrix products, arithmetic and copies ran while one was open for 1% of the time, Pallas kernels for 4%

profile of v4, /device:TPU:1, one launch (start us, length us, event | category | flops | bytes accessed | tf_op | source)
XLA Modules:
  0.0 160.9 jit_solution(7412751479418469546)
XLA Ops:
  0.0 3.2 %collective-permute-start.5 = (bf16[1024,128]{1,0:T(8,128)(2,1)}, bf16[1024,128]{1,0:T(8,128)(2,1)S(1)}, u32[]{:S(2)}, u32[]{:S(2)}) collective-permute-start(bf16[1024,128]{1,0:T(8,128)(2,1)} %param.3), channel_id=1, source_target_pairs={{0,1},{1,0},{2,3},{3,2},{4,5},{5,4},{6,7},{7,6},{8,9},{9,8},{10,11... | collective-permute-start | bytes 786440 | tf_op jit(solution)/shard_map/ppermute | solution.py:306
  3.2 0.0 collective-permute-start
  3.2 1.0 slice_bitcast_fusion.4
  4.3 0.3 collective-permute-done.5
  4.6 0.1 slice_bitcast_fusion
  4.7 1.3 collective-permute-start.7
  6.0 0.8 collective-permute-start.6
  6.8 0.7 collective-permute-start.9
  7.5 5.7 %collective-permute-start.1 = (bf16[2,64,1024]{2,1,0:T(8,128)(2,1)S(1)}, bf16[2,64,1024]{2,1,0:T(8,128)(2,1)S(1)}, u32[]{:S(2)}, u32[]{:S(2)}) collective-permute-start(bf16[2,64,1024]{2,1,0:T(8,128)(2,1)S(1)} %maximum_select_fusion.refs_8_), channel_id=1, source_target_pairs={{0,32},{1,225},{32,64},{33,1},{64,96},{65,33},{96,128},{97,65},{12... | collective-permute-start | bytes 786440 | tf_op jit(solution)/shard_map/ppermute | solution.py:306
  13.2 0.1 collective-permute-done.6
  13.3 0.1 pad_maximum_fusion.1.refs_1_
  13.4 2.6 %collective-permute-start.13 = (bf16[2,2,512,128]{3,2,1,0:T(8,128)(2,1)S(1)}, bf16[2,2,512,128]{3,2,1,0:T(8,128)(2,1)S(1)}, u32[]{:S(2)}, u32[]{:S(2)}) collective-permute-start(bf16[2,2,512,128]{3,2,1,0:T(8,128)(2,1)S(1)} %pad_maximum_fusion.1.refs_1_), channel_id=1, source_target_pairs={{0,6},{1,25},{2,0},{3,27},{4,2},{5,29},{6,4},{7,31},{8,14},{9,1},{... | collective-permute-start | bytes 1572872 | tf_op jit(solution)/shard_map/ppermute | solution.py:306
  15.9 0.1 pad_maximum_fusion.2.refs_0_
  16.0 0.1 collective-permute-start.11
  16.1 0.4 collective-permute-done.1
  16.5 5.2 %collective-permute-start.2 = (bf16[2,64,1024]{2,1,0:T(8,128)(2,1)S(1)}, bf16[2,64,1024]{2,1,0:T(8,128)(2,1)S(1)}, u32[]{:S(2)}, u32[]{:S(2)}) collective-permute-start(bf16[2,64,1024]{2,1,0:T(8,128)(2,1)S(1)} %collective-permute-done.1), channel_id=1, source_target_pairs={{0,32},{1,225},{32,64},{33,1},{64,96},{65,33},{96,128},{97,65},{12... | collective-permute-start | bytes 786440 | tf_op jit(solution)/shard_map/ppermute | solution.py:306
  21.7 0.1 collective-permute-start.8
  21.8 2.6 %collective-permute-start.10 = (bf16[2,2,512,128]{3,2,1,0:T(8,128)(2,1)S(1)}, bf16[2,2,512,128]{3,2,1,0:T(8,128)(2,1)S(1)}, u32[]{:S(2)}, u32[]{:S(2)}) collective-permute-start(bf16[2,2,512,128]{3,2,1,0:T(8,128)(2,1)S(1)} %pad_maximum_fusion.2.refs_0_), channel_id=1, source_target_pairs={{0,6},{1,25},{2,0},{3,27},{4,2},{5,29},{6,4},{7,31},{8,14},{9,1},{... | collective-permute-start | bytes 1572872 | tf_op jit(solution)/shard_map/ppermute | solution.py:306
  24.4 0.6 collective-permute-done.2
  25.0 3.4 %collective-permute-start.3 = (bf16[2,64,1024]{2,1,0:T(8,128)(2,1)S(1)}, bf16[2,64,1024]{2,1,0:T(8,128)(2,1)S(1)}, u32[]{:S(2)}, u32[]{:S(2)}) collective-permute-start(bf16[2,64,1024]{2,1,0:T(8,128)(2,1)S(1)} %collective-permute-done.2), channel_id=1, source_target_pairs={{0,32},{1,225},{32,64},{33,1},{64,96},{65,33},{96,128},{97,65},{12... | collective-permute-start | bytes 786440 | tf_op jit(solution)/shard_map/ppermute | solution.py:306
  28.5 2.6 %collective-permute-start.14 = (bf16[2,2,512,128]{3,2,1,0:T(8,128)(2,1)S(1)}, bf16[2,2,512,128]{3,2,1,0:T(8,128)(2,1)S(1)}, u32[]{:S(2)}, u32[]{:S(2)}) collective-permute-start(bf16[2,2,512,128]{3,2,1,0:T(8,128)(2,1)S(1)} %collective-permute-done.13.refs_5_), channel_id=1, source_target_pairs={{0,6},{1,25},{2,0},{3,27},{4,2},{5,29},{6,4},{7,31},{8,14},{9,1},{... | collective-permute-start | bytes 1572872 | tf_op jit(solution)/shard_map/ppermute | solution.py:306
  31.1 0.7 collective-permute-done.3
  31.8 3.4 %collective-permute-start.4 = (bf16[2,64,1024]{2,1,0:T(8,128)(2,1)S(1)}, bf16[2,64,1024]{2,1,0:T(8,128)(2,1)S(1)}, u32[]{:S(2)}, u32[]{:S(2)}) collective-permute-start(bf16[2,64,1024]{2,1,0:T(8,128)(2,1)S(1)} %collective-permute-done.3), channel_id=1, source_target_pairs={{0,32},{1,225},{32,64},{33,1},{64,96},{65,33},{96,128},{97,65},{12... | collective-permute-start | bytes 786440 | tf_op jit(solution)/shard_map/ppermute | solution.py:306
  35.2 0.1 pad_maximum_fusion.refs_10_
  35.3 3.2 %collective-permute-done.4.refs_9_ = bf16[2,64,1024]{2,1,0:T(8,128)(2,1)S(1)} collective-permute-done((bf16[2,64,1024]{2,1,0:T(8,128)(2,1)S(1)}, bf16[2,64,1024]{2,1,0:T(8,128)(2,1)S(1)}, u32[]{:S(2)}, u32[]{:S(2)}) %collective-permute-start.4) | collective-permute-done | bytes 262176 | tf_op jit(solution)/shard_map/ppermute | solution.py:306
  38.5 2.1 %collective-permute-done.12.refs_6_ = bf16[2,2,512,128]{3,2,1,0:T(8,128)(2,1)S(1)} collective-permute-done((bf16[2,2,512,128]{3,2,1,0:T(8,128)(2,1)S(1)}, bf16[2,2,512,128]{3,2,1,0:T(8,128)(2,1)S(1)}, u32[]{:S(2)}, u32[]{:S(2)}) %collective-permute-start.12) | collective-permute-done | bytes 524320 | tf_op jit(solution)/shard_map/ppermute | solution.py:306
  40.6 2.4 %collective-permute-start.15 = (bf16[3,2,64,1024]{3,2,1,0:T(8,128)(2,1)S(1)}, bf16[3,2,64,1024]{3,2,1,0:T(8,128)(2,1)S(1)}, u32[]{:S(2)}, u32[]{:S(2)}) collective-permute-start(bf16[3,2,64,1024]{3,2,1,0:T(8,128)(2,1)S(1)} %pad_maximum_fusion.refs_10_), channel_id=1, source_target_pairs={{0,1},{1,0},{2,3},{3,2},{4,5},{5,4},{6,7},{7,6},{8,9},{9,8},{10,11... | collective-permute-start | bytes 2359304 | tf_op jit(solution)/shard_map/ppermute | solution.py:306
  43.0 3.8 %early_scores.1 = (bf16[4,8,512,128]{3,2,1,0:T(8,128)(2,1)S(1)}, f32[16,1024,128]{2,1,0:T(8,128)S(1)}) custom-call(bf16[2,2,512,128]{3,2,1,0:T(8,128)(2,1)S(1)} %pad_maximum_fusion.2.refs_0_, bf16[2,2,512,128]{3,2,1,0:T(8,128)(2,1)S(1)} %pad_maximum_fusion.1.refs_1_, bf16[2,2,512,128]{3,2,1,0:T(8,128)(2,1)S(1)} %collective-permute-done.11.refs_2_, ...), custom_call_target="tpu_custom_call" | custom-call | flops 2684354560 | bytes 25165824 | tf_op jit(solution)/shard_map/early_scores/pallas_call | solution.py:357
  46.8 0.0 copy-start.1
  46.8 3.5 %late_scores.1 = (f32[16,1024,128]{2,1,0:T(8,128)S(1)}, f32[16,16,128]{2,1,0:T(8,128)S(1)}) custom-call(bf16[3,2,64,1024]{3,2,1,0:T(8,128)(2,1)S(1)} %collective-permute-done.15.swapped_ref, bf16[4,8,512,128]{3,2,1,0:T(8,128)(2,1)S(1)} %get-tuple-element.29.p_ref, f32[16,1024,128]{2,1,0:T(8,128)S(1)} %get-tuple-element.30.old_ref), custom_call_target="tpu_custom_call", output_to_operand_aliasing={{0}: (2, {})} | custom-call | tf_op jit(solution)/shard_map/late_scores/pallas_call | solution.py:357
  50.3 12.9 %all_to_all.30.l_ref = f32[16,16,128]{2,1,0:T(8,128)S(1)} all-to-all(f32[16,16,128]{2,1,0:T(8,128)S(1)} %get-tuple-element.31), channel_id=1, replica_groups=mesh['z'=8,'x'=4,'y'=4,'core'=2] {'x','y'}, dimensions={0} | all-to-all | bytes 262144 | tf_op jit(solution)/shard_map/all_to_all | solution.py:377
  63.2 4.1 %first_columns.1 = (f32[16,128]{1,0:T(8,128)S(1)}, f32[16,1024,128]{2,1,0:T(8,128)S(1)}, f32[16,8,128]{2,1,0:T(8,128)S(1)}, f32[64,1024]{1,0:T(8,128)S(1)}) custom-call(f32[16,16,128]{2,1,0:T(8,128)S(1)} %all_to_all.30.l_ref, f32[16,1024,128]{2,1,0:T(8,128)S(1)} %get-tuple-element.32.t_ref, bf16[64,1024]{1,0:T(8,128)(2,1)S(1)} %copy-done, ...), custom_call_target="tpu_custom_call" | custom-call | tf_op jit(solution)/shard_map/first_columns/pallas_call | solution.py:357
  67.3 15.0 %all_to_all.31.lc_ref = f32[16,8,128]{2,1,0:T(8,128)S(1)} all-to-all(f32[16,8,128]{2,1,0:T(8,128)S(1)} %get-tuple-element.33), channel_id=1, replica_groups=mesh['z'=8,'x'=4,'y'=4,'core'=2] {'z','core'}, dimensions={0} | all-to-all | bytes 131072 | tf_op jit(solution)/shard_map/all_to_all | solution.py:380
  82.3 3.1 %second_rows.1 = (f32[16,1024,128]{2,1,0:T(8,128)S(1)}, f32[16,16,128]{2,1,0:T(8,128)S(1)}, f32[1024,128]{1,0:T(8,128)}) custom-call(f32[16,8,128]{2,1,0:T(8,128)S(1)} %all_to_all.31.lc_ref, f32[16,128]{1,0:T(8,128)S(1)} %get-tuple-element.34.r_ref, f32[16,1024,128]{2,1,0:T(8,128)S(1)} %get-tuple-element.32.t_ref, ...), custom_call_target="tpu_custom_call", output_to_operand_aliasing={{0}: (3, {})} | custom-call | tf_op jit(solution)/shard_map/second_rows/pallas_call | solution.py:357
  85.4 9.7 %all_to_all.32.rho_ref = f32[16,16,128]{2,1,0:T(8,128)S(1)} all-to-all(f32[16,16,128]{2,1,0:T(8,128)S(1)} %get-tuple-element.36), channel_id=1, replica_groups=mesh['z'=8,'x'=4,'y'=4,'core'=2] {'x','y'}, dimensions={0} | all-to-all | bytes 262144 | tf_op jit(solution)/shard_map/all_to_all | solution.py:377
  95.1 0.9 column_sums.1
  96.1 11.8 %all_to_all.33.sums_ref = f32[16,8,128]{2,1,0:T(8,128)S(1)} all-to-all(f32[16,8,128]{2,1,0:T(8,128)S(1)} %column_sums.1), channel_id=1, replica_groups=mesh['z'=8,'x'=4,'y'=4,'core'=2] {'z','core'}, dimensions={0} | all-to-all | bytes 131072 | tf_op jit(solution)/shard_map/all_to_all | solution.py:380
  107.8 1.0 row_sums.1
  108.8 9.9 %all_to_all.34.rho_ref = f32[16,16,128]{2,1,0:T(8,128)S(1)} all-to-all(f32[16,16,128]{2,1,0:T(8,128)S(1)} %get-tuple-element.38), channel_id=1, replica_groups=mesh['z'=8,'x'=4,'y'=4,'core'=2] {'x','y'}, dimensions={0} | all-to-all | bytes 262144 | tf_op jit(solution)/shard_map/all_to_all | solution.py:377
  118.7 3.0 %barycenter_other.1 = f32[520,1024]{1,0:T(8,128)S(1)} custom-call(f32[16,16,128]{2,1,0:T(8,128)S(1)} %all_to_all.34.rho_ref, f32[1024,128]{1,0:T(8,128)S(1)} %get-tuple-element.39.v_ref, f32[16,1024,128]{2,1,0:T(8,128)S(1)} %get-tuple-element.37.k_ref, bf16[4,8,512,128]{3,2,1,0:T(8,128)(2,1)S(1)} %get-tuple-element.29.p_ref), custom_call_target="tpu_custom_call" | custom-call | flops 2147483648 | bytes 16777216 | tf_op jit(solution)/shard_map/barycenter_other/pallas_call | solution.py:357
  121.7 1.8 %collective-permute-start.16 = (f32[520,1024]{1,0:T(8,128)S(1)}, f32[520,1024]{1,0:T(8,128)S(1)}, u32[]{:S(2)}, u32[]{:S(2)}) collective-permute-start(f32[520,1024]{1,0:T(8,128)S(1)} %barycenter_other.1), channel_id=1, source_target_pairs={{0,1},{1,0},{2,3},{3,2},{4,5},{5,4},{6,7},{7,6},{8,9},{9,8},{10,11... | collective-permute-start | bytes 6389768 | tf_op jit(solution)/shard_map/ppermute | solution.py:306
  123.5 3.0 %barycenter_own.1.a_ref = f32[520,1024]{1,0:T(8,128)S(1)} custom-call(f32[16,16,128]{2,1,0:T(8,128)S(1)} %all_to_all.34.rho_ref, f32[1024,128]{1,0:T(8,128)S(1)} %get-tuple-element.39.v_ref, f32[16,1024,128]{2,1,0:T(8,128)S(1)} %get-tuple-element.37.k_ref, bf16[4,8,512,128]{3,2,1,0:T(8,128)(2,1)S(1)} %get-tuple-element.29.p_ref), custom_call_target="tpu_custom_call" | custom-call | flops 2147483648 | bytes 16777216 | tf_op jit(solution)/shard_map/barycenter_own/pallas_call | solution.py:357
  126.5 0.8 collective-permute-done.16.b_ref
  127.3 0.3 means.1
  127.7 0.1 convert_element_type.6
  127.9 31.9 %all_to_all.35 = f16[8,528,128]{2,1,0:T(8,128)(2,1)S(1)} all-to-all(f16[8,528,128]{2,1,0:T(8,128)(2,1)S(1)} %convert_element_type.6), channel_id=1, replica_groups=mesh['z'=8,'x'=4,'y'=4,'core'=2] {'z'}, dimensions={0} | all-to-all | bytes 2162688 | tf_op jit(solution)/shard_map/all_to_all | solution.py:454
  159.8 0.1 convert_element_type.7.parts_ref
  159.9 1.0 update.1
  (16 shorter events, 0.2 us)
Async XLA Ops:
  0.0 7.5 %copy-start = (bf16[64,1024]{1,0:T(8,128)(2,1)S(1)}, bf16[64,1024]{1,0:T(8,128)(2,1)}, u32[]{:S(2)}) copy-start(bf16[64,1024]{1,0:T(8,128)(2,1)} %g_ref.1) | copy-start | bytes 393220
  0.0 4.6 %collective-permute-start.5 = (bf16[1024,128]{1,0:T(8,128)(2,1)}, bf16[1024,128]{1,0:T(8,128)(2,1)S(1)}, u32[]{:S(2)}, u32[]{:S(2)}) collective-permute-start(bf16[1024,128]{1,0:T(8,128)(2,1)} %param.3), channel_id=1, source_target_pairs={{0,1},{1,0},{2,3},{3,2},{4,5},{5,4},{6,7},{7,6},{8,9},{9,8},{10,11... | collective-permute-start | bytes 786440 | tf_op jit(solution)/shard_map/ppermute | solution.py:306
  3.2 4.2 %collective-permute-start = (bf16[64,1024]{1,0:T(8,128)(2,1)}, bf16[64,1024]{1,0:T(8,128)(2,1)S(1)}, u32[]{:S(2)}, u32[]{:S(2)}) collective-permute-start(bf16[64,1024]{1,0:T(8,128)(2,1)} %g_ref.1), channel_id=1, source_target_pairs={{0,1},{1,0},{2,3},{3,2},{4,5},{5,4},{6,7},{7,6},{8,9},{9,8},{10,11... | collective-permute-start | bytes 393224 | tf_op jit(solution)/shard_map/ppermute | solution.py:306
  4.7 8.5 %collective-permute-start.7 = (bf16[2,512,128]{2,1,0:T(8,128)(2,1)S(1)}, bf16[2,512,128]{2,1,0:T(8,128)(2,1)S(1)}, u32[]{:S(2)}, u32[]{:S(2)}) collective-permute-start(bf16[2,512,128]{2,1,0:T(8,128)(2,1)S(1)} %maximum_select_fusion.1), channel_id=1, source_target_pairs={{0,16},{1,5},{2,18},{3,7},{4,20},{5,1},{6,22},{7,3},{8,24},{9,13},... | collective-permute-start | bytes 786440 | tf_op jit(solution)/shard_map/ppermute | solution.py:306
  6.0 7.3 %collective-permute-start.6 = (bf16[2,512,128]{2,1,0:T(8,128)(2,1)S(1)}, bf16[2,512,128]{2,1,0:T(8,128)(2,1)S(1)}, u32[]{:S(2)}, u32[]{:S(2)}) collective-permute-start(bf16[2,512,128]{2,1,0:T(8,128)(2,1)S(1)} %maximum_select_fusion.1), channel_id=1, source_target_pairs={{0,24},{1,7},{2,26},{3,1},{4,28},{5,3},{6,30},{7,5},{8,0},{9,15},{... | collective-permute-start | bytes 786440 | tf_op jit(solution)/shard_map/ppermute | solution.py:306
  6.8 9.1 %collective-permute-start.9 = (bf16[2,512,128]{2,1,0:T(8,128)(2,1)S(1)}, bf16[2,512,128]{2,1,0:T(8,128)(2,1)S(1)}, u32[]{:S(2)}, u32[]{:S(2)}) collective-permute-start(bf16[2,512,128]{2,1,0:T(8,128)(2,1)S(1)} %maximum_select_fusion.1), channel_id=1, source_target_pairs={{0,8},{1,3},{2,10},{3,5},{4,12},{5,7},{6,14},{7,1},{8,16},{9,11},{... | collective-permute-start | bytes 786440 | tf_op jit(solution)/shard_map/ppermute | solution.py:306
  7.5 9.0 %collective-permute-start.1 = (bf16[2,64,1024]{2,1,0:T(8,128)(2,1)S(1)}, bf16[2,64,1024]{2,1,0:T(8,128)(2,1)S(1)}, u32[]{:S(2)}, u32[]{:S(2)}) collective-permute-start(bf16[2,64,1024]{2,1,0:T(8,128)(2,1)S(1)} %maximum_select_fusion.refs_8_), channel_id=1, source_target_pairs={{0,32},{1,225},{32,64},{33,1},{64,96},{65,33},{96,128},{97,65},{12... | collective-permute-start | bytes 786440 | tf_op jit(solution)/shard_map/ppermute | solution.py:306
  13.4 15.1 %collective-permute-start.13 = (bf16[2,2,512,128]{3,2,1,0:T(8,128)(2,1)S(1)}, bf16[2,2,512,128]{3,2,1,0:T(8,128)(2,1)S(1)}, u32[]{:S(2)}, u32[]{:S(2)}) collective-permute-start(bf16[2,2,512,128]{3,2,1,0:T(8,128)(2,1)S(1)} %pad_maximum_fusion.1.refs_1_), channel_id=1, source_target_pairs={{0,6},{1,25},{2,0},{3,27},{4,2},{5,29},{6,4},{7,31},{8,14},{9,1},{... | collective-permute-start | bytes 1572872 | tf_op jit(solution)/shard_map/ppermute | solution.py:306
  16.0 15.1 %collective-permute-start.11 = (bf16[2,2,512,128]{3,2,1,0:T(8,128)(2,1)S(1)}, bf16[2,2,512,128]{3,2,1,0:T(8,128)(2,1)S(1)}, u32[]{:S(2)}, u32[]{:S(2)}) collective-permute-start(bf16[2,2,512,128]{3,2,1,0:T(8,128)(2,1)S(1)} %pad_maximum_fusion.2.refs_0_), channel_id=1, source_target_pairs={{0,2},{1,9},{2,4},{3,11},{4,6},{5,13},{6,0},{7,15},{8,10},{9,17},{... | collective-permute-start | bytes 1572872 | tf_op jit(solution)/shard_map/ppermute | solution.py:306
  16.5 8.6 %collective-permute-start.2 = (bf16[2,64,1024]{2,1,0:T(8,128)(2,1)S(1)}, bf16[2,64,1024]{2,1,0:T(8,128)(2,1)S(1)}, u32[]{:S(2)}, u32[]{:S(2)}) collective-permute-start(bf16[2,64,1024]{2,1,0:T(8,128)(2,1)S(1)} %collective-permute-done.1), channel_id=1, source_target_pairs={{0,32},{1,225},{32,64},{33,1},{64,96},{65,33},{96,128},{97,65},{12... | collective-permute-start | bytes 786440 | tf_op jit(solution)/shard_map/ppermute | solution.py:306
  21.7 13.6 %collective-permute-start.8 = (bf16[2,2,512,128]{3,2,1,0:T(8,128)(2,1)S(1)}, bf16[2,2,512,128]{3,2,1,0:T(8,128)(2,1)S(1)}, u32[]{:S(2)}, u32[]{:S(2)}) collective-permute-start(bf16[2,2,512,128]{3,2,1,0:T(8,128)(2,1)S(1)} %pad_maximum_fusion.1.refs_1_), channel_id=1, source_target_pairs={{0,2},{1,9},{2,4},{3,11},{4,6},{5,13},{6,0},{7,15},{8,10},{9,17},{... | collective-permute-start | bytes 1572872 | tf_op jit(solution)/shard_map/ppermute | solution.py:306
  21.8 13.5 %collective-permute-start.10 = (bf16[2,2,512,128]{3,2,1,0:T(8,128)(2,1)S(1)}, bf16[2,2,512,128]{3,2,1,0:T(8,128)(2,1)S(1)}, u32[]{:S(2)}, u32[]{:S(2)}) collective-permute-start(bf16[2,2,512,128]{3,2,1,0:T(8,128)(2,1)S(1)} %pad_maximum_fusion.2.refs_0_), channel_id=1, source_target_pairs={{0,6},{1,25},{2,0},{3,27},{4,2},{5,29},{6,4},{7,31},{8,14},{9,1},{... | collective-permute-start | bytes 1572872 | tf_op jit(solution)/shard_map/ppermute | solution.py:306
  25.0 6.7 %collective-permute-start.3 = (bf16[2,64,1024]{2,1,0:T(8,128)(2,1)S(1)}, bf16[2,64,1024]{2,1,0:T(8,128)(2,1)S(1)}, u32[]{:S(2)}, u32[]{:S(2)}) collective-permute-start(bf16[2,64,1024]{2,1,0:T(8,128)(2,1)S(1)} %collective-permute-done.2), channel_id=1, source_target_pairs={{0,32},{1,225},{32,64},{33,1},{64,96},{65,33},{96,128},{97,65},{12... | collective-permute-start | bytes 786440 | tf_op jit(solution)/shard_map/ppermute | solution.py:306
  28.5 10.0 %collective-permute-start.14 = (bf16[2,2,512,128]{3,2,1,0:T(8,128)(2,1)S(1)}, bf16[2,2,512,128]{3,2,1,0:T(8,128)(2,1)S(1)}, u32[]{:S(2)}, u32[]{:S(2)}) collective-permute-start(bf16[2,2,512,128]{3,2,1,0:T(8,128)(2,1)S(1)} %collective-permute-done.13.refs_5_), channel_id=1, source_target_pairs={{0,6},{1,25},{2,0},{3,27},{4,2},{5,29},{6,4},{7,31},{8,14},{9,1},{... | collective-permute-start | bytes 1572872 | tf_op jit(solution)/shard_map/ppermute | solution.py:306
  31.0 9.5 %collective-permute-start.12 = (bf16[2,2,512,128]{3,2,1,0:T(8,128)(2,1)S(1)}, bf16[2,2,512,128]{3,2,1,0:T(8,128)(2,1)S(1)}, u32[]{:S(2)}, u32[]{:S(2)}) collective-permute-start(bf16[2,2,512,128]{3,2,1,0:T(8,128)(2,1)S(1)} %collective-permute-done.11.refs_2_), channel_id=1, source_target_pairs={{0,2},{1,9},{2,4},{3,11},{4,6},{5,13},{6,0},{7,15},{8,10},{9,17},{... | collective-permute-start | bytes 1572872 | tf_op jit(solution)/shard_map/ppermute | solution.py:306
  31.8 6.7 %collective-permute-start.4 = (bf16[2,64,1024]{2,1,0:T(8,128)(2,1)S(1)}, bf16[2,64,1024]{2,1,0:T(8,128)(2,1)S(1)}, u32[]{:S(2)}, u32[]{:S(2)}) collective-permute-start(bf16[2,64,1024]{2,1,0:T(8,128)(2,1)S(1)} %collective-permute-done.3), channel_id=1, source_target_pairs={{0,32},{1,225},{32,64},{33,1},{64,96},{65,33},{96,128},{97,65},{12... | collective-permute-start | bytes 786440 | tf_op jit(solution)/shard_map/ppermute | solution.py:306
  40.6 6.2 %collective-permute-start.15 = (bf16[3,2,64,1024]{3,2,1,0:T(8,128)(2,1)S(1)}, bf16[3,2,64,1024]{3,2,1,0:T(8,128)(2,1)S(1)}, u32[]{:S(2)}, u32[]{:S(2)}) collective-permute-start(bf16[3,2,64,1024]{3,2,1,0:T(8,128)(2,1)S(1)} %pad_maximum_fusion.refs_10_), channel_id=1, source_target_pairs={{0,1},{1,0},{2,3},{3,2},{4,5},{5,4},{6,7},{7,6},{8,9},{9,8},{10,11... | collective-permute-start | bytes 2359304 | tf_op jit(solution)/shard_map/ppermute | solution.py:306
  46.8 16.4 %copy-start.1 = (f32[64,1024]{1,0:T(8,128)S(1)}, f32[64,1024]{1,0:T(8,128)}, u32[]{:S(2)}) copy-start(f32[64,1024]{1,0:T(8,128)} %n_ref.1) | copy-start | bytes 786436
  121.7 5.7 %collective-permute-start.16 = (f32[520,1024]{1,0:T(8,128)S(1)}, f32[520,1024]{1,0:T(8,128)S(1)}, u32[]{:S(2)}, u32[]{:S(2)}) collective-permute-start(f32[520,1024]{1,0:T(8,128)S(1)} %barycenter_other.1), channel_id=1, source_target_pairs={{0,1},{1,0},{2,3},{3,2},{4,5},{5,4},{6,7},{7,6},{8,9},{9,8},{10,11... | collective-permute-start | bytes 6389768 | tf_op jit(solution)/shard_map/ppermute | solution.py:306

commit v5 on v4

--- a/solution.py
+++ b/solution.py
@@ -62,7 +62,7 @@
             p_ref[px, 2 * py + f] = ref[n, f]
 
 
-def score_columns(scale, blocks, p_ref, t_ref, g_ref, c0_ref, after):
+def score_columns(scale, blocks, p_ref, t_ref, rows_ref, g_ref, c0_ref):
     nx, slices, rows, _ = p_ref.shape
     nz = 8
     z = lax.axis_index("z")
@@ -79,52 +79,55 @@
             c0_ref[at, :] = jnp.broadcast_to(sq * (-0.5 * scale), (own, LANES))
             starts.append(pl.multiple_of((c * nz + pz) * own, own))
 
+    def reduce(k):
+        top = jnp.full((8, LANES), -jnp.inf, F32)
+        for start in starts:
+            t = t_ref[k, pl.ds(start, own), :]
+            top = jnp.maximum(top, jnp.max(t.reshape(own // 8, 8, LANES), axis=0))
+        top = jnp.max(top, axis=0, keepdims=True)
+        total = jnp.zeros((8, LANES), F32)
+        for start in starts:
+            e = jnp.exp2(t_ref[k, pl.ds(start, own), :] - top)
+            total = total + jnp.sum(e.reshape(own // 8, 8, LANES), axis=0)
+        rows_ref[k:k + 1, :] = top + jnp.log2(jnp.sum(total, axis=0, keepdims=True))
+
     per = rows // WIDE
     for n in range(nx * per):
         at = pl.ds(n % per * WIDE, WIDE)
         p = jnp.concatenate([p_ref[n // per, f, at, :] for f in range(slices)], axis=1)
         cross = lax.dot_general(g_ref[...], p, (((1,), (1,)), ((), ())), preferred_element_type=F32)
         if n:
-            after(n - 1)
+            reduce(2 * n - 2)
+            reduce(2 * n - 1)
         for k in range(2):
             for m, start in enumerate(starts):
                 part = slice(m * own, (m + 1) * own)
                 t_ref[2 * n + k, pl.ds(start, own), :] = (
                     cross[part, k * LANES:(k + 1) * LANES] * scale + c0_ref[part, :]
                 )
-    after(nx * per - 1)
+    reduce(2 * nx * per - 2)
+    reduce(2 * nx * per - 1)
 
 
 def early_score_kernel(scale, *refs):
     blocks, (own_ref, far_ref, near_ref) = refs[:8], refs[8:11]
-    p_ref, t_ref, g_ref, c0_ref = refs[11:]
+    p_ref, t_ref, rows_ref, g_ref, c0_ref = refs[11:]
     for ref, pair, second in zip(blocks, (0, 1, 0, 0, 1, 1, 0, 1), (0, 0, -1, 1, -1, 1, -2, 2)):
         place(ref, pair, second, p_ref)
     sign = jnp.where(lax.axis_index("core") == 0, -1, 1)
     columns = [(own_ref, 0), (far_ref, 4)] + [(near_ref.at[k - 1], sign * k) for k in (1, 2, 3)]
-    score_columns(scale, columns, p_ref, t_ref, g_ref, c0_ref, lambda n: None)
-
-
-def late_score_kernel(scale, swapped_ref, p_ref, old_ref, t_ref, l_ref, g_ref, c0_ref, rows_ref):
+    score_columns(scale, columns, p_ref, t_ref, rows_ref, g_ref, c0_ref)
+
+
+def late_score_kernel(scale, swapped_ref, p_ref, early_ref, old_ref, t_ref, l_ref, g_ref, c0_ref, rows_ref):
     del old_ref
-    cols = t_ref.shape[1]
-
-    def reduce(n):
-        for k in (2 * n, 2 * n + 1):
-            top = jnp.full((8, LANES), -jnp.inf, F32)
-            for at in chunks(cols):
-                top = jnp.maximum(top, jnp.max(t_ref[k, at, :].reshape(SUB // 8, 8, LANES), axis=0))
-            top = jnp.max(top, axis=0, keepdims=True)
-            total = jnp.zeros((8, LANES), F32)
-            for at in chunks(cols):
-                e = jnp.exp2(t_ref[k, at, :] - top)
-                total = total + jnp.sum(e.reshape(SUB // 8, 8, LANES), axis=0)
-            rows_ref[k:k + 1, :] = top + jnp.log2(jnp.sum(total, axis=0, keepdims=True))
-
     sign = jnp.where(lax.axis_index("core") == 0, 1, -1)
     columns = [(swapped_ref.at[k - 1], sign * k) for k in (1, 2, 3)]
-    score_columns(scale, columns, p_ref, t_ref, g_ref, c0_ref, reduce)
-    l_ref[...] = jnp.broadcast_to(rows_ref[...][None], l_ref.shape)
+    score_columns(scale, columns, p_ref, t_ref, rows_ref, g_ref, c0_ref)
+    late, early = rows_ref[...], early_ref[...]
+    top = jnp.maximum(late, early)
+    total = top + jnp.log2(jnp.exp2(late - top) + jnp.exp2(early - top))
+    l_ref[...] = jnp.broadcast_to(total[None], l_ref.shape)
 
 
 def first_column_kernel(log_ng, l_ref, t_ref, g_ref, n_ref, r_ref, k_ref, lc_ref, base_ref, m_ref, s_ref):
@@ -233,18 +236,6 @@
     scaled = ng / jnp.sum(rho_ref[...], axis=0)
     u = [scaled[n:n + 1, :] for n in range(tiles)]
 
-    @pl.loop(0, cols, step=SUB)
-    def _(c):
-        at = pl.ds(pl.multiple_of(c, SUB), SUB)
-        source = pl.ds(pl.multiple_of(begin + c, SUB), SUB)
-        v = v_ref[source, :]
-        total = jnp.zeros((SUB, LANES), F32)
-        for n in range(tiles):
-            w = k_ref[n, source, :] * u[n] * v
-            total = total + w
-            w_ref[at, n * LANES:(n + 1) * LANES] = w.astype(BF16)
-        mass_ref[at, :] = total
-
     p = jnp.concatenate(
         [
             jnp.concatenate([p_ref[x, f] for f in range(p_ref.shape[1])], axis=1)
@@ -252,7 +243,21 @@
         ],
         axis=0,
     )
-    out_ref[0:cols, :] = jnp.dot(w_ref[...], p, preferred_element_type=F32)
+    part = cols // 2
+    for first in range(0, cols, part):
+        for c in range(first, first + part, SUB):
+            at = pl.ds(c, SUB)
+            source = pl.ds(pl.multiple_of(begin + c, SUB), SUB)
+            v = v_ref[source, :]
+            total = jnp.zeros((SUB, LANES), F32)
+            for n in range(tiles):
+                w = k_ref[n, source, :] * u[n] * v
+                total = total + w
+                w_ref[at, n * LANES:(n + 1) * LANES] = w.astype(BF16)
+            mass_ref[at, :] = total
+        out_ref[first:first + part, :] = jnp.dot(
+            w_ref[first:first + part, :], p, preferred_element_type=F32
+        )
     mass = jnp.sum(jnp.transpose(mass_ref[...]), axis=0, keepdims=True)
     out_ref[cols:, 0:cols] = jnp.broadcast_to(mass, (out_ref.shape[0] - cols, cols))
 
@@ -330,14 +335,16 @@
     h1, h2 = along(False, 1, s1), along(False, -1, t2)
 
     got = swap(generated)
-    chain = [jnp.where(core == 0, jnp.stack([generated, got]), jnp.stack([got, generated]))]
-    for _ in range(4):
-        chain.append(
-            permuted(chain[-1], ("z", "core"), lambda z, c: (z + (1 if c == 0 else -1), c))
-        )
-    near = jnp.stack(chain[1:4])
-    near, far, t1, s2, h1, h2 = lax.optimization_barrier((near, chain[4], t1, s2, h1, h2))
-    return (s, t, s1, s2, t1, t2, h1, h2), (chain[0], far, near), swap(near)
+    g0 = jnp.where(core == 0, jnp.stack([generated, got]), jnp.stack([got, generated]))
+
+    def onward(g, d):
+        return permuted(g, ("z", "core"), lambda z, c: (z + (d if c == 0 else -d), c))
+
+    g1, g2 = onward(g0, 1), onward(g0, 2)
+    g34 = onward(jnp.stack([g1, g2]), 2)
+    near, far = jnp.stack([g1, g2, g34[0]]), g34[1]
+    near, far, t1, s2, h1, h2 = lax.optimization_barrier((near, far, t1, s2, h1, h2))
+    return (s, t, s1, s2, t1, t2, h1, h2), (g0, far, near), swap(near)
 
 
 def shards(private, generated, noise):
@@ -381,10 +388,14 @@
 
     blocks, columns, swapped = gather(private, generated)
     others = cols * 3 // 8
-    p, t = call(
+    p, t, early = call(
         functools.partial(early_score_kernel, scale),
         "early_scores",
-        [jax.ShapeDtypeStruct((nx, 2 * ny, rows_per // 2, width), BF16), k_shape],
+        [
+            jax.ShapeDtypeStruct((nx, 2 * ny, rows_per // 2, width), BF16),
+            k_shape,
+            f32(row_tiles, LANES),
+        ],
         [pltpu.VMEM((cols - others, features), BF16), pltpu.VMEM((cols - others, LANES), F32)],
         *blocks, *columns,
         cost=pl.CostEstimate(
@@ -400,8 +411,8 @@
             pltpu.VMEM((others, LANES), F32),
             pltpu.VMEM((row_tiles, LANES), F32),
         ],
-        swapped, p, t,
-        aliases={2: 0},
+        swapped, p, early, t,
+        aliases={3: 0},
     )
     r, k, lc, base = call(
         functools.partial(first_column_kernel, math.log2(ng)),

time: 161 us -> 159 us (0.988)
  starting transfers between devices: 35.9 us -> 26 us
  waiting for transfers between devices: 8.33 us -> 17.9 us
    ppermute x17 -> x16, starting transfers between devices: 35.9 us -> 26 us  [permuted(): return lax.ppermute(a, axes, pairs)]
    ppermute x17 -> x16, waiting for transfers between devices: 8.33 us -> 17.9 us  [permuted(): return lax.ppermute(a, axes, pairs)]
  transfers between devices with their start and end apart: 17 -> 16, of which waited for: 8 -> 7; matrix products, arithmetic and copies ran while one was open for 1% -> 1% of each run, Pallas kernels for 4% -> 4%
where the time goes in v5:
time: 159 us
  blocking collectives  90.2 us (57%)
  starting transfers between devices  26 us (16%)
  Pallas kernels  22.5 us (14%)
  waiting for transfers between devices  17.9 us (11%)
    all_to_all x1, blocking collectives, shards(): parts = lax.all_to_all(parts.astype(F16), 'z', 0, 0, tiled=True).astype(F32)  31.9 us
    all_to_all x3, blocking collectives, over_rows(): return lax.all_to_all(a, ('x', 'y'), 0, 0, tiled=True)  31.9 us
    all_to_all x2, blocking collectives, over_columns(): return lax.all_to_all(a, ('z', 'core'), 0, 0, tiled=True)  26.4 us
    ppermute x16, starting transfers between devices, permuted(): return lax.ppermute(a, axes, pairs)  26 us
    pallas_call x10, Pallas kernels, call(): pl.pallas_call(body, out_shape=out_shape, scratch_shapes=scratch, compile...  22.5 us
    ppermute x16, waiting for transfers between devices, permuted(): return lax.ppermute(a, axes, pairs)  17.9 us
  transfers between devices with their start and end apart: 16, of which 7 were waited for; matrix products, arithmetic and copies ran while one was open for 1% of the time, Pallas kernels for 4%

profile of v5, /device:TPU:1, one launch (start us, length us, event | category | flops | bytes accessed | tf_op | source)
XLA Modules:
  0.0 158.6 jit_solution(8207953074196369998)
XLA Ops:
  0.0 3.2 %collective-permute-start.4 = (bf16[1024,128]{1,0:T(8,128)(2,1)}, bf16[1024,128]{1,0:T(8,128)(2,1)S(1)}, u32[]{:S(2)}, u32[]{:S(2)}) collective-permute-start(bf16[1024,128]{1,0:T(8,128)(2,1)} %param.3), channel_id=1, source_target_pairs={{0,1},{1,0},{2,3},{3,2},{4,5},{5,4},{6,7},{7,6},{8,9},{9,8},{10,11... | collective-permute-start | bytes 786440 | tf_op jit(solution)/shard_map/ppermute | solution.py:311
  3.2 0.0 collective-permute-start
  3.2 1.0 slice_bitcast_fusion.5
  4.3 0.3 collective-permute-done.4
  4.6 0.1 slice_bitcast_fusion.1
  4.7 1.3 collective-permute-start.6
  6.0 0.8 collective-permute-start.5
  6.8 0.7 collective-permute-start.8
  7.5 6.1 %collective-permute-start.2 = (bf16[2,64,1024]{2,1,0:T(8,128)(2,1)S(1)}, bf16[2,64,1024]{2,1,0:T(8,128)(2,1)S(1)}, u32[]{:S(2)}, u32[]{:S(2)}) collective-permute-start(bf16[2,64,1024]{2,1,0:T(8,128)(2,1)S(1)} %maximum_select_fusion.refs_8_), channel_id=1, source_target_pairs={{0,64},{1,193},{32,96},{33,225},{64,128},{65,1},{96,160},{97,33},{... | collective-permute-start | bytes 786440 | tf_op jit(solution)/shard_map/ppermute | solution.py:311
  13.6 0.7 collective-permute-start.1
  14.4 0.1 pad_maximum_fusion.2.refs_1_
  14.5 2.6 %collective-permute-start.12 = (bf16[2,2,512,128]{3,2,1,0:T(8,128)(2,1)S(1)}, bf16[2,2,512,128]{3,2,1,0:T(8,128)(2,1)S(1)}, u32[]{:S(2)}, u32[]{:S(2)}) collective-permute-start(bf16[2,2,512,128]{3,2,1,0:T(8,128)(2,1)S(1)} %pad_maximum_fusion.2.refs_1_), channel_id=1, source_target_pairs={{0,6},{1,25},{2,0},{3,27},{4,2},{5,29},{6,4},{7,31},{8,14},{9,1},{... | collective-permute-start | bytes 1572872 | tf_op jit(solution)/shard_map/ppermute | solution.py:311
  17.0 0.1 pad_maximum_fusion.3.refs_0_
  17.1 0.1 collective-permute-start.10
  17.2 2.6 %collective-permute-done.2 = bf16[2,64,1024]{2,1,0:T(8,128)(2,1)S(1)} collective-permute-done((bf16[2,64,1024]{2,1,0:T(8,128)(2,1)S(1)}, bf16[2,64,1024]{2,1,0:T(8,128)(2,1)S(1)}, u32[]{:S(2)}, u32[]{:S(2)}) %collective-permute-start.2) | collective-permute-done | bytes 262176 | tf_op jit(solution)/shard_map/ppermute | solution.py:311
  19.7 2.8 %collective-permute-done.1 = bf16[2,64,1024]{2,1,0:T(8,128)(2,1)S(1)} collective-permute-done((bf16[2,64,1024]{2,1,0:T(8,128)(2,1)S(1)}, bf16[2,64,1024]{2,1,0:T(8,128)(2,1)S(1)}, u32[]{:S(2)}, u32[]{:S(2)}) %collective-permute-start.1) | collective-permute-done | bytes 262176 | tf_op jit(solution)/shard_map/ppermute | solution.py:311
  22.6 0.1 pad_maximum_fusion.1
  22.6 2.7 %collective-permute-start.3 = (bf16[2,2,64,1024]{3,2,1,0:T(8,128)(2,1)S(1)}, bf16[2,2,64,1024]{3,2,1,0:T(8,128)(2,1)S(1)}, u32[]{:S(2)}, u32[]{:S(2)}) collective-permute-start(bf16[2,2,64,1024]{3,2,1,0:T(8,128)(2,1)S(1)} %pad_maximum_fusion.1), channel_id=1, source_target_pairs={{0,64},{1,193},{32,96},{33,225},{64,128},{65,1},{96,160},{97,33},{... | collective-permute-start | bytes 1572872 | tf_op jit(solution)/shard_map/ppermute | solution.py:311
  25.4 1.2 collective-permute-start.7
  26.6 1.5 collective-permute-start.9
  28.0 1.3 collective-permute-start.13
  29.3 0.2 collective-permute-start.11
  29.5 4.7 %collective-permute-done.3 = bf16[2,2,64,1024]{3,2,1,0:T(8,128)(2,1)S(1)} collective-permute-done((bf16[2,2,64,1024]{3,2,1,0:T(8,128)(2,1)S(1)}, bf16[2,2,64,1024]{3,2,1,0:T(8,128)(2,1)S(1)}, u32[]{:S(2)}, u32[]{:S(2)}) %collective-permute-start.3) | collective-permute-done | bytes 524320 | tf_op jit(solution)/shard_map/ppermute | solution.py:311
  34.2 0.1 pad_maximum_fusion.refs_10_
  34.3 0.6 collective-permute-done.7.refs_4_
  34.9 5.6 %collective-permute-done.13.refs_7_ = bf16[2,2,512,128]{3,2,1,0:T(8,128)(2,1)S(1)} collective-permute-done((bf16[2,2,512,128]{3,2,1,0:T(8,128)(2,1)S(1)}, bf16[2,2,512,128]{3,2,1,0:T(8,128)(2,1)S(1)}, u32[]{:S(2)}, u32[]{:S(2)}) %collective-permute-start.13) | collective-permute-done | bytes 524320 | tf_op jit(solution)/shard_map/ppermute | solution.py:311
  40.5 1.8 %collective-permute-start.14 = (bf16[3,2,64,1024]{3,2,1,0:T(8,128)(2,1)S(1)}, bf16[3,2,64,1024]{3,2,1,0:T(8,128)(2,1)S(1)}, u32[]{:S(2)}, u32[]{:S(2)}) collective-permute-start(bf16[3,2,64,1024]{3,2,1,0:T(8,128)(2,1)S(1)} %pad_maximum_fusion.refs_10_), channel_id=1, source_target_pairs={{0,1},{1,0},{2,3},{3,2},{4,5},{5,4},{6,7},{7,6},{8,9},{9,8},{10,11... | collective-permute-start | bytes 2359304 | tf_op jit(solution)/shard_map/ppermute | solution.py:311
  42.4 4.6 %early_scores.1 = (bf16[4,8,512,128]{3,2,1,0:T(8,128)(2,1)S(1)}, f32[16,1024,128]{2,1,0:T(8,128)S(1)}, f32[16,128]{1,0:T(8,128)S(1)}) custom-call(bf16[2,2,512,128]{3,2,1,0:T(8,128)(2,1)S(1)} %pad_maximum_fusion.3.refs_0_, bf16[2,2,512,128]{3,2,1,0:T(8,128)(2,1)S(1)} %pad_maximum_fusion.2.refs_1_, ...), custom_call_target="tpu_custom_call" | custom-call | flops 2684354560 | bytes 25165824 | tf_op jit(solution)/shard_map/early_scores/pallas_call | solution.py:364
  46.9 0.0 copy-start.1
  46.9 2.6 %late_scores.1 = (f32[16,1024,128]{2,1,0:T(8,128)S(1)}, f32[16,16,128]{2,1,0:T(8,128)S(1)}) custom-call(bf16[3,2,64,1024]{3,2,1,0:T(8,128)(2,1)S(1)} %collective-permute-done.14.swapped_ref, bf16[4,8,512,128]{3,2,1,0:T(8,128)(2,1)S(1)} %get-tuple-element.30.p_ref, f32[16,128]{1,0:T(8,128)S(1)} %get-tuple-element.31.early_ref, ...), custom_call_target="tpu_custom_call", output_to_operand_aliasing={{0}: (3, {})} | custom-call | tf_op jit(solution)/shard_map/late_scores/pallas_call | solution.py:364
  49.5 12.3 %all_to_all.30.l_ref = f32[16,16,128]{2,1,0:T(8,128)S(1)} all-to-all(f32[16,16,128]{2,1,0:T(8,128)S(1)} %get-tuple-element.33), channel_id=1, replica_groups=mesh['z'=8,'x'=4,'y'=4,'core'=2] {'x','y'}, dimensions={0} | all-to-all | bytes 262144 | tf_op jit(solution)/shard_map/all_to_all | solution.py:384
  61.8 4.1 %first_columns.1 = (f32[16,128]{1,0:T(8,128)S(1)}, f32[16,1024,128]{2,1,0:T(8,128)S(1)}, f32[16,8,128]{2,1,0:T(8,128)S(1)}, f32[64,1024]{1,0:T(8,128)S(1)}) custom-call(f32[16,16,128]{2,1,0:T(8,128)S(1)} %all_to_all.30.l_ref, f32[16,1024,128]{2,1,0:T(8,128)S(1)} %get-tuple-element.34.t_ref, bf16[64,1024]{1,0:T(8,128)(2,1)S(1)} %copy-done, ...), custom_call_target="tpu_custom_call" | custom-call | tf_op jit(solution)/shard_map/first_columns/pallas_call | solution.py:364
  65.9 14.6 %all_to_all.31.lc_ref = f32[16,8,128]{2,1,0:T(8,128)S(1)} all-to-all(f32[16,8,128]{2,1,0:T(8,128)S(1)} %get-tuple-element.35), channel_id=1, replica_groups=mesh['z'=8,'x'=4,'y'=4,'core'=2] {'z','core'}, dimensions={0} | all-to-all | bytes 131072 | tf_op jit(solution)/shard_map/all_to_all | solution.py:387
  80.5 3.1 %second_rows.1 = (f32[16,1024,128]{2,1,0:T(8,128)S(1)}, f32[16,16,128]{2,1,0:T(8,128)S(1)}, f32[1024,128]{1,0:T(8,128)}) custom-call(f32[16,8,128]{2,1,0:T(8,128)S(1)} %all_to_all.31.lc_ref, f32[16,128]{1,0:T(8,128)S(1)} %get-tuple-element.36.r_ref, f32[16,1024,128]{2,1,0:T(8,128)S(1)} %get-tuple-element.34.t_ref, ...), custom_call_target="tpu_custom_call", output_to_operand_aliasing={{0}: (3, {})} | custom-call | tf_op jit(solution)/shard_map/second_rows/pallas_call | solution.py:364
  83.6 9.7 %all_to_all.32.rho_ref = f32[16,16,128]{2,1,0:T(8,128)S(1)} all-to-all(f32[16,16,128]{2,1,0:T(8,128)S(1)} %get-tuple-element.38), channel_id=1, replica_groups=mesh['z'=8,'x'=4,'y'=4,'core'=2] {'x','y'}, dimensions={0} | all-to-all | bytes 262144 | tf_op jit(solution)/shard_map/all_to_all | solution.py:384
  93.4 0.9 column_sums.1
  94.3 11.8 %all_to_all.33.sums_ref = f32[16,8,128]{2,1,0:T(8,128)S(1)} all-to-all(f32[16,8,128]{2,1,0:T(8,128)S(1)} %column_sums.1), channel_id=1, replica_groups=mesh['z'=8,'x'=4,'y'=4,'core'=2] {'z','core'}, dimensions={0} | all-to-all | bytes 131072 | tf_op jit(solution)/shard_map/all_to_all | solution.py:387
  106.1 1.0 row_sums.1
  107.1 9.9 %all_to_all.34.rho_ref = f32[16,16,128]{2,1,0:T(8,128)S(1)} all-to-all(f32[16,16,128]{2,1,0:T(8,128)S(1)} %get-tuple-element.40), channel_id=1, replica_groups=mesh['z'=8,'x'=4,'y'=4,'core'=2] {'x','y'}, dimensions={0} | all-to-all | bytes 262144 | tf_op jit(solution)/shard_map/all_to_all | solution.py:384
  116.9 2.5 %barycenter_other.1 = f32[520,1024]{1,0:T(8,128)S(1)} custom-call(f32[16,16,128]{2,1,0:T(8,128)S(1)} %all_to_all.34.rho_ref, f32[1024,128]{1,0:T(8,128)S(1)} %get-tuple-element.41.v_ref, f32[16,1024,128]{2,1,0:T(8,128)S(1)} %get-tuple-element.39.k_ref, bf16[4,8,512,128]{3,2,1,0:T(8,128)(2,1)S(1)} %get-tuple-element.30.p_ref), custom_call_target="tpu_custom_call" | custom-call | flops 2147483648 | bytes 16777216 | tf_op jit(solution)/shard_map/barycenter_other/pallas_call | solution.py:364
  119.4 1.8 %collective-permute-start.15 = (f32[520,1024]{1,0:T(8,128)S(1)}, f32[520,1024]{1,0:T(8,128)S(1)}, u32[]{:S(2)}, u32[]{:S(2)}) collective-permute-start(f32[520,1024]{1,0:T(8,128)S(1)} %barycenter_other.1), channel_id=1, source_target_pairs={{0,1},{1,0},{2,3},{3,2},{4,5},{5,4},{6,7},{7,6},{8,9},{9,8},{10,11... | collective-permute-start | bytes 6389768 | tf_op jit(solution)/shard_map/ppermute | solution.py:311
  121.3 2.5 %barycenter_own.1.a_ref = f32[520,1024]{1,0:T(8,128)S(1)} custom-call(f32[16,16,128]{2,1,0:T(8,128)S(1)} %all_to_all.34.rho_ref, f32[1024,128]{1,0:T(8,128)S(1)} %get-tuple-element.41.v_ref, f32[16,1024,128]{2,1,0:T(8,128)S(1)} %get-tuple-element.39.k_ref, bf16[4,8,512,128]{3,2,1,0:T(8,128)(2,1)S(1)} %get-tuple-element.30.p_ref), custom_call_target="tpu_custom_call" | custom-call | flops 2147483648 | bytes 16777216 | tf_op jit(solution)/shard_map/barycenter_own/pallas_call | solution.py:364
  123.8 1.3 collective-permute-done.15.b_ref
  125.1 0.3 means.1
  125.5 0.1 convert_element_type.6
  125.6 31.9 %all_to_all.35 = f16[8,528,128]{2,1,0:T(8,128)(2,1)S(1)} all-to-all(f16[8,528,128]{2,1,0:T(8,128)(2,1)S(1)} %convert_element_type.6), channel_id=1, replica_groups=mesh['z'=8,'x'=4,'y'=4,'core'=2] {'z'}, dimensions={0} | all-to-all | bytes 2162688 | tf_op jit(solution)/shard_map/all_to_all | solution.py:465
  157.5 0.1 convert_element_type.7.parts_ref
  157.7 1.0 update.1
  (16 shorter events, 0.2 us)
Async XLA Ops:
  0.0 7.5 %copy-start = (bf16[64,1024]{1,0:T(8,128)(2,1)S(1)}, bf16[64,1024]{1,0:T(8,128)(2,1)}, u32[]{:S(2)}) copy-start(bf16[64,1024]{1,0:T(8,128)(2,1)} %g_ref.1) | copy-start | bytes 393220
  0.0 4.6 %collective-permute-start.4 = (bf16[1024,128]{1,0:T(8,128)(2,1)}, bf16[1024,128]{1,0:T(8,128)(2,1)S(1)}, u32[]{:S(2)}, u32[]{:S(2)}) collective-permute-start(bf16[1024,128]{1,0:T(8,128)(2,1)} %param.3), channel_id=1, source_target_pairs={{0,1},{1,0},{2,3},{3,2},{4,5},{5,4},{6,7},{7,6},{8,9},{9,8},{10,11... | collective-permute-start | bytes 786440 | tf_op jit(solution)/shard_map/ppermute | solution.py:311
  3.2 4.2 %collective-permute-start = (bf16[64,1024]{1,0:T(8,128)(2,1)}, bf16[64,1024]{1,0:T(8,128)(2,1)S(1)}, u32[]{:S(2)}, u32[]{:S(2)}) collective-permute-start(bf16[64,1024]{1,0:T(8,128)(2,1)} %g_ref.1), channel_id=1, source_target_pairs={{0,1},{1,0},{2,3},{3,2},{4,5},{5,4},{6,7},{7,6},{8,9},{9,8},{10,11... | collective-permute-start | bytes 393224 | tf_op jit(solution)/shard_map/ppermute | solution.py:311
  4.7 9.6 %collective-permute-start.6 = (bf16[2,512,128]{2,1,0:T(8,128)(2,1)S(1)}, bf16[2,512,128]{2,1,0:T(8,128)(2,1)S(1)}, u32[]{:S(2)}, u32[]{:S(2)}) collective-permute-start(bf16[2,512,128]{2,1,0:T(8,128)(2,1)S(1)} %maximum_select_fusion.1), channel_id=1, source_target_pairs={{0,16},{1,5},{2,18},{3,7},{4,20},{5,1},{6,22},{7,3},{8,24},{9,13},... | collective-permute-start | bytes 786440 | tf_op jit(solution)/shard_map/ppermute | solution.py:311
  6.0 8.4 %collective-permute-start.5 = (bf16[2,512,128]{2,1,0:T(8,128)(2,1)S(1)}, bf16[2,512,128]{2,1,0:T(8,128)(2,1)S(1)}, u32[]{:S(2)}, u32[]{:S(2)}) collective-permute-start(bf16[2,512,128]{2,1,0:T(8,128)(2,1)S(1)} %maximum_select_fusion.1), channel_id=1, source_target_pairs={{0,24},{1,7},{2,26},{3,1},{4,28},{5,3},{6,30},{7,5},{8,0},{9,15},{... | collective-permute-start | bytes 786440 | tf_op jit(solution)/shard_map/ppermute | solution.py:311
  6.8 10.2 %collective-permute-start.8 = (bf16[2,512,128]{2,1,0:T(8,128)(2,1)S(1)}, bf16[2,512,128]{2,1,0:T(8,128)(2,1)S(1)}, u32[]{:S(2)}, u32[]{:S(2)}) collective-permute-start(bf16[2,512,128]{2,1,0:T(8,128)(2,1)S(1)} %maximum_select_fusion.1), channel_id=1, source_target_pairs={{0,8},{1,3},{2,10},{3,5},{4,12},{5,7},{6,14},{7,1},{8,16},{9,11},{... | collective-permute-start | bytes 786440 | tf_op jit(solution)/shard_map/ppermute | solution.py:311
  7.5 12.2 %collective-permute-start.2 = (bf16[2,64,1024]{2,1,0:T(8,128)(2,1)S(1)}, bf16[2,64,1024]{2,1,0:T(8,128)(2,1)S(1)}, u32[]{:S(2)}, u32[]{:S(2)}) collective-permute-start(bf16[2,64,1024]{2,1,0:T(8,128)(2,1)S(1)} %maximum_select_fusion.refs_8_), channel_id=1, source_target_pairs={{0,64},{1,193},{32,96},{33,225},{64,128},{65,1},{96,160},{97,33},{... | collective-permute-start | bytes 786440 | tf_op jit(solution)/shard_map/ppermute | solution.py:311
  13.6 9.0 %collective-permute-start.1 = (bf16[2,64,1024]{2,1,0:T(8,128)(2,1)S(1)}, bf16[2,64,1024]{2,1,0:T(8,128)(2,1)S(1)}, u32[]{:S(2)}, u32[]{:S(2)}) collective-permute-start(bf16[2,64,1024]{2,1,0:T(8,128)(2,1)S(1)} %maximum_select_fusion.refs_8_), channel_id=1, source_target_pairs={{0,32},{1,225},{32,64},{33,1},{64,96},{65,33},{96,128},{97,65},{12... | collective-permute-start | bytes 786440 | tf_op jit(solution)/shard_map/ppermute | solution.py:311
  14.5 13.6 %collective-permute-start.12 = (bf16[2,2,512,128]{3,2,1,0:T(8,128)(2,1)S(1)}, bf16[2,2,512,128]{3,2,1,0:T(8,128)(2,1)S(1)}, u32[]{:S(2)}, u32[]{:S(2)}) collective-permute-start(bf16[2,2,512,128]{3,2,1,0:T(8,128)(2,1)S(1)} %pad_maximum_fusion.2.refs_1_), channel_id=1, source_target_pairs={{0,6},{1,25},{2,0},{3,27},{4,2},{5,29},{6,4},{7,31},{8,14},{9,1},{... | collective-permute-start | bytes 1572872 | tf_op jit(solution)/shard_map/ppermute | solution.py:311
  17.1 12.2 %collective-permute-start.10 = (bf16[2,2,512,128]{3,2,1,0:T(8,128)(2,1)S(1)}, bf16[2,2,512,128]{3,2,1,0:T(8,128)(2,1)S(1)}, u32[]{:S(2)}, u32[]{:S(2)}) collective-permute-start(bf16[2,2,512,128]{3,2,1,0:T(8,128)(2,1)S(1)} %pad_maximum_fusion.3.refs_0_), channel_id=1, source_target_pairs={{0,2},{1,9},{2,4},{3,11},{4,6},{5,13},{6,0},{7,15},{8,10},{9,17},{... | collective-permute-start | bytes 1572872 | tf_op jit(solution)/shard_map/ppermute | solution.py:311
  22.6 11.6 %collective-permute-start.3 = (bf16[2,2,64,1024]{3,2,1,0:T(8,128)(2,1)S(1)}, bf16[2,2,64,1024]{3,2,1,0:T(8,128)(2,1)S(1)}, u32[]{:S(2)}, u32[]{:S(2)}) collective-permute-start(bf16[2,2,64,1024]{3,2,1,0:T(8,128)(2,1)S(1)} %pad_maximum_fusion.1), channel_id=1, source_target_pairs={{0,64},{1,193},{32,96},{33,225},{64,128},{65,1},{96,160},{97,33},{... | collective-permute-start | bytes 1572872 | tf_op jit(solution)/shard_map/ppermute | solution.py:311
  25.4 9.5 %collective-permute-start.7 = (bf16[2,2,512,128]{3,2,1,0:T(8,128)(2,1)S(1)}, bf16[2,2,512,128]{3,2,1,0:T(8,128)(2,1)S(1)}, u32[]{:S(2)}, u32[]{:S(2)}) collective-permute-start(bf16[2,2,512,128]{3,2,1,0:T(8,128)(2,1)S(1)} %pad_maximum_fusion.2.refs_1_), channel_id=1, source_target_pairs={{0,2},{1,9},{2,4},{3,11},{4,6},{5,13},{6,0},{7,15},{8,10},{9,17},{... | collective-permute-start | bytes 1572872 | tf_op jit(solution)/shard_map/ppermute | solution.py:311
  26.6 8.3 %collective-permute-start.9 = (bf16[2,2,512,128]{3,2,1,0:T(8,128)(2,1)S(1)}, bf16[2,2,512,128]{3,2,1,0:T(8,128)(2,1)S(1)}, u32[]{:S(2)}, u32[]{:S(2)}) collective-permute-start(bf16[2,2,512,128]{3,2,1,0:T(8,128)(2,1)S(1)} %pad_maximum_fusion.3.refs_0_), channel_id=1, source_target_pairs={{0,6},{1,25},{2,0},{3,27},{4,2},{5,29},{6,4},{7,31},{8,14},{9,1},{... | collective-permute-start | bytes 1572872 | tf_op jit(solution)/shard_map/ppermute | solution.py:311
  28.0 12.5 %collective-permute-start.13 = (bf16[2,2,512,128]{3,2,1,0:T(8,128)(2,1)S(1)}, bf16[2,2,512,128]{3,2,1,0:T(8,128)(2,1)S(1)}, u32[]{:S(2)}, u32[]{:S(2)}) collective-permute-start(bf16[2,2,512,128]{3,2,1,0:T(8,128)(2,1)S(1)} %collective-permute-done.12.refs_5_), channel_id=1, source_target_pairs={{0,6},{1,25},{2,0},{3,27},{4,2},{5,29},{6,4},{7,31},{8,14},{9,1},{... | collective-permute-start | bytes 1572872 | tf_op jit(solution)/shard_map/ppermute | solution.py:311
  29.3 11.2 %collective-permute-start.11 = (bf16[2,2,512,128]{3,2,1,0:T(8,128)(2,1)S(1)}, bf16[2,2,512,128]{3,2,1,0:T(8,128)(2,1)S(1)}, u32[]{:S(2)}, u32[]{:S(2)}) collective-permute-start(bf16[2,2,512,128]{3,2,1,0:T(8,128)(2,1)S(1)} %collective-permute-done.10.refs_2_), channel_id=1, source_target_pairs={{0,2},{1,9},{2,4},{3,11},{4,6},{5,13},{6,0},{7,15},{8,10},{9,17},{... | collective-permute-start | bytes 1572872 | tf_op jit(solution)/shard_map/ppermute | solution.py:311
  40.5 6.4 %collective-permute-start.14 = (bf16[3,2,64,1024]{3,2,1,0:T(8,128)(2,1)S(1)}, bf16[3,2,64,1024]{3,2,1,0:T(8,128)(2,1)S(1)}, u32[]{:S(2)}, u32[]{:S(2)}) collective-permute-start(bf16[3,2,64,1024]{3,2,1,0:T(8,128)(2,1)S(1)} %pad_maximum_fusion.refs_10_), channel_id=1, source_target_pairs={{0,1},{1,0},{2,3},{3,2},{4,5},{5,4},{6,7},{7,6},{8,9},{9,8},{10,11... | collective-permute-start | bytes 2359304 | tf_op jit(solution)/shard_map/ppermute | solution.py:311
  46.9 14.9 %copy-start.1 = (f32[64,1024]{1,0:T(8,128)S(1)}, f32[64,1024]{1,0:T(8,128)}, u32[]{:S(2)}) copy-start(f32[64,1024]{1,0:T(8,128)} %n_ref.1) | copy-start | bytes 786436
  119.4 5.7 %collective-permute-start.15 = (f32[520,1024]{1,0:T(8,128)S(1)}, f32[520,1024]{1,0:T(8,128)S(1)}, u32[]{:S(2)}, u32[]{:S(2)}) collective-permute-start(f32[520,1024]{1,0:T(8,128)S(1)} %barycenter_other.1), channel_id=1, source_target_pairs={{0,1},{1,0},{2,3},{3,2},{4,5},{5,4},{6,7},{7,6},{8,9},{9,8},{10,11... | collective-permute-start | bytes 6389768 | tf_op jit(solution)/shard_map/ppermute | solution.py:311

commit v6 on v5

--- a/solution.py
+++ b/solution.py
@@ -330,8 +330,11 @@
     a0 = jnp.where(core == 0, jnp.stack([mine[0], got[0]]), jnp.stack([got[1], mine[1]]))
     a1, a2 = along(True, 1, a0), along(True, -1, a0)
     a3 = along(True, 2, a0)
-    s, t = jnp.stack([a0, a1]), jnp.stack([a2, a3])
-    s1, t2, t1, s2 = along(False, 1, s), along(False, -1, t), along(False, 1, t), along(False, -1, s)
+    s = jnp.stack([a0, a1])
+    s1, s2 = along(False, 1, s), along(False, -1, s)
+    s, a2, a3 = lax.optimization_barrier((s, a2, a3))
+    t = jnp.stack([a2, a3])
+    t1, t2 = along(False, 1, t), along(False, -1, t)
     h1, h2 = along(False, 1, s1), along(False, -1, t2)
 
     got = swap(generated)
@@ -421,11 +424,11 @@
         [lanes, lanes],
         over_rows(lr), t, generated, noise,
     )
-    k, rho, v = call(
+    k, rho = call(
         functools.partial(second_row_kernel, math.log2(np_)),
         "second_rows",
-        [k_shape, row_out, v_shape],
-        [],
+        [k_shape, row_out],
+        [lanes],
         over_columns(lc), r, t, k,
         aliases={3: 0},
     )

time: 159 us -> 157 us (0.987)
  blocking collectives: 90.2 us -> 88.5 us
    all_to_all x3, blocking collectives: 31.9 us -> 30.1 us  [over_rows(): return lax.all_to_all(a, ('x', 'y'), 0, 0, tiled=True)]
  transfers between devices with their start and end apart: 16 -> 16, of which waited for: 7 -> 7; matrix products, arithmetic and copies ran while one was open for 1% -> 1% of each run, Pallas kernels for 4% -> 5%
where the time goes in v6:
time: 157 us
  blocking collectives  88.5 us (56%)
  starting transfers between devices  26.5 us (17%)
  Pallas kernels  21.8 us (14%)
  waiting for transfers between devices  18 us (11%)
    all_to_all x1, blocking collectives, shards(): parts = lax.all_to_all(parts.astype(F16), 'z', 0, 0, tiled=True).astype(F32)  31.9 us
    all_to_all x3, blocking collectives, over_rows(): return lax.all_to_all(a, ('x', 'y'), 0, 0, tiled=True)  30.1 us
    ppermute x16, starting transfers between devices, permuted(): return lax.ppermute(a, axes, pairs)  26.5 us
    all_to_all x2, blocking collectives, over_columns(): return lax.all_to_all(a, ('z', 'core'), 0, 0, tiled=True)  26.4 us
    pallas_call x10, Pallas kernels, call(): pl.pallas_call(body, out_shape=out_shape, scratch_shapes=scratch, compile...  21.8 us
    ppermute x16, waiting for transfers between devices, permuted(): return lax.ppermute(a, axes, pairs)  18 us
  transfers between devices with their start and end apart: 16, of which 7 were waited for; matrix products, arithmetic and copies ran while one was open for 1% of the time, Pallas kernels for 5%

profile of v6, /device:TPU:1, one launch (start us, length us, event | category | flops | bytes accessed | tf_op | source)
XLA Modules:
  0.0 156.7 jit_solution(7784174470260374485)
XLA Ops:
  0.0 3.2 %collective-permute-start.4 = (bf16[1024,128]{1,0:T(8,128)(2,1)}, bf16[1024,128]{1,0:T(8,128)(2,1)S(1)}, u32[]{:S(2)}, u32[]{:S(2)}) collective-permute-start(bf16[1024,128]{1,0:T(8,128)(2,1)} %param.3), channel_id=1, source_target_pairs={{0,1},{1,0},{2,3},{3,2},{4,5},{5,4},{6,7},{7,6},{8,9},{9,8},{10,11... | collective-permute-start | bytes 786440 | tf_op jit(solution)/shard_map/ppermute | solution.py:311
  3.2 0.0 collective-permute-start
  3.2 1.0 slice_bitcast_fusion.6
  4.3 0.3 collective-permute-done.4
  4.6 0.1 slice_bitcast_fusion.2
  4.7 0.1 collective-permute-start.5
  4.8 2.2 %collective-permute-start.7 = (bf16[2,512,128]{2,1,0:T(8,128)(2,1)S(1)}, bf16[2,512,128]{2,1,0:T(8,128)(2,1)S(1)}, u32[]{:S(2)}, u32[]{:S(2)}) collective-permute-start(bf16[2,512,128]{2,1,0:T(8,128)(2,1)S(1)} %maximum_select_fusion.2), channel_id=1, source_target_pairs={{0,16},{1,5},{2,18},{3,7},{4,20},{5,1},{6,22},{7,3},{8,24},{9,13},... | collective-permute-start | bytes 786440 | tf_op jit(solution)/shard_map/ppermute | solution.py:311
  7.0 1.1 collective-permute-start.6
  8.1 0.0 collective-permute-done
  8.1 6.1 %collective-permute-start.2 = (bf16[2,64,1024]{2,1,0:T(8,128)(2,1)S(1)}, bf16[2,64,1024]{2,1,0:T(8,128)(2,1)S(1)}, u32[]{:S(2)}, u32[]{:S(2)}) collective-permute-start(bf16[2,64,1024]{2,1,0:T(8,128)(2,1)S(1)} %maximum_select_fusion.refs_8_), channel_id=1, source_target_pairs={{0,64},{1,193},{32,96},{33,225},{64,128},{65,1},{96,160},{97,33},{... | collective-permute-start | bytes 786440 | tf_op jit(solution)/shard_map/ppermute | solution.py:311
  14.2 0.7 collective-permute-start.1
  15.0 0.1 pad_maximum_fusion.2.refs_0_
  15.1 0.1 pad_maximum_fusion.3.refs_1_
  15.1 2.6 %collective-permute-start.12 = (bf16[2,2,512,128]{3,2,1,0:T(8,128)(2,1)S(1)}, bf16[2,2,512,128]{3,2,1,0:T(8,128)(2,1)S(1)}, u32[]{:S(2)}, u32[]{:S(2)}) collective-permute-start(bf16[2,2,512,128]{3,2,1,0:T(8,128)(2,1)S(1)} %pad_maximum_fusion.3.refs_1_), channel_id=1, source_target_pairs={{0,6},{1,25},{2,0},{3,27},{4,2},{5,29},{6,4},{7,31},{8,14},{9,1},{... | collective-permute-start | bytes 1572872 | tf_op jit(solution)/shard_map/ppermute | solution.py:311
  17.7 2.6 %collective-permute-done.2 = bf16[2,64,1024]{2,1,0:T(8,128)(2,1)S(1)} collective-permute-done((bf16[2,64,1024]{2,1,0:T(8,128)(2,1)S(1)}, bf16[2,64,1024]{2,1,0:T(8,128)(2,1)S(1)}, u32[]{:S(2)}, u32[]{:S(2)}) %collective-permute-start.2) | collective-permute-done | bytes 262176 | tf_op jit(solution)/shard_map/ppermute | solution.py:311
  20.3 2.8 %collective-permute-done.1 = bf16[2,64,1024]{2,1,0:T(8,128)(2,1)S(1)} collective-permute-done((bf16[2,64,1024]{2,1,0:T(8,128)(2,1)S(1)}, bf16[2,64,1024]{2,1,0:T(8,128)(2,1)S(1)}, u32[]{:S(2)}, u32[]{:S(2)}) %collective-permute-start.1) | collective-permute-done | bytes 262176 | tf_op jit(solution)/shard_map/ppermute | solution.py:311
  23.2 0.1 pad_maximum_fusion.1
  23.2 2.7 %collective-permute-start.3 = (bf16[2,2,64,1024]{3,2,1,0:T(8,128)(2,1)S(1)}, bf16[2,2,64,1024]{3,2,1,0:T(8,128)(2,1)S(1)}, u32[]{:S(2)}, u32[]{:S(2)}) collective-permute-start(bf16[2,2,64,1024]{3,2,1,0:T(8,128)(2,1)S(1)} %pad_maximum_fusion.1), channel_id=1, source_target_pairs={{0,64},{1,193},{32,96},{33,225},{64,128},{65,1},{96,160},{97,33},{... | collective-permute-start | bytes 1572872 | tf_op jit(solution)/shard_map/ppermute | solution.py:311
  26.0 1.2 collective-permute-start.8
  27.2 1.5 collective-permute-start.9
  28.6 1.3 collective-permute-start.13
  29.9 0.2 collective-permute-start.11
  30.1 4.7 %collective-permute-done.3 = bf16[2,2,64,1024]{3,2,1,0:T(8,128)(2,1)S(1)} collective-permute-done((bf16[2,2,64,1024]{3,2,1,0:T(8,128)(2,1)S(1)}, bf16[2,2,64,1024]{3,2,1,0:T(8,128)(2,1)S(1)}, u32[]{:S(2)}, u32[]{:S(2)}) %collective-permute-start.3) | collective-permute-done | bytes 524320 | tf_op jit(solution)/shard_map/ppermute | solution.py:311
  34.8 0.1 pad_maximum_fusion.refs_10_
  34.9 0.6 collective-permute-done.8.refs_4_
  35.5 5.6 %collective-permute-done.13.refs_7_ = bf16[2,2,512,128]{3,2,1,0:T(8,128)(2,1)S(1)} collective-permute-done((bf16[2,2,512,128]{3,2,1,0:T(8,128)(2,1)S(1)}, bf16[2,2,512,128]{3,2,1,0:T(8,128)(2,1)S(1)}, u32[]{:S(2)}, u32[]{:S(2)}) %collective-permute-start.13) | collective-permute-done | bytes 524320 | tf_op jit(solution)/shard_map/ppermute | solution.py:311
  41.1 1.8 %collective-permute-start.14 = (bf16[3,2,64,1024]{3,2,1,0:T(8,128)(2,1)S(1)}, bf16[3,2,64,1024]{3,2,1,0:T(8,128)(2,1)S(1)}, u32[]{:S(2)}, u32[]{:S(2)}) collective-permute-start(bf16[3,2,64,1024]{3,2,1,0:T(8,128)(2,1)S(1)} %pad_maximum_fusion.refs_10_), channel_id=1, source_target_pairs={{0,1},{1,0},{2,3},{3,2},{4,5},{5,4},{6,7},{7,6},{8,9},{9,8},{10,11... | collective-permute-start | bytes 2359304 | tf_op jit(solution)/shard_map/ppermute | solution.py:311
  43.0 4.6 %early_scores.1 = (bf16[4,8,512,128]{3,2,1,0:T(8,128)(2,1)S(1)}, f32[16,1024,128]{2,1,0:T(8,128)S(1)}, f32[16,128]{1,0:T(8,128)S(1)}) custom-call(bf16[2,2,512,128]{3,2,1,0:T(8,128)(2,1)S(1)} %pad_maximum_fusion.2.refs_0_, bf16[2,2,512,128]{3,2,1,0:T(8,128)(2,1)S(1)} %pad_maximum_fusion.3.refs_1_, ...), custom_call_target="tpu_custom_call" | custom-call | flops 2684354560 | bytes 25165824 | tf_op jit(solution)/shard_map/early_scores/pallas_call | solution.py:367
  47.5 0.0 copy-start.1
  47.5 2.6 %late_scores.1 = (f32[16,1024,128]{2,1,0:T(8,128)S(1)}, f32[16,16,128]{2,1,0:T(8,128)S(1)}) custom-call(bf16[3,2,64,1024]{3,2,1,0:T(8,128)(2,1)S(1)} %collective-permute-done.14.swapped_ref, bf16[4,8,512,128]{3,2,1,0:T(8,128)(2,1)S(1)} %get-tuple-element.36.p_ref, f32[16,128]{1,0:T(8,128)S(1)} %get-tuple-element.37.early_ref, ...), custom_call_target="tpu_custom_call", output_to_operand_aliasing={{0}: (3, {})} | custom-call | tf_op jit(solution)/shard_map/late_scores/pallas_call | solution.py:367
  50.1 10.5 %all_to_all.30.l_ref = f32[16,16,128]{2,1,0:T(8,128)S(1)} all-to-all(f32[16,16,128]{2,1,0:T(8,128)S(1)} %get-tuple-element.39), channel_id=1, replica_groups=mesh['z'=8,'x'=4,'y'=4,'core'=2] {'x','y'}, dimensions={0} | all-to-all | bytes 262144 | tf_op jit(solution)/shard_map/all_to_all | solution.py:387
  60.7 4.1 %first_columns.1 = (f32[16,128]{1,0:T(8,128)S(1)}, f32[16,1024,128]{2,1,0:T(8,128)S(1)}, f32[16,8,128]{2,1,0:T(8,128)S(1)}, f32[64,1024]{1,0:T(8,128)S(1)}) custom-call(f32[16,16,128]{2,1,0:T(8,128)S(1)} %all_to_all.30.l_ref, f32[16,1024,128]{2,1,0:T(8,128)S(1)} %get-tuple-element.40.t_ref, bf16[64,1024]{1,0:T(8,128)(2,1)S(1)} %copy-done, ...), custom_call_target="tpu_custom_call" | custom-call | tf_op jit(solution)/shard_map/first_columns/pallas_call | solution.py:367
  64.8 14.6 %all_to_all.31.lc_ref = f32[16,8,128]{2,1,0:T(8,128)S(1)} all-to-all(f32[16,8,128]{2,1,0:T(8,128)S(1)} %get-tuple-element.41), channel_id=1, replica_groups=mesh['z'=8,'x'=4,'y'=4,'core'=2] {'z','core'}, dimensions={0} | all-to-all | bytes 131072 | tf_op jit(solution)/shard_map/all_to_all | solution.py:390
  79.4 2.3 %second_rows.1 = (f32[16,1024,128]{2,1,0:T(8,128)S(1)}, f32[16,16,128]{2,1,0:T(8,128)S(1)}) custom-call(f32[16,8,128]{2,1,0:T(8,128)S(1)} %all_to_all.31.lc_ref, f32[16,128]{1,0:T(8,128)S(1)} %get-tuple-element.42.r_ref, f32[16,1024,128]{2,1,0:T(8,128)S(1)} %get-tuple-element.40.t_ref, ...), custom_call_target="tpu_custom_call", output_to_operand_aliasing={{0}: (3, {})} | custom-call | tf_op jit(solution)/shard_map/second_rows/pallas_call | solution.py:367
  81.7 9.7 %all_to_all.32.rho_ref = f32[16,16,128]{2,1,0:T(8,128)S(1)} all-to-all(f32[16,16,128]{2,1,0:T(8,128)S(1)} %get-tuple-element.44), channel_id=1, replica_groups=mesh['z'=8,'x'=4,'y'=4,'core'=2] {'x','y'}, dimensions={0} | all-to-all | bytes 262144 | tf_op jit(solution)/shard_map/all_to_all | solution.py:387
  91.5 0.9 column_sums.1
  92.4 11.8 %all_to_all.33.sums_ref = f32[16,8,128]{2,1,0:T(8,128)S(1)} all-to-all(f32[16,8,128]{2,1,0:T(8,128)S(1)} %column_sums.1), channel_id=1, replica_groups=mesh['z'=8,'x'=4,'y'=4,'core'=2] {'z','core'}, dimensions={0} | all-to-all | bytes 131072 | tf_op jit(solution)/shard_map/all_to_all | solution.py:390
  104.2 1.0 row_sums.1
  105.2 9.9 %all_to_all.34.rho_ref = f32[16,16,128]{2,1,0:T(8,128)S(1)} all-to-all(f32[16,16,128]{2,1,0:T(8,128)S(1)} %get-tuple-element.46), channel_id=1, replica_groups=mesh['z'=8,'x'=4,'y'=4,'core'=2] {'x','y'}, dimensions={0} | all-to-all | bytes 262144 | tf_op jit(solution)/shard_map/all_to_all | solution.py:387
  115.0 2.5 %barycenter_other.1 = f32[520,1024]{1,0:T(8,128)S(1)} custom-call(f32[16,16,128]{2,1,0:T(8,128)S(1)} %all_to_all.34.rho_ref, f32[1024,128]{1,0:T(8,128)S(1)} %get-tuple-element.47.v_ref, f32[16,1024,128]{2,1,0:T(8,128)S(1)} %get-tuple-element.45.k_ref, bf16[4,8,512,128]{3,2,1,0:T(8,128)(2,1)S(1)} %get-tuple-element.36.p_ref), custom_call_target="tpu_custom_call" | custom-call | flops 2147483648 | bytes 16777216 | tf_op jit(solution)/shard_map/barycenter_other/pallas_call | solution.py:367
  117.5 1.8 %collective-permute-start.15 = (f32[520,1024]{1,0:T(8,128)S(1)}, f32[520,1024]{1,0:T(8,128)S(1)}, u32[]{:S(2)}, u32[]{:S(2)}) collective-permute-start(f32[520,1024]{1,0:T(8,128)S(1)} %barycenter_other.1), channel_id=1, source_target_pairs={{0,1},{1,0},{2,3},{3,2},{4,5},{5,4},{6,7},{7,6},{8,9},{9,8},{10,11... | collective-permute-start | bytes 6389768 | tf_op jit(solution)/shard_map/ppermute | solution.py:311
  119.4 2.5 %barycenter_own.1.a_ref = f32[520,1024]{1,0:T(8,128)S(1)} custom-call(f32[16,16,128]{2,1,0:T(8,128)S(1)} %all_to_all.34.rho_ref, f32[1024,128]{1,0:T(8,128)S(1)} %get-tuple-element.47.v_ref, f32[16,1024,128]{2,1,0:T(8,128)S(1)} %get-tuple-element.45.k_ref, bf16[4,8,512,128]{3,2,1,0:T(8,128)(2,1)S(1)} %get-tuple-element.36.p_ref), custom_call_target="tpu_custom_call" | custom-call | flops 2147483648 | bytes 16777216 | tf_op jit(solution)/shard_map/barycenter_own/pallas_call | solution.py:367
  121.9 1.3 collective-permute-done.15.b_ref
  123.2 0.3 means.1
  123.6 0.1 convert_element_type.6
  123.7 31.9 %all_to_all.35 = f16[8,528,128]{2,1,0:T(8,128)(2,1)S(1)} all-to-all(f16[8,528,128]{2,1,0:T(8,128)(2,1)S(1)} %convert_element_type.6), channel_id=1, replica_groups=mesh['z'=8,'x'=4,'y'=4,'core'=2] {'z'}, dimensions={0} | all-to-all | bytes 2162688 | tf_op jit(solution)/shard_map/all_to_all | solution.py:468
  155.6 0.1 convert_element_type.7.parts_ref
  155.8 1.0 update.1
  (16 shorter events, 0.2 us)
Async XLA Ops:
  0.0 8.1 %copy-start = (bf16[64,1024]{1,0:T(8,128)(2,1)S(1)}, bf16[64,1024]{1,0:T(8,128)(2,1)}, u32[]{:S(2)}) copy-start(bf16[64,1024]{1,0:T(8,128)(2,1)} %g_ref.1) | copy-start | bytes 393220
  0.0 4.6 %collective-permute-start.4 = (bf16[1024,128]{1,0:T(8,128)(2,1)}, bf16[1024,128]{1,0:T(8,128)(2,1)S(1)}, u32[]{:S(2)}, u32[]{:S(2)}) collective-permute-start(bf16[1024,128]{1,0:T(8,128)(2,1)} %param.3), channel_id=1, source_target_pairs={{0,1},{1,0},{2,3},{3,2},{4,5},{5,4},{6,7},{7,6},{8,9},{9,8},{10,11... | collective-permute-start | bytes 786440 | tf_op jit(solution)/shard_map/ppermute | solution.py:311
  3.2 4.8 %collective-permute-start = (bf16[64,1024]{1,0:T(8,128)(2,1)}, bf16[64,1024]{1,0:T(8,128)(2,1)S(1)}, u32[]{:S(2)}, u32[]{:S(2)}) collective-permute-start(bf16[64,1024]{1,0:T(8,128)(2,1)} %g_ref.1), channel_id=1, source_target_pairs={{0,1},{1,0},{2,3},{3,2},{4,5},{5,4},{6,7},{7,6},{8,9},{9,8},{10,11... | collective-permute-start | bytes 393224 | tf_op jit(solution)/shard_map/ppermute | solution.py:311
  4.7 10.2 %collective-permute-start.5 = (bf16[2,512,128]{2,1,0:T(8,128)(2,1)S(1)}, bf16[2,512,128]{2,1,0:T(8,128)(2,1)S(1)}, u32[]{:S(2)}, u32[]{:S(2)}) collective-permute-start(bf16[2,512,128]{2,1,0:T(8,128)(2,1)S(1)} %maximum_select_fusion.2), channel_id=1, source_target_pairs={{0,8},{1,3},{2,10},{3,5},{4,12},{5,7},{6,14},{7,1},{8,16},{9,11},{... | collective-permute-start | bytes 786440 | tf_op jit(solution)/shard_map/ppermute | solution.py:311
  4.8 10.2 %collective-permute-start.7 = (bf16[2,512,128]{2,1,0:T(8,128)(2,1)S(1)}, bf16[2,512,128]{2,1,0:T(8,128)(2,1)S(1)}, u32[]{:S(2)}, u32[]{:S(2)}) collective-permute-start(bf16[2,512,128]{2,1,0:T(8,128)(2,1)S(1)} %maximum_select_fusion.2), channel_id=1, source_target_pairs={{0,16},{1,5},{2,18},{3,7},{4,20},{5,1},{6,22},{7,3},{8,24},{9,13},... | collective-permute-start | bytes 786440 | tf_op jit(solution)/shard_map/ppermute | solution.py:311
  7.0 8.1 %collective-permute-start.6 = (bf16[2,512,128]{2,1,0:T(8,128)(2,1)S(1)}, bf16[2,512,128]{2,1,0:T(8,128)(2,1)S(1)}, u32[]{:S(2)}, u32[]{:S(2)}) collective-permute-start(bf16[2,512,128]{2,1,0:T(8,128)(2,1)S(1)} %maximum_select_fusion.2), channel_id=1, source_target_pairs={{0,24},{1,7},{2,26},{3,1},{4,28},{5,3},{6,30},{7,5},{8,0},{9,15},{... | collective-permute-start | bytes 786440 | tf_op jit(solution)/shard_map/ppermute | solution.py:311
  8.1 12.2 %collective-permute-start.2 = (bf16[2,64,1024]{2,1,0:T(8,128)(2,1)S(1)}, bf16[2,64,1024]{2,1,0:T(8,128)(2,1)S(1)}, u32[]{:S(2)}, u32[]{:S(2)}) collective-permute-start(bf16[2,64,1024]{2,1,0:T(8,128)(2,1)S(1)} %maximum_select_fusion.refs_8_), channel_id=1, source_target_pairs={{0,64},{1,193},{32,96},{33,225},{64,128},{65,1},{96,160},{97,33},{... | collective-permute-start | bytes 786440 | tf_op jit(solution)/shard_map/ppermute | solution.py:311
  14.2 9.0 %collective-permute-start.1 = (bf16[2,64,1024]{2,1,0:T(8,128)(2,1)S(1)}, bf16[2,64,1024]{2,1,0:T(8,128)(2,1)S(1)}, u32[]{:S(2)}, u32[]{:S(2)}) collective-permute-start(bf16[2,64,1024]{2,1,0:T(8,128)(2,1)S(1)} %maximum_select_fusion.refs_8_), channel_id=1, source_target_pairs={{0,32},{1,225},{32,64},{33,1},{64,96},{65,33},{96,128},{97,65},{12... | collective-permute-start | bytes 786440 | tf_op jit(solution)/shard_map/ppermute | solution.py:311
  15.1 13.5 %collective-permute-start.12 = (bf16[2,2,512,128]{3,2,1,0:T(8,128)(2,1)S(1)}, bf16[2,2,512,128]{3,2,1,0:T(8,128)(2,1)S(1)}, u32[]{:S(2)}, u32[]{:S(2)}) collective-permute-start(bf16[2,2,512,128]{3,2,1,0:T(8,128)(2,1)S(1)} %pad_maximum_fusion.3.refs_1_), channel_id=1, source_target_pairs={{0,6},{1,25},{2,0},{3,27},{4,2},{5,29},{6,4},{7,31},{8,14},{9,1},{... | collective-permute-start | bytes 1572872 | tf_op jit(solution)/shard_map/ppermute | solution.py:311
  17.7 12.2 %collective-permute-start.10 = (bf16[2,2,512,128]{3,2,1,0:T(8,128)(2,1)S(1)}, bf16[2,2,512,128]{3,2,1,0:T(8,128)(2,1)S(1)}, u32[]{:S(2)}, u32[]{:S(2)}) collective-permute-start(bf16[2,2,512,128]{3,2,1,0:T(8,128)(2,1)S(1)} %pad_maximum_fusion.2.refs_0_), channel_id=1, source_target_pairs={{0,2},{1,9},{2,4},{3,11},{4,6},{5,13},{6,0},{7,15},{8,10},{9,17},{... | collective-permute-start | bytes 1572872 | tf_op jit(solution)/shard_map/ppermute | solution.py:311
  23.2 11.6 %collective-permute-start.3 = (bf16[2,2,64,1024]{3,2,1,0:T(8,128)(2,1)S(1)}, bf16[2,2,64,1024]{3,2,1,0:T(8,128)(2,1)S(1)}, u32[]{:S(2)}, u32[]{:S(2)}) collective-permute-start(bf16[2,2,64,1024]{3,2,1,0:T(8,128)(2,1)S(1)} %pad_maximum_fusion.1), channel_id=1, source_target_pairs={{0,64},{1,193},{32,96},{33,225},{64,128},{65,1},{96,160},{97,33},{... | collective-permute-start | bytes 1572872 | tf_op jit(solution)/shard_map/ppermute | solution.py:311
  26.0 9.5 %collective-permute-start.8 = (bf16[2,2,512,128]{3,2,1,0:T(8,128)(2,1)S(1)}, bf16[2,2,512,128]{3,2,1,0:T(8,128)(2,1)S(1)}, u32[]{:S(2)}, u32[]{:S(2)}) collective-permute-start(bf16[2,2,512,128]{3,2,1,0:T(8,128)(2,1)S(1)} %pad_maximum_fusion.3.refs_1_), channel_id=1, source_target_pairs={{0,2},{1,9},{2,4},{3,11},{4,6},{5,13},{6,0},{7,15},{8,10},{9,17},{... | collective-permute-start | bytes 1572872 | tf_op jit(solution)/shard_map/ppermute | solution.py:311
  27.2 8.3 %collective-permute-start.9 = (bf16[2,2,512,128]{3,2,1,0:T(8,128)(2,1)S(1)}, bf16[2,2,512,128]{3,2,1,0:T(8,128)(2,1)S(1)}, u32[]{:S(2)}, u32[]{:S(2)}) collective-permute-start(bf16[2,2,512,128]{3,2,1,0:T(8,128)(2,1)S(1)} %pad_maximum_fusion.2.refs_0_), channel_id=1, source_target_pairs={{0,6},{1,25},{2,0},{3,27},{4,2},{5,29},{6,4},{7,31},{8,14},{9,1},{... | collective-permute-start | bytes 1572872 | tf_op jit(solution)/shard_map/ppermute | solution.py:311
  28.6 12.5 %collective-permute-start.13 = (bf16[2,2,512,128]{3,2,1,0:T(8,128)(2,1)S(1)}, bf16[2,2,512,128]{3,2,1,0:T(8,128)(2,1)S(1)}, u32[]{:S(2)}, u32[]{:S(2)}) collective-permute-start(bf16[2,2,512,128]{3,2,1,0:T(8,128)(2,1)S(1)} %collective-permute-done.12.refs_5_), channel_id=1, source_target_pairs={{0,6},{1,25},{2,0},{3,27},{4,2},{5,29},{6,4},{7,31},{8,14},{9,1},{... | collective-permute-start | bytes 1572872 | tf_op jit(solution)/shard_map/ppermute | solution.py:311
  29.9 11.2 %collective-permute-start.11 = (bf16[2,2,512,128]{3,2,1,0:T(8,128)(2,1)S(1)}, bf16[2,2,512,128]{3,2,1,0:T(8,128)(2,1)S(1)}, u32[]{:S(2)}, u32[]{:S(2)}) collective-permute-start(bf16[2,2,512,128]{3,2,1,0:T(8,128)(2,1)S(1)} %collective-permute-done.10.refs_2_), channel_id=1, source_target_pairs={{0,2},{1,9},{2,4},{3,11},{4,6},{5,13},{6,0},{7,15},{8,10},{9,17},{... | collective-permute-start | bytes 1572872 | tf_op jit(solution)/shard_map/ppermute | solution.py:311
  41.1 6.4 %collective-permute-start.14 = (bf16[3,2,64,1024]{3,2,1,0:T(8,128)(2,1)S(1)}, bf16[3,2,64,1024]{3,2,1,0:T(8,128)(2,1)S(1)}, u32[]{:S(2)}, u32[]{:S(2)}) collective-permute-start(bf16[3,2,64,1024]{3,2,1,0:T(8,128)(2,1)S(1)} %pad_maximum_fusion.refs_10_), channel_id=1, source_target_pairs={{0,1},{1,0},{2,3},{3,2},{4,5},{5,4},{6,7},{7,6},{8,9},{9,8},{10,11... | collective-permute-start | bytes 2359304 | tf_op jit(solution)/shard_map/ppermute | solution.py:311
  47.5 13.1 %copy-start.1 = (f32[64,1024]{1,0:T(8,128)S(1)}, f32[64,1024]{1,0:T(8,128)}, u32[]{:S(2)}) copy-start(f32[64,1024]{1,0:T(8,128)} %n_ref.1) | copy-start | bytes 786436
  117.5 5.7 %collective-permute-start.15 = (f32[520,1024]{1,0:T(8,128)S(1)}, f32[520,1024]{1,0:T(8,128)S(1)}, u32[]{:S(2)}, u32[]{:S(2)}) collective-permute-start(f32[520,1024]{1,0:T(8,128)S(1)} %barycenter_other.1), channel_id=1, source_target_pairs={{0,1},{1,0},{2,3},{3,2},{4,5},{5,4},{6,7},{7,6},{8,9},{9,8},{10,11... | collective-permute-start | bytes 6389768 | tf_op jit(solution)/shard_map/ppermute | solution.py:311

commit v7 on v6

--- a/solution.py
+++ b/solution.py
@@ -228,6 +228,11 @@
     scaled_row_sums(k_ref, v_ref, rho_ref)
 
 
+def two_parts(log_mass):
+    high = jnp.round(log_mass * 16.0) * 0.0625
+    return high, log_mass - high
+
+
 def barycenter_kernel(ng, other, rho_ref, v_ref, k_ref, p_ref, out_ref, mass_ref, w_ref):
     tiles = k_ref.shape[0]
     cols = mass_ref.shape[0]
@@ -255,11 +260,17 @@
                 total = total + w
                 w_ref[at, n * LANES:(n + 1) * LANES] = w.astype(BF16)
             mass_ref[at, :] = total
-        out_ref[first:first + part, :] = jnp.dot(
-            w_ref[first:first + part, :], p, preferred_element_type=F32
-        )
+        sums = jnp.dot(w_ref[first:first + part, :], p, preferred_element_type=F32)
+        if other:
+            weight = jnp.sum(mass_ref[first:first + part, :], axis=1, keepdims=True)
+            sums = sums * (1.0 / jnp.maximum(weight, 1e-30))
+        out_ref[first:first + part, :] = sums
     mass = jnp.sum(jnp.transpose(mass_ref[...]), axis=0, keepdims=True)
-    out_ref[cols:, 0:cols] = jnp.broadcast_to(mass, (out_ref.shape[0] - cols, cols))
+    if other:
+        high, low = two_parts(jnp.log2(jnp.maximum(mass, 1e-30)))
+        mass = jnp.concatenate([high] * 4 + [low] * 4, axis=0)
+    mass = jnp.broadcast_to(mass, (out_ref.shape[0] - cols, cols))
+    out_ref[cols:, :] = jnp.concatenate([mass] * (out_ref.shape[1] // cols), axis=1)
 
 
 def mean_kernel(a_ref, b_ref, out_ref):
@@ -268,17 +279,19 @@
     blocks = features // LANES
     rows = (out_ref.shape[1] - 16) // blocks
     cols = owners * rows
-    mass = jnp.maximum(a_ref[cols:cols + 1, 0:cols] + b_ref[cols:cols + 1, 0:cols], 1e-30)
+    other = jnp.exp2(b_ref[cols:cols + 1, 0:cols] + b_ref[cols + 4:cols + 5, 0:cols])
+    mass = jnp.maximum(a_ref[cols:cols + 1, 0:cols] + other, 1e-30)
     log_mass = jnp.log2(mass)
     inverse = jnp.transpose(jnp.broadcast_to(1.0 / mass, (LANES, cols)))
+    share = jnp.transpose(jnp.broadcast_to(other / mass, (LANES, cols)))
     for z in range(owners):
         at = slice(z * rows, (z + 1) * rows)
         for q in range(blocks):
             lanes = slice(q * LANES, (q + 1) * LANES)
-            out_ref[z, q * rows:(q + 1) * rows, :] = (a_ref[at, lanes] + b_ref[at, lanes]) * inverse[at, :]
-        part = jnp.concatenate([log_mass[:, at]] * (LANES // rows), axis=1)
-        high = jnp.round(part * 16.0) * 0.0625
-        low = part - high
+            out_ref[z, q * rows:(q + 1) * rows, :] = (
+                a_ref[at, lanes] * inverse[at, :] + b_ref[at, lanes] * share[at, :]
+            )
+        high, low = two_parts(jnp.concatenate([log_mass[:, at]] * (LANES // rows), axis=1))
         out_ref[z, blocks * rows:, :] = jnp.concatenate([high] * 8 + [low] * 8, axis=0)
 
 
@@ -460,7 +473,7 @@
             ),
         )
 
-    theirs = swap(barycenter(True))
+    theirs = swap(barycenter(True).astype(F16)).astype(F32)
     mine = barycenter(False)
     parts = call(
         mean_kernel, "means", f32(nz, own * (features // LANES) + 16, LANES), [], mine, theirs

time: 157 us -> 156 us (level)
  transfers between devices with their start and end apart: 16 -> 16, of which waited for: 7 -> 6; matrix products, arithmetic and copies ran while one was open for 1% -> 1% of each run, Pallas kernels for 5% -> 5%
where the time goes in v7:
time: 156 us
  blocking collectives  88.5 us (57%)
  starting transfers between devices  26.5 us (17%)
  Pallas kernels  22 us (14%)
  waiting for transfers between devices  16.7 us (11%)
    all_to_all x1, blocking collectives, shards(): parts = lax.all_to_all(parts.astype(F16), 'z', 0, 0, tiled=True).astype(F32)  31.9 us
    all_to_all x3, blocking collectives, over_rows(): return lax.all_to_all(a, ('x', 'y'), 0, 0, tiled=True)  30.1 us
    ppermute x16, starting transfers between devices, permuted(): return lax.ppermute(a, axes, pairs)  26.5 us
    all_to_all x2, blocking collectives, over_columns(): return lax.all_to_all(a, ('z', 'core'), 0, 0, tiled=True)  26.4 us
    pallas_call x10, Pallas kernels, call(): pl.pallas_call(body, out_shape=out_shape, scratch_shapes=scratch, compile...  22 us
    ppermute x16, waiting for transfers between devices, permuted(): return lax.ppermute(a, axes, pairs)  16.7 us
  transfers between devices with their start and end apart: 16, of which 6 were waited for; matrix products, arithmetic and copies ran while one was open for 1% of the time, Pallas kernels for 5%

profile of v7, /device:TPU:1, one launch (start us, length us, event | category | flops | bytes accessed | tf_op | source)
XLA Modules:
  0.0 156.1 jit_solution(11025003380427479790)
XLA Ops:
  0.0 3.2 %collective-permute-start.4 = (bf16[1024,128]{1,0:T(8,128)(2,1)}, bf16[1024,128]{1,0:T(8,128)(2,1)S(1)}, u32[]{:S(2)}, u32[]{:S(2)}) collective-permute-start(bf16[1024,128]{1,0:T(8,128)(2,1)} %param.3), channel_id=1, source_target_pairs={{0,1},{1,0},{2,3},{3,2},{4,5},{5,4},{6,7},{7,6},{8,9},{9,8},{10,11... | collective-permute-start | bytes 786440 | tf_op jit(solution)/shard_map/ppermute | solution.py:324
  3.2 0.0 collective-permute-start
  3.2 1.0 slice_bitcast_fusion.6
  4.3 0.3 collective-permute-done.4
  4.6 0.1 slice_bitcast_fusion.2
  4.7 0.1 collective-permute-start.5
  4.8 2.2 %collective-permute-start.7 = (bf16[2,512,128]{2,1,0:T(8,128)(2,1)S(1)}, bf16[2,512,128]{2,1,0:T(8,128)(2,1)S(1)}, u32[]{:S(2)}, u32[]{:S(2)}) collective-permute-start(bf16[2,512,128]{2,1,0:T(8,128)(2,1)S(1)} %maximum_select_fusion.2), channel_id=1, source_target_pairs={{0,16},{1,5},{2,18},{3,7},{4,20},{5,1},{6,22},{7,3},{8,24},{9,13},... | collective-permute-start | bytes 786440 | tf_op jit(solution)/shard_map/ppermute | solution.py:324
  7.0 1.1 collective-permute-start.6
  8.1 6.1 %collective-permute-start.2 = (bf16[2,64,1024]{2,1,0:T(8,128)(2,1)S(1)}, bf16[2,64,1024]{2,1,0:T(8,128)(2,1)S(1)}, u32[]{:S(2)}, u32[]{:S(2)}) collective-permute-start(bf16[2,64,1024]{2,1,0:T(8,128)(2,1)S(1)} %maximum_select_fusion.refs_8_), channel_id=1, source_target_pairs={{0,64},{1,193},{32,96},{33,225},{64,128},{65,1},{96,160},{97,33},{... | collective-permute-start | bytes 786440 | tf_op jit(solution)/shard_map/ppermute | solution.py:324
  14.2 0.7 collective-permute-start.1
  15.0 0.1 pad_maximum_fusion.2.refs_0_
  15.1 0.1 pad_maximum_fusion.3.refs_1_
  15.1 2.6 %collective-permute-start.12 = (bf16[2,2,512,128]{3,2,1,0:T(8,128)(2,1)S(1)}, bf16[2,2,512,128]{3,2,1,0:T(8,128)(2,1)S(1)}, u32[]{:S(2)}, u32[]{:S(2)}) collective-permute-start(bf16[2,2,512,128]{3,2,1,0:T(8,128)(2,1)S(1)} %pad_maximum_fusion.3.refs_1_), channel_id=1, source_target_pairs={{0,6},{1,25},{2,0},{3,27},{4,2},{5,29},{6,4},{7,31},{8,14},{9,1},{... | collective-permute-start | bytes 1572872 | tf_op jit(solution)/shard_map/ppermute | solution.py:324
  17.7 2.6 %collective-permute-done.2 = bf16[2,64,1024]{2,1,0:T(8,128)(2,1)S(1)} collective-permute-done((bf16[2,64,1024]{2,1,0:T(8,128)(2,1)S(1)}, bf16[2,64,1024]{2,1,0:T(8,128)(2,1)S(1)}, u32[]{:S(2)}, u32[]{:S(2)}) %collective-permute-start.2) | collective-permute-done | bytes 262176 | tf_op jit(solution)/shard_map/ppermute | solution.py:324
  20.3 2.8 %collective-permute-done.1 = bf16[2,64,1024]{2,1,0:T(8,128)(2,1)S(1)} collective-permute-done((bf16[2,64,1024]{2,1,0:T(8,128)(2,1)S(1)}, bf16[2,64,1024]{2,1,0:T(8,128)(2,1)S(1)}, u32[]{:S(2)}, u32[]{:S(2)}) %collective-permute-start.1) | collective-permute-done | bytes 262176 | tf_op jit(solution)/shard_map/ppermute | solution.py:324
  23.2 0.1 pad_maximum_fusion.1
  23.2 2.7 %collective-permute-start.3 = (bf16[2,2,64,1024]{3,2,1,0:T(8,128)(2,1)S(1)}, bf16[2,2,64,1024]{3,2,1,0:T(8,128)(2,1)S(1)}, u32[]{:S(2)}, u32[]{:S(2)}) collective-permute-start(bf16[2,2,64,1024]{3,2,1,0:T(8,128)(2,1)S(1)} %pad_maximum_fusion.1), channel_id=1, source_target_pairs={{0,64},{1,193},{32,96},{33,225},{64,128},{65,1},{96,160},{97,33},{... | collective-permute-start | bytes 1572872 | tf_op jit(solution)/shard_map/ppermute | solution.py:324
  26.0 1.2 collective-permute-start.8
  27.2 1.5 collective-permute-start.9
  28.6 1.3 collective-permute-start.13
  29.9 0.2 collective-permute-start.11
  30.1 4.7 %collective-permute-done.3 = bf16[2,2,64,1024]{3,2,1,0:T(8,128)(2,1)S(1)} collective-permute-done((bf16[2,2,64,1024]{3,2,1,0:T(8,128)(2,1)S(1)}, bf16[2,2,64,1024]{3,2,1,0:T(8,128)(2,1)S(1)}, u32[]{:S(2)}, u32[]{:S(2)}) %collective-permute-start.3) | collective-permute-done | bytes 524320 | tf_op jit(solution)/shard_map/ppermute | solution.py:324
  34.8 0.1 pad_maximum_fusion.refs_10_
  34.9 0.6 collective-permute-done.8.refs_4_
  35.5 5.6 %collective-permute-done.13.refs_7_ = bf16[2,2,512,128]{3,2,1,0:T(8,128)(2,1)S(1)} collective-permute-done((bf16[2,2,512,128]{3,2,1,0:T(8,128)(2,1)S(1)}, bf16[2,2,512,128]{3,2,1,0:T(8,128)(2,1)S(1)}, u32[]{:S(2)}, u32[]{:S(2)}) %collective-permute-start.13) | collective-permute-done | bytes 524320 | tf_op jit(solution)/shard_map/ppermute | solution.py:324
  41.1 1.8 %collective-permute-start.14 = (bf16[3,2,64,1024]{3,2,1,0:T(8,128)(2,1)S(1)}, bf16[3,2,64,1024]{3,2,1,0:T(8,128)(2,1)S(1)}, u32[]{:S(2)}, u32[]{:S(2)}) collective-permute-start(bf16[3,2,64,1024]{3,2,1,0:T(8,128)(2,1)S(1)} %pad_maximum_fusion.refs_10_), channel_id=1, source_target_pairs={{0,1},{1,0},{2,3},{3,2},{4,5},{5,4},{6,7},{7,6},{8,9},{9,8},{10,11... | collective-permute-start | bytes 2359304 | tf_op jit(solution)/shard_map/ppermute | solution.py:324
  43.0 4.6 %early_scores.1 = (bf16[4,8,512,128]{3,2,1,0:T(8,128)(2,1)S(1)}, f32[16,1024,128]{2,1,0:T(8,128)S(1)}, f32[16,128]{1,0:T(8,128)S(1)}) custom-call(bf16[2,2,512,128]{3,2,1,0:T(8,128)(2,1)S(1)} %pad_maximum_fusion.2.refs_0_, bf16[2,2,512,128]{3,2,1,0:T(8,128)(2,1)S(1)} %pad_maximum_fusion.3.refs_1_, ...), custom_call_target="tpu_custom_call" | custom-call | flops 2684354560 | bytes 25165824 | tf_op jit(solution)/shard_map/early_scores/pallas_call | solution.py:380
  47.5 0.0 copy-start.1
  47.5 2.6 %late_scores.1 = (f32[16,1024,128]{2,1,0:T(8,128)S(1)}, f32[16,16,128]{2,1,0:T(8,128)S(1)}) custom-call(bf16[3,2,64,1024]{3,2,1,0:T(8,128)(2,1)S(1)} %collective-permute-done.14.swapped_ref, bf16[4,8,512,128]{3,2,1,0:T(8,128)(2,1)S(1)} %get-tuple-element.36.p_ref, f32[16,128]{1,0:T(8,128)S(1)} %get-tuple-element.37.early_ref, ...), custom_call_target="tpu_custom_call", output_to_operand_aliasing={{0}: (3, {})} | custom-call | tf_op jit(solution)/shard_map/late_scores/pallas_call | solution.py:380
  50.1 10.5 %all_to_all.30.l_ref = f32[16,16,128]{2,1,0:T(8,128)S(1)} all-to-all(f32[16,16,128]{2,1,0:T(8,128)S(1)} %get-tuple-element.39), channel_id=1, replica_groups=mesh['z'=8,'x'=4,'y'=4,'core'=2] {'x','y'}, dimensions={0} | all-to-all | bytes 262144 | tf_op jit(solution)/shard_map/all_to_all | solution.py:400
  60.7 4.1 %first_columns.1 = (f32[16,128]{1,0:T(8,128)S(1)}, f32[16,1024,128]{2,1,0:T(8,128)S(1)}, f32[16,8,128]{2,1,0:T(8,128)S(1)}, f32[64,1024]{1,0:T(8,128)S(1)}) custom-call(f32[16,16,128]{2,1,0:T(8,128)S(1)} %all_to_all.30.l_ref, f32[16,1024,128]{2,1,0:T(8,128)S(1)} %get-tuple-element.40.t_ref, bf16[64,1024]{1,0:T(8,128)(2,1)S(1)} %copy-done, ...), custom_call_target="tpu_custom_call" | custom-call | tf_op jit(solution)/shard_map/first_columns/pallas_call | solution.py:380
  64.8 14.6 %all_to_all.31.lc_ref = f32[16,8,128]{2,1,0:T(8,128)S(1)} all-to-all(f32[16,8,128]{2,1,0:T(8,128)S(1)} %get-tuple-element.41), channel_id=1, replica_groups=mesh['z'=8,'x'=4,'y'=4,'core'=2] {'z','core'}, dimensions={0} | all-to-all | bytes 131072 | tf_op jit(solution)/shard_map/all_to_all | solution.py:403
  79.4 2.3 %second_rows.1 = (f32[16,1024,128]{2,1,0:T(8,128)S(1)}, f32[16,16,128]{2,1,0:T(8,128)S(1)}) custom-call(f32[16,8,128]{2,1,0:T(8,128)S(1)} %all_to_all.31.lc_ref, f32[16,128]{1,0:T(8,128)S(1)} %get-tuple-element.42.r_ref, f32[16,1024,128]{2,1,0:T(8,128)S(1)} %get-tuple-element.40.t_ref, ...), custom_call_target="tpu_custom_call", output_to_operand_aliasing={{0}: (3, {})} | custom-call | tf_op jit(solution)/shard_map/second_rows/pallas_call | solution.py:380
  81.7 9.7 %all_to_all.32.rho_ref = f32[16,16,128]{2,1,0:T(8,128)S(1)} all-to-all(f32[16,16,128]{2,1,0:T(8,128)S(1)} %get-tuple-element.44), channel_id=1, replica_groups=mesh['z'=8,'x'=4,'y'=4,'core'=2] {'x','y'}, dimensions={0} | all-to-all | bytes 262144 | tf_op jit(solution)/shard_map/all_to_all | solution.py:400
  91.5 0.9 column_sums.1
  92.4 11.8 %all_to_all.33.sums_ref = f32[16,8,128]{2,1,0:T(8,128)S(1)} all-to-all(f32[16,8,128]{2,1,0:T(8,128)S(1)} %column_sums.1), channel_id=1, replica_groups=mesh['z'=8,'x'=4,'y'=4,'core'=2] {'z','core'}, dimensions={0} | all-to-all | bytes 131072 | tf_op jit(solution)/shard_map/all_to_all | solution.py:403
  104.2 1.0 row_sums.1
  105.2 9.9 %all_to_all.34.rho_ref = f32[16,16,128]{2,1,0:T(8,128)S(1)} all-to-all(f32[16,16,128]{2,1,0:T(8,128)S(1)} %get-tuple-element.46), channel_id=1, replica_groups=mesh['z'=8,'x'=4,'y'=4,'core'=2] {'x','y'}, dimensions={0} | all-to-all | bytes 262144 | tf_op jit(solution)/shard_map/all_to_all | solution.py:400
  115.0 2.6 %barycenter_other.1 = f32[520,1024]{1,0:T(8,128)S(1)} custom-call(f32[16,16,128]{2,1,0:T(8,128)S(1)} %all_to_all.34.rho_ref, f32[1024,128]{1,0:T(8,128)S(1)} %get-tuple-element.47.v_ref, f32[16,1024,128]{2,1,0:T(8,128)S(1)} %get-tuple-element.45.k_ref, bf16[4,8,512,128]{3,2,1,0:T(8,128)(2,1)S(1)} %get-tuple-element.36.p_ref), custom_call_target="tpu_custom_call" | custom-call | flops 2147483648 | bytes 16777216 | tf_op jit(solution)/shard_map/barycenter_other/pallas_call | solution.py:380
  117.6 0.2 convert_element_type.12
  117.8 1.8 %collective-permute-start.15 = (f16[520,1024]{1,0:T(8,128)(2,1)S(1)}, f16[520,1024]{1,0:T(8,128)(2,1)S(1)}, u32[]{:S(2)}, u32[]{:S(2)}) collective-permute-start(f16[520,1024]{1,0:T(8,128)(2,1)S(1)} %convert_element_type.12), channel_id=1, source_target_pairs={{0,1},{1,0},{2,3},{3,2},{4,5},{5,4},{6,7},{7,6},{8,9},{9,8},{10,11... | collective-permute-start | bytes 3194888 | tf_op jit(solution)/shard_map/ppermute | solution.py:324
  119.7 2.5 %barycenter_own.1.a_ref = f32[520,1024]{1,0:T(8,128)S(1)} custom-call(f32[16,16,128]{2,1,0:T(8,128)S(1)} %all_to_all.34.rho_ref, f32[1024,128]{1,0:T(8,128)S(1)} %get-tuple-element.47.v_ref, f32[16,1024,128]{2,1,0:T(8,128)S(1)} %get-tuple-element.45.k_ref, bf16[4,8,512,128]{3,2,1,0:T(8,128)(2,1)S(1)} %get-tuple-element.36.p_ref), custom_call_target="tpu_custom_call" | custom-call | flops 2147483648 | bytes 16777216 | tf_op jit(solution)/shard_map/barycenter_own/pallas_call | solution.py:380
  122.2 0.2 convert_element_type.13.b_ref
  122.4 0.5 means.1
  122.9 0.1 convert_element_type.14
  123.0 31.9 %all_to_all.35 = f16[8,528,128]{2,1,0:T(8,128)(2,1)S(1)} all-to-all(f16[8,528,128]{2,1,0:T(8,128)(2,1)S(1)} %convert_element_type.14), channel_id=1, replica_groups=mesh['z'=8,'x'=4,'y'=4,'core'=2] {'z'}, dimensions={0} | all-to-all | bytes 2162688 | tf_op jit(solution)/shard_map/all_to_all | solution.py:481
  154.9 0.1 convert_element_type.15.parts_ref
  155.1 1.0 update.1
  (18 shorter events, 0.2 us)
Async XLA Ops:
  0.0 8.1 %copy-start = (bf16[64,1024]{1,0:T(8,128)(2,1)S(1)}, bf16[64,1024]{1,0:T(8,128)(2,1)}, u32[]{:S(2)}) copy-start(bf16[64,1024]{1,0:T(8,128)(2,1)} %g_ref.1) | copy-start | bytes 393220
  0.0 4.6 %collective-permute-start.4 = (bf16[1024,128]{1,0:T(8,128)(2,1)}, bf16[1024,128]{1,0:T(8,128)(2,1)S(1)}, u32[]{:S(2)}, u32[]{:S(2)}) collective-permute-start(bf16[1024,128]{1,0:T(8,128)(2,1)} %param.3), channel_id=1, source_target_pairs={{0,1},{1,0},{2,3},{3,2},{4,5},{5,4},{6,7},{7,6},{8,9},{9,8},{10,11... | collective-permute-start | bytes 786440 | tf_op jit(solution)/shard_map/ppermute | solution.py:324
  3.2 4.8 %collective-permute-start = (bf16[64,1024]{1,0:T(8,128)(2,1)}, bf16[64,1024]{1,0:T(8,128)(2,1)S(1)}, u32[]{:S(2)}, u32[]{:S(2)}) collective-permute-start(bf16[64,1024]{1,0:T(8,128)(2,1)} %g_ref.1), channel_id=1, source_target_pairs={{0,1},{1,0},{2,3},{3,2},{4,5},{5,4},{6,7},{7,6},{8,9},{9,8},{10,11... | collective-permute-start | bytes 393224 | tf_op jit(solution)/shard_map/ppermute | solution.py:324
  4.7 10.2 %collective-permute-start.5 = (bf16[2,512,128]{2,1,0:T(8,128)(2,1)S(1)}, bf16[2,512,128]{2,1,0:T(8,128)(2,1)S(1)}, u32[]{:S(2)}, u32[]{:S(2)}) collective-permute-start(bf16[2,512,128]{2,1,0:T(8,128)(2,1)S(1)} %maximum_select_fusion.2), channel_id=1, source_target_pairs={{0,8},{1,3},{2,10},{3,5},{4,12},{5,7},{6,14},{7,1},{8,16},{9,11},{... | collective-permute-start | bytes 786440 | tf_op jit(solution)/shard_map/ppermute | solution.py:324
  4.8 10.2 %collective-permute-start.7 = (bf16[2,512,128]{2,1,0:T(8,128)(2,1)S(1)}, bf16[2,512,128]{2,1,0:T(8,128)(2,1)S(1)}, u32[]{:S(2)}, u32[]{:S(2)}) collective-permute-start(bf16[2,512,128]{2,1,0:T(8,128)(2,1)S(1)} %maximum_select_fusion.2), channel_id=1, source_target_pairs={{0,16},{1,5},{2,18},{3,7},{4,20},{5,1},{6,22},{7,3},{8,24},{9,13},... | collective-permute-start | bytes 786440 | tf_op jit(solution)/shard_map/ppermute | solution.py:324
  7.0 8.1 %collective-permute-start.6 = (bf16[2,512,128]{2,1,0:T(8,128)(2,1)S(1)}, bf16[2,512,128]{2,1,0:T(8,128)(2,1)S(1)}, u32[]{:S(2)}, u32[]{:S(2)}) collective-permute-start(bf16[2,512,128]{2,1,0:T(8,128)(2,1)S(1)} %maximum_select_fusion.2), channel_id=1, source_target_pairs={{0,24},{1,7},{2,26},{3,1},{4,28},{5,3},{6,30},{7,5},{8,0},{9,15},{... | collective-permute-start | bytes 786440 | tf_op jit(solution)/shard_map/ppermute | solution.py:324
  8.1 12.2 %collective-permute-start.2 = (bf16[2,64,1024]{2,1,0:T(8,128)(2,1)S(1)}, bf16[2,64,1024]{2,1,0:T(8,128)(2,1)S(1)}, u32[]{:S(2)}, u32[]{:S(2)}) collective-permute-start(bf16[2,64,1024]{2,1,0:T(8,128)(2,1)S(1)} %maximum_select_fusion.refs_8_), channel_id=1, source_target_pairs={{0,64},{1,193},{32,96},{33,225},{64,128},{65,1},{96,160},{97,33},{... | collective-permute-start | bytes 786440 | tf_op jit(solution)/shard_map/ppermute | solution.py:324
  14.2 9.0 %collective-permute-start.1 = (bf16[2,64,1024]{2,1,0:T(8,128)(2,1)S(1)}, bf16[2,64,1024]{2,1,0:T(8,128)(2,1)S(1)}, u32[]{:S(2)}, u32[]{:S(2)}) collective-permute-start(bf16[2,64,1024]{2,1,0:T(8,128)(2,1)S(1)} %maximum_select_fusion.refs_8_), channel_id=1, source_target_pairs={{0,32},{1,225},{32,64},{33,1},{64,96},{65,33},{96,128},{97,65},{12... | collective-permute-start | bytes 786440 | tf_op jit(solution)/shard_map/ppermute | solution.py:324
  15.1 13.5 %collective-permute-start.12 = (bf16[2,2,512,128]{3,2,1,0:T(8,128)(2,1)S(1)}, bf16[2,2,512,128]{3,2,1,0:T(8,128)(2,1)S(1)}, u32[]{:S(2)}, u32[]{:S(2)}) collective-permute-start(bf16[2,2,512,128]{3,2,1,0:T(8,128)(2,1)S(1)} %pad_maximum_fusion.3.refs_1_), channel_id=1, source_target_pairs={{0,6},{1,25},{2,0},{3,27},{4,2},{5,29},{6,4},{7,31},{8,14},{9,1},{... | collective-permute-start | bytes 1572872 | tf_op jit(solution)/shard_map/ppermute | solution.py:324
  17.7 12.2 %collective-permute-start.10 = (bf16[2,2,512,128]{3,2,1,0:T(8,128)(2,1)S(1)}, bf16[2,2,512,128]{3,2,1,0:T(8,128)(2,1)S(1)}, u32[]{:S(2)}, u32[]{:S(2)}) collective-permute-start(bf16[2,2,512,128]{3,2,1,0:T(8,128)(2,1)S(1)} %pad_maximum_fusion.2.refs_0_), channel_id=1, source_target_pairs={{0,2},{1,9},{2,4},{3,11},{4,6},{5,13},{6,0},{7,15},{8,10},{9,17},{... | collective-permute-start | bytes 1572872 | tf_op jit(solution)/shard_map/ppermute | solution.py:324
  23.2 11.6 %collective-permute-start.3 = (bf16[2,2,64,1024]{3,2,1,0:T(8,128)(2,1)S(1)}, bf16[2,2,64,1024]{3,2,1,0:T(8,128)(2,1)S(1)}, u32[]{:S(2)}, u32[]{:S(2)}) collective-permute-start(bf16[2,2,64,1024]{3,2,1,0:T(8,128)(2,1)S(1)} %pad_maximum_fusion.1), channel_id=1, source_target_pairs={{0,64},{1,193},{32,96},{33,225},{64,128},{65,1},{96,160},{97,33},{... | collective-permute-start | bytes 1572872 | tf_op jit(solution)/shard_map/ppermute | solution.py:324
  26.0 9.5 %collective-permute-start.8 = (bf16[2,2,512,128]{3,2,1,0:T(8,128)(2,1)S(1)}, bf16[2,2,512,128]{3,2,1,0:T(8,128)(2,1)S(1)}, u32[]{:S(2)}, u32[]{:S(2)}) collective-permute-start(bf16[2,2,512,128]{3,2,1,0:T(8,128)(2,1)S(1)} %pad_maximum_fusion.3.refs_1_), channel_id=1, source_target_pairs={{0,2},{1,9},{2,4},{3,11},{4,6},{5,13},{6,0},{7,15},{8,10},{9,17},{... | collective-permute-start | bytes 1572872 | tf_op jit(solution)/shard_map/ppermute | solution.py:324
  27.2 8.3 %collective-permute-start.9 = (bf16[2,2,512,128]{3,2,1,0:T(8,128)(2,1)S(1)}, bf16[2,2,512,128]{3,2,1,0:T(8,128)(2,1)S(1)}, u32[]{:S(2)}, u32[]{:S(2)}) collective-permute-start(bf16[2,2,512,128]{3,2,1,0:T(8,128)(2,1)S(1)} %pad_maximum_fusion.2.refs_0_), channel_id=1, source_target_pairs={{0,6},{1,25},{2,0},{3,27},{4,2},{5,29},{6,4},{7,31},{8,14},{9,1},{... | collective-permute-start | bytes 1572872 | tf_op jit(solution)/shard_map/ppermute | solution.py:324
  28.6 12.5 %collective-permute-start.13 = (bf16[2,2,512,128]{3,2,1,0:T(8,128)(2,1)S(1)}, bf16[2,2,512,128]{3,2,1,0:T(8,128)(2,1)S(1)}, u32[]{:S(2)}, u32[]{:S(2)}) collective-permute-start(bf16[2,2,512,128]{3,2,1,0:T(8,128)(2,1)S(1)} %collective-permute-done.12.refs_5_), channel_id=1, source_target_pairs={{0,6},{1,25},{2,0},{3,27},{4,2},{5,29},{6,4},{7,31},{8,14},{9,1},{... | collective-permute-start | bytes 1572872 | tf_op jit(solution)/shard_map/ppermute | solution.py:324
  29.9 11.2 %collective-permute-start.11 = (bf16[2,2,512,128]{3,2,1,0:T(8,128)(2,1)S(1)}, bf16[2,2,512,128]{3,2,1,0:T(8,128)(2,1)S(1)}, u32[]{:S(2)}, u32[]{:S(2)}) collective-permute-start(bf16[2,2,512,128]{3,2,1,0:T(8,128)(2,1)S(1)} %collective-permute-done.10.refs_2_), channel_id=1, source_target_pairs={{0,2},{1,9},{2,4},{3,11},{4,6},{5,13},{6,0},{7,15},{8,10},{9,17},{... | collective-permute-start | bytes 1572872 | tf_op jit(solution)/shard_map/ppermute | solution.py:324
  41.1 6.4 %collective-permute-start.14 = (bf16[3,2,64,1024]{3,2,1,0:T(8,128)(2,1)S(1)}, bf16[3,2,64,1024]{3,2,1,0:T(8,128)(2,1)S(1)}, u32[]{:S(2)}, u32[]{:S(2)}) collective-permute-start(bf16[3,2,64,1024]{3,2,1,0:T(8,128)(2,1)S(1)} %pad_maximum_fusion.refs_10_), channel_id=1, source_target_pairs={{0,1},{1,0},{2,3},{3,2},{4,5},{5,4},{6,7},{7,6},{8,9},{9,8},{10,11... | collective-permute-start | bytes 2359304 | tf_op jit(solution)/shard_map/ppermute | solution.py:324
  47.5 13.1 %copy-start.1 = (f32[64,1024]{1,0:T(8,128)S(1)}, f32[64,1024]{1,0:T(8,128)}, u32[]{:S(2)}) copy-start(f32[64,1024]{1,0:T(8,128)} %n_ref.1) | copy-start | bytes 786436
  117.8 4.4 %collective-permute-start.15 = (f16[520,1024]{1,0:T(8,128)(2,1)S(1)}, f16[520,1024]{1,0:T(8,128)(2,1)S(1)}, u32[]{:S(2)}, u32[]{:S(2)}) collective-permute-start(f16[520,1024]{1,0:T(8,128)(2,1)S(1)} %convert_element_type.12), channel_id=1, source_target_pairs={{0,1},{1,0},{2,3},{3,2},{4,5},{5,4},{6,7},{7,6},{8,9},{9,8},{10,11... | collective-permute-start | bytes 3194888 | tf_op jit(solution)/shard_map/ppermute | solution.py:324
